TPU v7x, 128 devices: a whole 4x4x4 slice. The times are simulated.
128 devices in a mesh: func: 16 (over z, y_lo, core), pts: 8 (over x, y_hi).
Axes of the slice: x: 4, y: 4 (y_hi: 2, y_lo: 2; y = y_hi * 2 + y_lo), z: 4, core: 2. Of those that a mesh axis runs over, the one named last changes fastest.
Arguments:
- sensors: bfloat16 [1024, 4096], P(('func', 'pts')), may hold values from -6 to 6
- forcing: bfloat16 [1024, 16384], P('func', 'pts'), may hold values from -6 to 6
- coords: float32 [2, 16384], P(None, 'pts'), may hold values from -3.14159 to 3.14159
- branch_first: bfloat16 [4096, 256], replicated, may hold values from -0.09375 to 0.09375
- branch_second: bfloat16 [256, 256], replicated, may hold values from -0.375 to 0.375
- branch_third: bfloat16 [256, 256], replicated, may hold values from -0.375 to 0.375
- trunk_first: float32 [2, 256], replicated, may hold values from -4 to 4
- trunk_second: bfloat16 [256, 256], replicated, may hold values from -0.375 to 0.375
- trunk_third: bfloat16 [256, 256], replicated, may hold values from -0.375 to 0.375
Outputs:
- grad_branch_first: float32 [4096, 256], replicated
- grad_branch_second: float32 [256, 256], replicated
- grad_branch_third: float32 [256, 256], replicated
- grad_trunk_first: float32 [2, 256], replicated
- grad_trunk_second: float32 [256, 256], replicated
- grad_trunk_third: float32 [256, 256], replicated
All inputs are finite; a program needn't handle non-finite values.
Results may differ from a plain program's by a relative error of at most 0.009.
Values may be sent and summed in bfloat16 or wider, within the bound.
No kernel may reach another device: no remote copies, remote signals or barrier semaphores. Data moves between devices by JAX's collectives and lax.ppermute only.
A program may use at most 192 MiB of HBM per device.

v0:
```python
import functools
import math

import jax
import jax.numpy as jnp
from jax import lax
from jax.experimental import pallas as pl
from jax.experimental.pallas import tpu as pltpu
from jax.sharding import PartitionSpec as P

DRAG = 0.5
TILE = 512
ROWS = 16
LANES = 128
F32 = jnp.float32
BF16 = jnp.bfloat16
GROUP = (0, 1, 1, 2, 2, 2, 3, 3)
NT = (((1,), (1,)), ((), ()))
TN = (((0,), (0,)), ((), ()))


def dot(left, right, dims=(((1,), (0,)), ((), ()))):
    return lax.dot_general(left, right, dims, preferred_element_type=F32)


def slopes(squash):
    square = squash * squash
    one = 1.0 - square
    two = -2.0 * (squash * one)
    three = one * (4.0 * square - 2.0 * one)
    return square, one, two, three


def trunk_kernel(
    weight,
    scale,
    coords_ref,
    first_ref,
    weights_ref,
    second_ref,
    consts_ref,
    feats_ref,
    forcing_ref,
    u_ref,
    second_grad_ref,
    const_grad_ref,
    value_grad_ref,
    squash_ref,
    points_ref,
    inner_ref,
    combos_ref,
    back_ref,
    inner_back_ref,
    ones_ref,
    grads_ref,
    value_ref,
):
    step = pl.program_id(0)
    last = pl.num_programs(0) - 1
    tile = coords_ref.shape[0]
    width = first_ref.shape[1]

    @pl.when(step == 0)
    def _():
        u_ref[...] = jnp.zeros_like(u_ref)
        grads_ref[...] = jnp.zeros_like(grads_ref)
        value_ref[...] = jnp.zeros_like(value_ref)

    def chunks(body, unroll):
        def one(index, carry):
            start = pl.multiple_of(index * ROWS, ROWS)
            for lane in range(0, width, LANES):
                body(pl.ds(start, ROWS), pl.ds(lane, LANES))
            return carry

        lax.fori_loop(0, tile // ROWS, one, 0, unroll=unroll)

    def layer_one(rows, lanes):
        x, y = coords_ref[rows, 0:1], coords_ref[rows, 1:2]
        squash = jnp.tanh(x * first_ref[0:1, lanes] + y * first_ref[1:2, lanes])
        _, one, two, three = slopes(squash)
        squash_ref[rows, lanes] = squash
        for group, part in enumerate((squash, one, two, three)):
            points_ref[group, rows, lanes] = part.astype(BF16)

    chunks(layer_one, 2)
    for part, group in enumerate(GROUP):
        inner_ref[part] = dot(points_ref[group], weights_ref[part])

    def layer_two(rows, lanes):
        z, zx, zy, lap, dif, mix, px, py = (inner_ref[part, rows, lanes] for part in range(8))
        squash = jnp.tanh(z)
        inner_ref[0, rows, lanes] = squash
        _, one, two, three = slopes(squash)
        radius = zx * zx + zy * zy
        twice = lap + lap
        bend = three * radius
        along = zx * (twice + dif) + zy * mix
        across = zy * (twice - dif) + zx * mix
        combos = (
            one * zx,
            one * zy,
            one * lap - two * radius,
            one * px + two * along - bend * zx,
            one * py + two * across - bend * zy,
        )
        for k, combo in enumerate(combos):
            combos_ref[k, rows, lanes] = combo.astype(BF16)

    chunks(layer_two, 2)
    feats = feats_ref[...]
    px, py, om, omx, omy = (dot(feats, combos_ref[k], NT) * scale for k in range(5))
    slope = (py * omx - px * omy + DRAG * om - forcing_ref[...].astype(F32)) * weight
    cots = [
        cot.astype(BF16)
        for cot in (-slope * omy, slope * omx, DRAG * slope, slope * py, -slope * px)
    ]
    total = u_ref[...]
    for k in range(5):
        total += dot(cots[k], combos_ref[k])
        back_ref[k] = dot(cots[k], feats, TN) * scale
    u_ref[...] = total

    def layer_two_back(rows, lanes):
        squash, zx, zy, lap, dif, mix, px, py = (inner_ref[part, rows, lanes] for part in range(8))
        gx, gy, gl, gp, gq = (back_ref[k, rows, lanes] for k in range(5))
        square, one, two, three = slopes(squash)
        four = two * (4.0 * square - 8.0 * one)
        radius = zx * zx + zy * zy
        twice = lap + lap
        plus, minus = twice + dif, twice - dif
        along = zx * plus + zy * mix
        across = zy * minus + zx * mix
        pull = gp * zx + gq * zy
        one_bar = gx * zx + gy * zy + gl * lap + gp * px + gq * py
        two_bar = gp * along + gq * across - gl * radius
        three_bar = pull * radius
        along_bar, across_bar = two * gp, two * gq
        turn = -2.0 * (two * gl + three * pull)
        bend = three * radius
        xa, yc = zx * along_bar, zy * across_bar
        parts = (
            two * one_bar + three * two_bar - four * three_bar,
            one * gx - bend * gp + zx * turn + along_bar * plus + across_bar * mix,
            one * gy - bend * gq + zy * turn + across_bar * minus + along_bar * mix,
            one * gl + 2.0 * (xa + yc),
            xa - yc,
            zy * along_bar + zx * across_bar,
            one * gp,
            one * gq,
        )
        for part, value in enumerate(parts):
            inner_back_ref[part, rows, lanes] = value.astype(BF16)

    chunks(layer_two_back, 1)
    for part, group in enumerate(GROUP):
        grads_ref[part] += dot(points_ref[group], inner_back_ref[part], TN)
    for group in range(4):
        total = None
        for part in range(8):
            if GROUP[part] == group:
                term = dot(inner_back_ref[part], weights_ref[part], NT)
                total = term if total is None else total + term
        ones_ref[group] = total

    def layer_one_back(index, carry):
        start = pl.multiple_of(index * ROWS, ROWS)
        rows = pl.ds(start, ROWS)
        x, y = coords_ref[rows, 0:1], coords_ref[rows, 1:2]
        out = []
        for number, lane in enumerate(range(0, width, LANES)):
            lanes = pl.ds(lane, LANES)
            square, one, two, three = slopes(squash_ref[rows, lanes])
            four = two * (4.0 * square - 8.0 * one)
            back = (
                one * ones_ref[0, rows, lanes]
                + two * ones_ref[1, rows, lanes]
                + three * ones_ref[2, rows, lanes]
                + four * ones_ref[3, rows, lanes]
            )
            out += [carry[2 * number] + x * back, carry[2 * number + 1] + y * back]
        return tuple(out)

    zero = jnp.zeros((ROWS, LANES), F32)
    sums = lax.fori_loop(
        0, tile // ROWS, layer_one_back, (zero,) * (2 * (width // LANES)), unroll=2
    )
    for number, lane in enumerate(range(0, width, LANES)):
        for axis in range(2):
            value_ref[axis, :, lane : lane + LANES] += sums[2 * number + axis]

    @pl.when(step == last)
    def _():
        second = second_ref[...].astype(F32)
        total = jnp.zeros((width, width), F32)
        first = [jnp.zeros((width, 1), F32)] * 2
        for part in range(8):
            grad = grads_ref[part]
            total += consts_ref[:, part : part + 1] * grad
            row = jnp.sum(second * grad, axis=1, keepdims=True)
            for axis in range(2):
                column = 8 * (axis + 1) + part
                first[axis] = first[axis] + consts_ref[:, column : column + 1] * row
        second_grad_ref[...] = total
        for axis in range(2):
            const_grad_ref[:, axis : axis + 1] = first[axis]
            value_grad_ref[axis : axis + 1] = jnp.sum(value_ref[axis], axis=0, keepdims=True)


def trunk_call(coords, first, second, feats, forcing, weight, scale):
    points, width = coords.shape[1], first.shape[1]
    funcs = feats.shape[0]
    tile = min(TILE, points)
    a, b = first[0], first[1]
    one, zero = jnp.ones_like(a), jnp.zeros_like(a)
    consts = [
        one,
        a,
        b,
        -(a * a + b * b),
        -(a * a - b * b),
        -2.0 * a * b,
        -a * (a * a + b * b),
        -b * (a * a + b * b),
    ]
    by_a = [
        zero,
        one,
        zero,
        -2.0 * a,
        -2.0 * a,
        -2.0 * b,
        -(3.0 * a * a + b * b),
        -2.0 * a * b,
    ]
    by_b = [
        zero,
        zero,
        one,
        -2.0 * b,
        2.0 * b,
        -2.0 * a,
        -2.0 * a * b,
        -(a * a + 3.0 * b * b),
    ]
    columns = jnp.stack(consts + by_a + by_b, axis=1)
    weights = (jnp.stack(consts)[:, :, None] * second.astype(F32)[None]).astype(BF16)
    whole = lambda *shape: pl.BlockSpec(shape, lambda i: (0,) * len(shape))
    return pl.pallas_call(
        functools.partial(trunk_kernel, weight, scale),
        grid=(points // tile,),
        in_specs=[
            pl.BlockSpec((tile, 2), lambda i: (i, 0)),
            whole(2, width),
            whole(8, width, width),
            whole(width, width),
            whole(width, 24),
            whole(funcs, width),
            pl.BlockSpec((funcs, tile), lambda i: (0, i)),
        ],
        out_specs=[whole(funcs, width), whole(width, width), whole(width, 2), whole(2, width)],
        out_shape=[
            jax.ShapeDtypeStruct((funcs, width), F32),
            jax.ShapeDtypeStruct((width, width), F32),
            jax.ShapeDtypeStruct((width, 2), F32),
            jax.ShapeDtypeStruct((2, width), F32),
        ],
        scratch_shapes=[
            pltpu.VMEM((tile, width), F32),
            pltpu.VMEM((4, tile, width), BF16),
            pltpu.VMEM((8, tile, width), F32),
            pltpu.VMEM((5, tile, width), BF16),
            pltpu.VMEM((5, tile, width), F32),
            pltpu.VMEM((8, tile, width), BF16),
            pltpu.VMEM((4, tile, width), F32),
            pltpu.VMEM((8, width, width), F32),
            pltpu.VMEM((2, ROWS, width), F32),
        ],
        compiler_params=pltpu.CompilerParams(
            dimension_semantics=("arbitrary",), vmem_limit_bytes=48 * 1024 * 1024
        ),
        name="trunk",
    )(coords.T, first, weights, second, columns, feats, forcing)


def swap(parts):
    return lax.all_to_all(parts, ("func", "pts"), split_axis=0, concat_axis=0, tiled=True)


def tell(part, count):
    return swap(jnp.broadcast_to(part[None], (count, *part.shape)))


def per_device(
    sensors,
    forcing,
    coords,
    branch_first,
    branch_second,
    branch_third,
    trunk_first,
    trunk_second,
    trunk_third,
):
    func_size, pts_size = lax.axis_size("func"), lax.axis_size("pts")
    count = func_size * pts_size
    funcs = forcing.shape[0]
    weight = 1.0 / math.sqrt(funcs * func_size * forcing.shape[1] * pts_size)
    width_out = trunk_third.shape[1]
    width = trunk_second.shape[0]
    scale = width_out ** (-0.5)
    own = sensors.shape[0]
    fields = sensors.shape[1] // count

    own_one = jnp.tanh(dot(sensors, branch_first)).astype(BF16)
    blocks = sensors.reshape(own, count, fields).transpose(1, 0, 2)
    sent = jnp.concatenate(
        [jnp.broadcast_to(own_one[None], (count, own, own_one.shape[1])), blocks], axis=2
    )
    got = swap(sent)
    branch_one = got[:, :, : own_one.shape[1]].reshape(count * own, -1)
    sensor_columns = got[:, :, own_one.shape[1] :].reshape(count * own, fields)
    hidden_two = jnp.tanh(dot(branch_one, branch_second))
    branch_two = hidden_two.astype(BF16)
    features = dot(branch_two, branch_third).astype(BF16)
    block = lax.dynamic_slice_in_dim(features, lax.axis_index("func") * funcs, funcs, 0)
    feats = dot(block, trunk_third, NT).astype(BF16)

    u_part, second_part, const_part, value_part = trunk_call(
        coords, trunk_first, trunk_second, feats, forcing, weight, scale
    )
    first_part = value_part + const_part.T
    pieces = jnp.concatenate(
        [
            u_part.reshape(count, -1, LANES),
            second_part.reshape(count, -1, LANES),
            jnp.pad(
                first_part.reshape(count, 1, -1),
                ((0, 0), (0, 0), (0, LANES - first_part.size // count)),
            ),
        ],
        axis=1,
    ).astype(BF16)
    u_rows = funcs * width // count // LANES
    arrived = swap(pieces).astype(F32)
    u_sum = arrived[:, :u_rows].reshape(func_size, pts_size, u_rows, LANES).sum(1)
    rest = arrived[:, u_rows:].sum(0)
    summed = jnp.concatenate([u_sum.reshape(func_size * u_rows, LANES), rest], 0).astype(BF16)
    every = tell(summed, count)
    cut = func_size * u_rows
    u = (
        every[:, :cut]
        .reshape(count, func_size, u_rows, LANES)
        .transpose(1, 0, 2, 3)
        .reshape(func_size * funcs, width)
    )
    grad_t2 = every[:, cut:-1].astype(F32).reshape(trunk_second.shape)
    grad_t1 = (
        every[:, -1, : trunk_first.size // count].astype(F32).reshape(trunk_first.shape)
    )

    feature_back = (dot(u, trunk_third) * scale).astype(BF16)
    grad_t3 = dot(u, features, TN) * scale
    grad_b3 = dot(branch_two, feature_back, TN)
    back_two = (dot(feature_back, branch_third, NT) * (1.0 - hidden_two * hidden_two)).astype(BF16)
    grad_b2 = dot(branch_one, back_two, TN)
    hidden_one = branch_one.astype(F32)
    back_one = (dot(back_two, branch_second, NT) * (1.0 - hidden_one * hidden_one)).astype(BF16)
    own_rows = dot(sensor_columns, back_one, TN).astype(BF16)
    grad_b1 = tell(own_rows, count).reshape(branch_first.shape).astype(F32)
    return (grad_b1, grad_b2, grad_b3, grad_t1, grad_t2, grad_t3)


def solution(mesh):
    return jax.shard_map(
        per_device,
        mesh=mesh,
        in_specs=(
            P(("func", "pts"), None),
            P("func", "pts"),
            P(None, "pts"),
            P(),
            P(),
            P(),
            P(),
            P(),
            P(),
        ),
        out_specs=(P(), P(), P(), P(), P(), P()),
        check_vma=False,
    )
```

profile of v0, /device:TPU:1, one launch (start us, length us, event | category | flops | bytes accessed | tf_op | source)
XLA Modules:
  0.0 161.4 jit_solution(5432486128369562279)
XLA Ops:
  0.6 1.2 reshape.260
  2.3 1.2 fusion.5
  3.7 1.0 pad_maximum_fusion
  4.7 11.9 %all-to-all-start = ((bf16[128,8,288]{2,1,0:T(8,128)(2,1)}), bf16[128,8,288]{2,1,0:T(8,128)(2,1)}, u32[]{:S(2)}, u32[]{:S(2)}) async-start(bf16[128,8,288]{2,1,0:T(8,128)(2,1)} %pad_maximum_fusion), calls=%async_computation | async-start | bytes 1572864 | tf_op jit(solution)/shard_map/all_to_all | solution.py:287
  17.6 1.3 copy.43
  19.0 1.3 multiply_convert_fusion.weights_ref
  20.4 12.8 %all-to-all-done = bf16[128,8,288]{2,1,0:T(8,128)(2,1)} async-done(((bf16[128,8,288]{2,1,0:T(8,128)(2,1)}), bf16[128,8,288]{2,1,0:T(8,128)(2,1)}, u32[]{:S(2)}, u32[]{:S(2)}) %all-to-all-start) | async-done | bytes 589856 | tf_op jit(solution)/shard_map/all_to_all | solution.py:287
  33.2 1.5 convolution_tanh_fusion
  35.6 1.2 convolution_convert_fusion
  37.0 37.0 %trunk.1 = (f32[64,256]{1,0:T(8,128)S(1)}, f32[256,256]{1,0:T(8,128)S(1)}, f32[256,2]{1,0:T(8,128)S(1)}, f32[2,256]{1,0:T(2,128)S(1)}) custom-call(f32[2048,2]{1,0:T(8,128)S(1)} %bitcast.77, f32[2,256]{1,0:T(2,128)S(1)} %copy-done.5, bf16[8,256,256]{2,1,0:T(8,128)(2,1)S(1)} %multiply_convert_fusion.weights_ref, bf16[256,256]{1,0:T(8,128)(2,1)S(1)} %copy-done.2, ...), custom_call_target="tpu_custom_call" | custom-call | tf_op jit(solution)/shard_map/trunk/pallas_call | solution.py:249
  76.3 14.6 %all_to_all.20 = bf16[128,6,128]{2,1,0:T(8,128)(2,1)S(1)} all-to-all(bf16[128,6,128]{2,1,0:T(8,128)(2,1)S(1)} %fusion.12), channel_id=1, replica_groups=mesh['func'=16,'pts'=8] {'func','pts'}, dimensions={0} | all-to-all | bytes 393216 | tf_op jit(solution)/shard_map/all_to_all | solution.py:287
  91.4 20.7 %all_to_all.21 = bf16[128,21,128]{2,1,0:T(8,128)(2,1)S(1)} all-to-all(bf16[128,21,128]{2,1,0:T(8,128)(2,1)S(1)} %broadcast_in_dim.7), channel_id=1, replica_groups=mesh['func'=16,'pts'=8] {'func','pts'}, dimensions={0} | all-to-all | bytes 1376256 | tf_op jit(solution)/shard_map/all_to_all | solution.py:287
  114.0 2.1 %reshape.268 = bf16[1024,256]{1,0:T(8,128)(2,1)} reshape(bf16[16,128,1,128]{3,1,0,2:T(8,128)(2,1)} %copy.48) | data formatting | bytes 1048576 | tf_op jit(solution)/shard_map/reshape | solution.py:355
  116.0 1.3 fusion
  118.2 1.2 fusion.1
  119.3 1.8 %fusion.4 = bf16[32,256]{1,0:T(8,128)(2,1)S(1)} fusion(bf16[1024,256]{1,0:T(8,128)(2,1)} %fusion.1, bf16[256,256]{1,0:T(8,128)(2,1)S(1)} %copy-done.15, bf16[128,8,288]{2,1,0:T(8,128)(2,1)} %all-to-all-done), kind=kOutput, calls=%fused_computation.13 | convolution fusion | flops 152313856 | bytes 1261568 | tf_op jit(solution)/shard_map/dot_general | solution.py:23
  121.1 1.6 broadcast_in_dim.8
  122.7 4.7 %all-to-all-start.3 = ((bf16[128,32,256]{2,1,0:T(8,128)(2,1)}), bf16[128,32,256]{2,1,0:T(8,128)(2,1)}, u32[]{:S(2)}, u32[]{:S(2)}) async-start(bf16[128,32,256]{2,1,0:T(8,128)(2,1)} %broadcast_in_dim.8), calls=%async_computation.3 | async-start | bytes 4194304 | tf_op jit(solution)/shard_map/all_to_all | solution.py:287
  127.5 1.2 fusion.16
  131.2 2.3 %convolution_multiply_fusion.3 = f32[256,256]{1,0:T(8,128)} fusion(bf16[1024,256]{1,0:T(8,128)(2,1)} %reshape.268, bf16[1024,256]{1,0:T(8,128)(2,1)} %copy-done.11), kind=kOutput, calls=%fused_computation.11 | convolution fusion | flops 134283264 | bytes 1310720 | tf_op jit(solution)/shard_map/dot_general | solution.py:23
  133.5 2.2 %fusion.11 = f32[256,256]{1,0:T(8,128)} fusion(bf16[1024,256]{1,0:T(8,128)(2,1)} %fusion.1, bf16[128,8,288]{2,1,0:T(8,128)(2,1)} %all-to-all-done), kind=kOutput, calls=%fused_computation.26 | convolution fusion | flops 134217728 | bytes 1310720 | tf_op jit(solution)/shard_map/dot_general | solution.py:23
  135.7 1.0 fusion.13
  136.7 20.7 %all-to-all-done.3 = bf16[128,32,256]{2,1,0:T(8,128)(2,1)} async-done(((bf16[128,32,256]{2,1,0:T(8,128)(2,1)}), bf16[128,32,256]{2,1,0:T(8,128)(2,1)}, u32[]{:S(2)}, u32[]{:S(2)}) %all-to-all-start.3) | async-done | bytes 2097184 | tf_op jit(solution)/shard_map/all_to_all | solution.py:287
  157.5 3.9 %bitcast_convert_fusion = f32[4096,256]{1,0:T(8,128)} fusion(bf16[128,32,256]{2,1,0:T(8,128)(2,1)} %all-to-all-done.3), kind=kLoop, calls=%fused_computation | loop fusion | flops 1048576 | bytes 6291456 | tf_op jit(solution)/shard_map/convert_element_type | solution.py:370
  (66 shorter events, 10.5 us)
Async XLA Ops:
  0.6 1.6 %copy-start = (bf16[4096,256]{1,0:T(8,128)(2,1)S(1)}, bf16[4096,256]{1,0:T(8,128)(2,1)}, u32[]{:S(2)}) copy-start(bf16[4096,256]{1,0:T(8,128)(2,1)} %param.12) | copy-start | bytes 6291460
  3.5 13.2 %copy-start.5 = (f32[2,256]{1,0:T(2,128)S(1)}, f32[2,256]{1,0:T(2,128)}, u32[]{:S(2)}) copy-start(f32[2,256]{1,0:T(2,128)} %first_ref.1) | copy-start | bytes 6148
  3.7 13.2 %copy-start.2 = (bf16[256,256]{1,0:T(8,128)(2,1)S(1)}, bf16[256,256]{1,0:T(8,128)(2,1)}, u32[]{:S(2)}) copy-start(bf16[256,256]{1,0:T(8,128)(2,1)} %second_ref.1) | copy-start | bytes 393220
  3.7 14.0 %copy-start.16 = (f32[2,2048]{1,0:T(2,128)S(1)}, f32[2,2048]{1,0:T(2,128)}, u32[]{:S(2)}) copy-start(f32[2,2048]{1,0:T(2,128)} %param.11) | copy-start | bytes 49156
  4.7 28.4 %all-to-all-start = ((bf16[128,8,288]{2,1,0:T(8,128)(2,1)}), bf16[128,8,288]{2,1,0:T(8,128)(2,1)}, u32[]{:S(2)}, u32[]{:S(2)}) async-start(bf16[128,8,288]{2,1,0:T(8,128)(2,1)} %pad_maximum_fusion), calls=%async_computation | async-start | bytes 1572864 | tf_op jit(solution)/shard_map/all_to_all | solution.py:287
  19.0 17.8 %copy-start.12 = (bf16[256,256]{1,0:T(8,128)(2,1)S(1)}, bf16[256,256]{1,0:T(8,128)(2,1)}, u32[]{:S(2)}) copy-start(bf16[256,256]{1,0:T(8,128)(2,1)} %param.17) | copy-start | bytes 393220
  33.2 3.8 %copy-start.1 = (f32[2,2048]{0,1:T(8,128)S(1)}, f32[2,2048]{0,1:T(8,128)}, u32[]{:S(2)}) copy-start(f32[2,2048]{0,1:T(8,128)} %copy.43) | copy-start | bytes 49156
  33.2 3.9 %copy-start.3 = (bf16[64,2048]{1,0:T(8,128)(2,1)S(1)}, bf16[64,2048]{1,0:T(8,128)(2,1)}, u32[]{:S(2)}) copy-start(bf16[64,2048]{1,0:T(8,128)(2,1)} %forcing_ref.1) | copy-start | bytes 786436
  34.6 1.0 copy-start.6
  36.8 38.0 %copy-start.11 = (bf16[1024,256]{1,0:T(8,128)(2,1)}, bf16[1024,256]{1,0:T(8,128)(2,1)S(1)}, u32[]{:S(2)}) copy-start(bf16[1024,256]{1,0:T(8,128)(2,1)S(1)} %convolution_convert_fusion) | copy-start | bytes 1572868
  74.1 0.7 copy-start.4
  91.4 24.7 %copy-start.13 = (bf16[256,256]{1,0:T(8,128)(2,1)S(1)}, bf16[256,256]{1,0:T(8,128)(2,1)}, u32[]{:S(2)}) copy-start(bf16[256,256]{1,0:T(8,128)(2,1)} %param.17) | copy-start | bytes 393220
  112.1 0.9 copy-start.10
  113.0 5.2 %copy-start.7 = (f32[1024,256]{1,0:T(8,128)S(1)}, f32[1024,256]{1,0:T(8,128)}, u32[]{:S(2)}) copy-start(f32[1024,256]{1,0:T(8,128)} %copy-done.6) | copy-start | bytes 3145732
  113.0 5.2 %copy-start.14 = (bf16[256,256]{1,0:T(8,128)(2,1)S(1)}, bf16[256,256]{1,0:T(8,128)(2,1)}, u32[]{:S(2)}) copy-start(bf16[256,256]{1,0:T(8,128)(2,1)} %param.14) | copy-start | bytes 393220
  114.0 5.4 %copy-start.15 = (bf16[256,256]{1,0:T(8,128)(2,1)S(1)}, bf16[256,256]{1,0:T(8,128)(2,1)}, u32[]{:S(2)}) copy-start(bf16[256,256]{1,0:T(8,128)(2,1)} %param.13) | copy-start | bytes 393220
  117.4 0.8 copy-start.8
  122.7 34.7 %all-to-all-start.3 = ((bf16[128,32,256]{2,1,0:T(8,128)(2,1)}), bf16[128,32,256]{2,1,0:T(8,128)(2,1)}, u32[]{:S(2)}, u32[]{:S(2)}) async-start(bf16[128,32,256]{2,1,0:T(8,128)(2,1)} %broadcast_in_dim.8), calls=%async_computation.3 | async-start | bytes 4194304 | tf_op jit(solution)/shard_map/all_to_all | solution.py:287
  131.2 4.5 %copy-start.9 = (bf16[1024,256]{1,0:T(8,128)(2,1)S(1)}, bf16[1024,256]{1,0:T(8,128)(2,1)}, u32[]{:S(2)}) copy-start(bf16[1024,256]{1,0:T(8,128)(2,1)} %copy-done.8) | copy-start | bytes 1572868
where the time goes:
time: 162 us; the launch traced here: 161 us
  Pallas kernels  37 us (23%)
  blocking collectives  35.4 us (22%)
  waiting for transfers between devices  33.5 us (21%)
  starting transfers between devices  16.6 us (10%)
  matrix products  13.9 us (9%)
  local copies, waits for them, and re-layouts  13.4 us (8%)
  other arithmetic  10.6 us (7%)
    pallas_call x1, Pallas kernels, trunk_call(): pl.pallas_call(functools.partial(trunk_kernel, weight, scale), grid=(poin...  37 us
    all_to_all x2, blocking collectives, swap(): lax.all_to_all(parts, ('func', 'pts'), split_axis=0, concat_axis=0, tiled...  35.4 us
    all_to_all x2, waiting for transfers between devices, swap(): lax.all_to_all(parts, ('func', 'pts'), split_axis=0, concat_axis=0, tiled...  33.5 us
    all_to_all x2, starting transfers between devices, swap(): lax.all_to_all(parts, ('func', 'pts'), split_axis=0, concat_axis=0, tiled...  16.6 us
    dot_general x10, matrix products, dot(): return lax.dot_general(left, right, dims, preferred_element_type=F32)  13.9 us
    unnamed x35, local copies, waits for them, and re-layouts  5.16 us
    convert_element_type x1, other arithmetic, per_device(): grad_b1 = tell(own_rows, count).reshape(branch_first.shape).astype(F32)  3.93 us
  transfers between devices with their start and end apart: 2, of which 2 were waited for; matrix products, arithmetic and copies ran while one was open for 8% of the time, Pallas kernels for 0%

commit v1 on v0

v1 whole, which is shorter than its diff:
```python
import functools
import math

import jax
import jax.numpy as jnp
from jax import lax
from jax.experimental import pallas as pl
from jax.experimental.pallas import tpu as pltpu
from jax.sharding import PartitionSpec as P

DRAG = 0.5
PTS = 8
TILE = 512
ROWS = 16
LANES = 128
F32 = jnp.float32
BF16 = jnp.bfloat16
AXES = ("pairs", "core", "pts")
GROUP = (0, 1, 1, 2, 2, 2, 3, 3)
NT = (((1,), (1,)), ((), ()))
TN = (((0,), (0,)), ((), ()))
PARAMS = pltpu.CompilerParams(
    dimension_semantics=("arbitrary",), vmem_limit_bytes=48 * 1024 * 1024
)


def dot(left, right, dims=(((1,), (0,)), ((), ()))):
    return lax.dot_general(left, right, dims, preferred_element_type=F32)


def slopes(squash):
    square = squash * squash
    one = 1.0 - square
    two = -2.0 * (squash * one)
    three = one * (4.0 * square - 2.0 * one)
    return square, one, two, three


def chunks(shape, body, unroll):
    def one(index, carry):
        start = pl.multiple_of(index * ROWS, ROWS)
        for lane in range(0, shape[1], LANES):
            body(pl.ds(start, ROWS), pl.ds(lane, LANES))
        return carry

    lax.fori_loop(0, shape[0] // ROWS, one, 0, unroll=unroll)


def forward_kernel(values_ref, weights_ref, squash_ref, points_ref, inner_ref, combos_ref):
    def layer_one(rows, lanes):
        squash = jnp.tanh(values_ref[rows, lanes])
        _, one, two, three = slopes(squash)
        squash_ref[rows, lanes] = squash
        for group, part in enumerate((squash, one, two, three)):
            points_ref[group, rows, lanes] = part.astype(BF16)

    chunks(values_ref.shape, layer_one, 4)
    for part, group in enumerate(GROUP):
        inner_ref[part] = dot(points_ref[group], weights_ref[part])

    def layer_two(rows, lanes):
        z, zx, zy, lap, dif, mix, px, py = (inner_ref[part, rows, lanes] for part in range(8))
        squash = jnp.tanh(z)
        inner_ref[0, rows, lanes] = squash
        _, one, two, three = slopes(squash)
        radius = zx * zx + zy * zy
        twice = lap + lap
        bend = three * radius
        along = zx * (twice + dif) + zy * mix
        across = zy * (twice - dif) + zx * mix
        combos = (
            one * zx,
            one * zy,
            one * lap - two * radius,
            one * px + two * along - bend * zx,
            one * py + two * across - bend * zy,
        )
        for k, combo in enumerate(combos):
            combos_ref[k, rows, lanes] = combo.astype(BF16)

    chunks(values_ref.shape, layer_two, 4)


def project_kernel(weight, scale, feats_ref, combos_ref, forcing_ref, u_ref, cots_ref):
    @pl.when(pl.program_id(0) == 0)
    def _():
        u_ref[...] = jnp.zeros_like(u_ref)

    feats = feats_ref[...]
    px, py, om, omx, omy = (dot(feats, combos_ref[k], NT) * scale for k in range(5))
    slope = (py * omx - px * omy + DRAG * om - forcing_ref[...].astype(F32)) * weight
    total = u_ref[...]
    parts = (-slope * omy, slope * omx, DRAG * slope, slope * py, -slope * px)
    for k, part in enumerate(parts):
        cot = part.astype(BF16)
        cots_ref[k] = cot
        total += dot(cot, combos_ref[k])
    u_ref[...] = total


def backward_kernel(
    scale,
    squash_ref,
    points_ref,
    inner_ref,
    cots_ref,
    feats_ref,
    coords_ref,
    weights_ref,
    second_ref,
    consts_ref,
    pieces_ref,
    back_ref,
    inner_back_ref,
    ones_ref,
    one_back_ref,
    grads_ref,
    value_ref,
):
    step = pl.program_id(0)
    last = pl.num_programs(0) - 1
    width = second_ref.shape[0]

    @pl.when(step == 0)
    def _():
        grads_ref[...] = jnp.zeros_like(grads_ref)
        value_ref[...] = jnp.zeros_like(value_ref)

    feats = feats_ref[...]
    for k in range(5):
        back_ref[k] = dot(cots_ref[k], feats, TN) * scale

    def layer_two_back(rows, lanes):
        squash, zx, zy, lap, dif, mix, px, py = (inner_ref[part, rows, lanes] for part in range(8))
        gx, gy, gl, gp, gq = (back_ref[k, rows, lanes] for k in range(5))
        square, one, two, three = slopes(squash)
        four = two * (4.0 * square - 8.0 * one)
        radius = zx * zx + zy * zy
        twice = lap + lap
        plus, minus = twice + dif, twice - dif
        along = zx * plus + zy * mix
        across = zy * minus + zx * mix
        pull = gp * zx + gq * zy
        one_bar = gx * zx + gy * zy + gl * lap + gp * px + gq * py
        two_bar = gp * along + gq * across - gl * radius
        three_bar = pull * radius
        along_bar, across_bar = two * gp, two * gq
        turn = -2.0 * (two * gl + three * pull)
        bend = three * radius
        xa, yc = zx * along_bar, zy * across_bar
        parts = (
            two * one_bar + three * two_bar - four * three_bar,
            one * gx - bend * gp + zx * turn + along_bar * plus + across_bar * mix,
            one * gy - bend * gq + zy * turn + across_bar * minus + along_bar * mix,
            one * gl + 2.0 * (xa + yc),
            xa - yc,
            zy * along_bar + zx * across_bar,
            one * gp,
            one * gq,
        )
        for part, value in enumerate(parts):
            inner_back_ref[part, rows, lanes] = value.astype(BF16)

    chunks(squash_ref.shape, layer_two_back, 4)
    for part, group in enumerate(GROUP):
        grads_ref[part] += dot(points_ref[group], inner_back_ref[part], TN)
    for group in range(4):
        total = None
        for part in range(8):
            if GROUP[part] == group:
                term = dot(inner_back_ref[part], weights_ref[part], NT)
                total = term if total is None else total + term
        ones_ref[group] = total

    def layer_one_back(rows, lanes):
        square, one, two, three = slopes(squash_ref[rows, lanes])
        four = two * (4.0 * square - 8.0 * one)
        back = (
            one * ones_ref[0, rows, lanes]
            + two * ones_ref[1, rows, lanes]
            + three * ones_ref[2, rows, lanes]
            + four * ones_ref[3, rows, lanes]
        )
        one_back_ref[rows, lanes] = back.astype(BF16)

    chunks(squash_ref.shape, layer_one_back, 4)
    value_ref[...] += dot(coords_ref[...], one_back_ref[...])

    @pl.when(step == last)
    def _():
        second = second_ref[...].astype(F32)
        total = jnp.zeros((width, width), F32)
        first = [jnp.zeros((width, 1), F32)] * 2
        for part in range(8):
            grad = grads_ref[part]
            total += consts_ref[:, part : part + 1] * grad
            row = jnp.sum(second * grad, axis=1, keepdims=True)
            for axis in range(2):
                column = 8 * (axis + 1) + part
                first[axis] = first[axis] + consts_ref[:, column : column + 1] * row
        lane = lax.broadcasted_iota(jnp.int32, (width, LANES), 1)
        both = jnp.where(lane == 0, first[0], 0.0) + jnp.where(lane == 1, first[1], 0.0)
        first_grad = value_ref[0:2] + value_ref[2:4] + both.T[0:2]
        count, own, _ = pieces_ref.shape
        pieces_ref[...] = jnp.zeros_like(pieces_ref)
        across = width * width // (count * own)
        deep = LANES // across
        for core in range(2):
            for chunk in range(count // 2 // PTS):
                strip, row = divmod(chunk * PTS * own, width)
                lanes = core * LANES + strip * across
                place = (2 * chunk + core) * PTS
                block = total[row : row + PTS * own, lanes : lanes + across]
                pieces_ref[place : place + PTS, :, 0:across] = block.reshape(PTS, own, across)
            for axis in range(2):
                for strip in range(deep):
                    lanes = core * LANES + strip * across
                    row = axis * deep + strip
                    pieces_ref[core * PTS, row : row + 1, across : 2 * across] = first_grad[
                        axis : axis + 1, lanes : lanes + across
                    ]


def branch_kernel(
    scale,
    every_ref,
    two_ref,
    one_ref,
    columns_ref,
    third_ref,
    branch_third_ref,
    branch_second_ref,
    u_ref,
    feature_back_ref,
    back_two_ref,
    rows_ref,
):
    width = third_ref.shape[0]
    u = every_ref[:, :, 0:width].astype(F32).reshape(u_ref.shape).astype(BF16)
    u_ref[...] = u
    feature_back = (dot(u, third_ref[...]) * scale).astype(BF16)
    feature_back_ref[...] = feature_back
    two = two_ref[...]
    back_two = (dot(feature_back, branch_third_ref[...], NT) * (1.0 - two * two)).astype(BF16)
    back_two_ref[...] = back_two
    one = one_ref[...].astype(F32)
    back_one = (dot(back_two, branch_second_ref[...], NT) * (1.0 - one * one)).astype(BF16)
    rows = dot(columns_ref[...], back_one, TN)
    parts = [rows[:, lane : lane + LANES] for lane in range(0, rows.shape[1], LANES)]
    parts.append(jnp.sum(every_ref[:, :, width:].astype(F32), axis=0))
    rows_ref[...] = jnp.concatenate(parts, axis=0).astype(BF16)


def spread_kernel(core_ref, mine_ref, other_ref, grad_ref, second_ref, first_ref):
    half, step = pl.program_id(0), pl.program_id(1)
    fields = grad_ref.shape[0] // mine_ref.shape[0]
    own = mine_ref.shape[1] - 2 * fields
    across = LANES // 2
    steps = second_ref.shape[0] // own * 2 // mine_ref.shape[0]

    def place(from_ref):
        got = from_ref[...].astype(F32)
        for number in range(2):
            grad_ref[:, number * LANES : (number + 1) * LANES] = got[
                :, number * fields : (number + 1) * fields
            ].reshape(-1, LANES)
        tail = got[:, 2 * fields :]
        for now in range(steps):

            @pl.when(step == now)
            def _():
                strip, row = divmod(now * tail.shape[0] * own, second_ref.shape[0])
                second_ref[
                    row : row + tail.shape[0] * own, strip * across : (strip + 1) * across
                ] = tail[:, :, 0:across].reshape(-1, across)

        @pl.when(step == 0)
        def _():
            for axis in range(2):
                for strip in range(2):
                    row = 2 * axis + strip
                    first_ref[axis : axis + 1, strip * across : (strip + 1) * across] = tail[
                        0, row : row + 1, across : 2 * across
                    ]

    @pl.when(half == 0)
    def _():
        place(mine_ref)

    @pl.when(half == 1)
    def _():
        place(other_ref)


def whole(*shape):
    return pl.BlockSpec(shape, lambda i: (0,) * len(shape))


def constants(first):
    a, b = first[0], first[1]
    one, zero = jnp.ones_like(a), jnp.zeros_like(a)
    square = a * a + b * b
    consts = [one, a, b, -square, b * b - a * a, -2.0 * a * b, -a * square, -b * square]
    by_a = [zero, one, zero, -2.0 * a, -2.0 * a, -2.0 * b, -(3.0 * a * a + b * b), -2.0 * a * b]
    by_b = [zero, zero, one, -2.0 * b, 2.0 * b, -2.0 * a, -2.0 * a * b, -(a * a + 3.0 * b * b)]
    return consts, jnp.stack(consts + by_a + by_b, axis=1)


def tiles(points):
    tile = min(TILE, points)
    deep = lambda n, width: pl.BlockSpec((n, tile, width), lambda i: (0, i, 0))
    return tile, deep


def forward_call(values, weights):
    points, width = values.shape
    tile, deep = tiles(points)
    flat = pl.BlockSpec((tile, width), lambda i: (i, 0))
    return pl.pallas_call(
        forward_kernel,
        grid=(points // tile,),
        in_specs=[flat, whole(8, width, width)],
        out_specs=[flat, deep(4, width), deep(8, width), deep(5, width)],
        out_shape=[
            jax.ShapeDtypeStruct((points, width), F32),
            jax.ShapeDtypeStruct((4, points, width), BF16),
            jax.ShapeDtypeStruct((8, points, width), F32),
            jax.ShapeDtypeStruct((5, points, width), BF16),
        ],
        compiler_params=PARAMS,
        name="trunk_forward",
    )(values, weights)


def project_call(feats, combos, forcing, weight, scale):
    funcs, width = feats.shape
    points = combos.shape[1]
    tile, deep = tiles(points)
    return pl.pallas_call(
        functools.partial(project_kernel, weight, scale),
        grid=(points // tile,),
        in_specs=[
            whole(funcs, width),
            deep(5, width),
            pl.BlockSpec((funcs, tile), lambda i: (0, i)),
        ],
        out_specs=[whole(funcs, width), pl.BlockSpec((5, funcs, tile), lambda i: (0, 0, i))],
        out_shape=[
            jax.ShapeDtypeStruct((funcs, width), F32),
            jax.ShapeDtypeStruct((5, funcs, points), BF16),
        ],
        compiler_params=PARAMS,
        name="project",
    )(feats, combos, forcing)


def backward_call(squash, points_all, inner, cots, feats, coords, weights, second, consts, pieces, scale):
    points, width = squash.shape
    funcs = feats.shape[0]
    tile, deep = tiles(points)
    return pl.pallas_call(
        functools.partial(backward_kernel, scale),
        grid=(points // tile,),
        in_specs=[
            pl.BlockSpec((tile, width), lambda i: (i, 0)),
            deep(4, width),
            deep(8, width),
            pl.BlockSpec((5, funcs, tile), lambda i: (0, 0, i)),
            whole(funcs, width),
            pl.BlockSpec((16, tile), lambda i: (0, i)),
            whole(8, width, width),
            whole(width, width),
            whole(width, 24),
        ],
        out_specs=whole(*pieces),
        out_shape=jax.ShapeDtypeStruct(pieces, F32),
        scratch_shapes=[
            pltpu.VMEM((5, tile, width), F32),
            pltpu.VMEM((8, tile, width), BF16),
            pltpu.VMEM((4, tile, width), F32),
            pltpu.VMEM((tile, width), BF16),
            pltpu.VMEM((8, width, width), F32),
            pltpu.VMEM((16, width), F32),
        ],
        compiler_params=PARAMS,
        cost_estimate=pl.CostEstimate(
            flops=42 * points * width * width, bytes_accessed=48 * points * width, transcendentals=0
        ),
        name="trunk_backward",
    )(squash, points_all, inner, cots, feats, coords, weights, second, consts)


def branch_call(every, hidden_two, branch_one, columns, third, branch_third, branch_second, scale):
    shape = branch_one.shape
    rows = columns.shape[1] * (shape[1] // LANES) + every.shape[1]
    return pl.pallas_call(
        functools.partial(branch_kernel, scale),
        out_shape=[jax.ShapeDtypeStruct(shape, BF16)] * 3
        + [jax.ShapeDtypeStruct((rows, LANES), BF16)],
        compiler_params=pltpu.CompilerParams(vmem_limit_bytes=48 * 1024 * 1024),
        name="branch_backward",
    )(every, hidden_two, branch_one, columns, third, branch_third, branch_second)


def spread_call(core, mine, other, shape, width):
    steps = 4
    part = mine.shape[0] // steps
    half = lambda h, c: c[0] + h - 2 * c[0] * h
    block = (part, *mine.shape[1:])
    return pl.pallas_call(
        spread_kernel,
        grid_spec=pltpu.PrefetchScalarGridSpec(
            num_scalar_prefetch=1,
            grid=(2, steps),
            in_specs=[
                pl.BlockSpec(block, lambda h, j, c: (j * (1 - h) + (steps - 1) * h, 0, 0)),
                pl.BlockSpec(block, lambda h, j, c: (j * h, 0, 0)),
            ],
            out_specs=[
                pl.BlockSpec(
                    (shape[0] // (2 * steps), shape[1]),
                    lambda h, j, c: (half(h, c) * steps + j, 0),
                ),
                pl.BlockSpec((width, LANES), lambda h, j, c: (0, half(h, c))),
                pl.BlockSpec((2, LANES), lambda h, j, c: (0, half(h, c))),
            ],
        ),
        out_shape=[
            jax.ShapeDtypeStruct(shape, F32),
            jax.ShapeDtypeStruct((width, width), F32),
            jax.ShapeDtypeStruct((2, width), F32),
        ],
        compiler_params=pltpu.CompilerParams(
            dimension_semantics=("arbitrary", "arbitrary"), vmem_limit_bytes=48 * 1024 * 1024
        ),
        name="spread",
    )(core.reshape(1), mine, other)


def swap(parts, axes=AXES):
    return lax.all_to_all(parts, axes, split_axis=0, concat_axis=0, tiled=True)


def tell(part, count, axes=AXES):
    return swap(jnp.broadcast_to(part[None], (count, *part.shape)), axes)


def per_device(
    sensors,
    forcing,
    coords,
    branch_first,
    branch_second,
    branch_third,
    trunk_first,
    trunk_second,
    trunk_third,
):
    pairs, pts_size = lax.axis_size("pairs"), lax.axis_size("pts")
    func_size = 2 * pairs
    count = func_size * pts_size
    core = lax.axis_index("core")
    funcs = forcing.shape[0]
    weight = 1.0 / math.sqrt(funcs * func_size * forcing.shape[1] * pts_size)
    width_out = trunk_third.shape[1]
    width = trunk_second.shape[0]
    scale = width_out ** (-0.5)
    own = sensors.shape[0]
    fields = sensors.shape[1] // count

    own_one = jnp.tanh(dot(sensors, branch_first)).astype(BF16)
    blocks = (
        sensors.reshape(own, 2, pairs, pts_size, fields)
        .transpose(2, 1, 3, 0, 4)
        .reshape(count, own, fields)
    )
    sent = jnp.concatenate(
        [
            jnp.broadcast_to(own_one[None], (count, own, own_one.shape[1])),
            jnp.pad(blocks, ((0, 0), (0, 0), (0, LANES - fields))),
        ],
        axis=2,
    )
    got = swap(sent)

    consts, const_columns = constants(trunk_first)
    weights = (jnp.stack(consts)[:, :, None] * trunk_second.astype(F32)[None]).astype(BF16)
    values = coords[0][:, None] * trunk_first[0] + coords[1][:, None] * trunk_first[1]
    high = lax.reduce_precision(coords, 8, 7)
    coord_rows = jnp.pad(
        jnp.concatenate([high, coords - high], axis=0).astype(BF16), ((0, 12), (0, 0))
    )
    squash, points_all, inner, combos = forward_call(values, weights)

    branch_one = got[:, :, : own_one.shape[1]].reshape(count * own, -1)
    sensor_columns = got[:, :, own_one.shape[1] : own_one.shape[1] + fields].reshape(
        count * own, fields
    )
    hidden_two = jnp.tanh(dot(branch_one, branch_second))
    branch_two = hidden_two.astype(BF16)
    features = dot(branch_two, branch_third).astype(BF16)
    block = lax.dynamic_slice_in_dim(features, (2 * lax.axis_index("pairs") + core) * funcs, funcs, 0)
    feats = dot(block, trunk_third, NT).astype(BF16)

    u_part, cots = project_call(feats, combos, forcing, weight, scale)
    u_blocks = swap(u_part.astype(BF16).reshape(pts_size, own, width), "pts")
    u_own = u_blocks.astype(F32).sum(0).astype(BF16)

    second_pieces = backward_call(
        squash,
        points_all,
        inner,
        cots,
        feats,
        coord_rows,
        weights,
        trunk_second,
        const_columns,
        (count, own, LANES),
        scale,
    )
    pieces = jnp.concatenate(
        [jnp.broadcast_to(u_own[None], (count, own, width)), second_pieces.astype(BF16)], axis=2
    )
    every = swap(pieces)
    u, feature_back, back_two, rows = branch_call(
        every,
        hidden_two,
        branch_one,
        sensor_columns,
        trunk_third,
        branch_third,
        branch_second,
        scale,
    )
    mine = tell(rows, count // 2, ("pairs", "pts"))
    other = lax.ppermute(mine, "core", [(0, 1), (1, 0)])
    grad_b1, grad_t2, grad_t1 = spread_call(core, mine, other, branch_first.shape, width)
    grad_t3 = dot(u, features, TN) * scale
    grad_b3 = dot(branch_two, feature_back, TN)
    grad_b2 = dot(branch_one, back_two, TN)
    return (grad_b1, grad_b2, grad_b3, grad_t1, grad_t2, grad_t3)


def solution(mesh):
    func_size, pts_size = mesh.devices.shape
    cores = jax.sharding.Mesh(mesh.devices.reshape(func_size // 2, 2, pts_size), AXES)
    return jax.shard_map(
        per_device,
        mesh=cores,
        in_specs=(
            P(AXES, None),
            P(("pairs", "core"), "pts"),
            P(None, "pts"),
            P(),
            P(),
            P(),
            P(),
            P(),
            P(),
        ),
        out_specs=(P(), P(), P(), P(), P(), P()),
        check_vma=False,
    )
```

time: 162 us -> 151 us (0.932)
  waiting for transfers between devices: 33.5 us -> 13.7 us
  starting transfers between devices: 16.6 us -> 31 us
  blocking collectives: 35.4 us -> 23.7 us
  Pallas kernels: 37 us -> 44.3 us
  local copies, waits for them, and re-layouts: 13.4 us -> 19.4 us
  matrix products: 13.9 us -> 8.15 us
  other arithmetic: 10.6 us -> 8.93 us
    all_to_all x2 -> x3, waiting for transfers between devices: 33.5 us -> 13.7 us  [swap(): return lax.all_to_all(parts, axes, split_axis=0, concat_axis=0, tiled=True)]
    all_to_all x2 -> x3, starting transfers between devices: 16.6 us -> 29.3 us  [swap(): return lax.all_to_all(parts, axes, split_axis=0, concat_axis=0, tiled=True)]
    all_to_all x2 -> x1, blocking collectives: 35.4 us -> 23.7 us  [swap(): return lax.all_to_all(parts, axes, split_axis=0, concat_axis=0, tiled=True)]
    unnamed x35 -> x46, local copies, waits for them, and re-layouts: 5.16 us -> 13.4 us
    pallas_call x1 -> x5, Pallas kernels: 37 us -> 44.3 us  [the longest x1 21.3 us: backward_call(): pl.pallas_call(functools.partial(backward_kernel, scale), grid=(points //...]
    convert_element_type x5 -> x3, other arithmetic: 7.19 us -> 1.08 us  [the longest x1 1.03 us: per_device(): (jnp.stack(consts)[:, :, None] * trunk_second.astype(F32)[None]).astype(B...]
    dot_general x10 -> x7, matrix products: 13.9 us -> 8.15 us  [dot(): return lax.dot_general(left, right, dims, preferred_element_type=F32)]
    add x0 -> x1, other arithmetic: none -> 2.52 us  [per_device(): coords[0][:, None] * trunk_first[0] + coords[1][:, None] * trunk_first[1]]
  transfers between devices with their start and end apart: 2 -> 4, of which waited for: 2 -> 1; matrix products, arithmetic and copies ran while one was open for 8% -> 9% of each run, Pallas kernels for 0% -> 22%
where the time goes in v1:
time: 151 us; the launch traced here: 150 us
  Pallas kernels  44.3 us (29%)
  starting transfers between devices  31 us (21%)
  blocking collectives  23.7 us (16%)
  local copies, waits for them, and re-layouts  19.4 us (13%)
  waiting for transfers between devices  13.7 us (9%)
  other arithmetic  8.93 us (6%)
  matrix products  8.15 us (5%)
    all_to_all x3, starting transfers between devices, swap(): return lax.all_to_all(parts, axes, split_axis=0, concat_axis=0, tiled=True)  29.3 us
    all_to_all x1, blocking collectives, swap(): return lax.all_to_all(parts, axes, split_axis=0, concat_axis=0, tiled=True)  23.7 us
    pallas_call x1, Pallas kernels, backward_call(): pl.pallas_call(functools.partial(backward_kernel, scale), grid=(points //...  21.3 us
    all_to_all x3, waiting for transfers between devices, swap(): return lax.all_to_all(parts, axes, split_axis=0, concat_axis=0, tiled=True)  13.7 us
    unnamed x46, local copies, waits for them, and re-layouts  13.4 us
    pallas_call x1, Pallas kernels, forward_call(): pl.pallas_call(forward_kernel, grid=(points // tile,), in_specs=[flat, wh...  11.1 us
    dot_general x7, matrix products, dot(): return lax.dot_general(left, right, dims, preferred_element_type=F32)  8.15 us
    pallas_call x1, Pallas kernels, project_call(): pl.pallas_call(functools.partial(project_kernel, weight, scale), grid=(po...  6.03 us
  transfers between devices with their start and end apart: 4, of which 1 were waited for; matrix products, arithmetic and copies ran while one was open for 9% of the time, Pallas kernels for 22%

profile of v1, /device:TPU:1, one launch (start us, length us, event | category | flops | bytes accessed | tf_op | source)
XLA Modules:
  0.0 150.0 jit_solution(6707636932386477233)
XLA Ops:
  0.6 1.2 reshape.217
  2.3 1.2 fusion.1
  4.5 11.9 %all-to-all-start = ((bf16[128,8,384]{2,1,0:T(8,128)(2,1)}), bf16[128,8,384]{2,1,0:T(8,128)(2,1)}, u32[]{:S(2)}, u32[]{:S(2)}) async-start(bf16[128,8,384]{2,1,0:T(8,128)(2,1)} %fusion.2), calls=%async_computation | async-start | bytes 1572864 | tf_op jit(solution)/shard_map/all_to_all | solution.py:441
  19.4 2.5 %multiply_add_fusion.values_ref = f32[2048,256]{1,0:T(8,128)} fusion(f32[256]{0:T(256)} %bitcast.61, f32[2048]{0:T(1024)} %bitcast.59, f32[256]{0:T(256)} %bitcast.60, f32[2048]{0:T(1024)} %bitcast.58), kind=kLoop, calls=%fused_computation.1 | loop fusion | flops 1572864 | bytes 2115584 | tf_op jit(solution)/shard_map/add | solution.py:488
  22.9 1.6 %copy-done.3 = f32[2048,256]{1,0:T(8,128)S(1)} copy-done((f32[2048,256]{1,0:T(8,128)S(1)}, f32[2048,256]{1,0:T(8,128)}, u32[]{:S(2)}) %copy-start.3) | copy-done | bytes 2097176
  24.5 11.1 %trunk_forward.1 = (f32[2048,256]{1,0:T(8,128)S(1)}, bf16[4,2048,256]{2,1,0:T(8,128)(2,1)}, f32[8,2048,256]{2,1,0:T(8,128)}, bf16[5,2048,256]{2,1,0:T(8,128)(2,1)}) custom-call(f32[2048,256]{1,0:T(8,128)S(1)} %copy-done.3, bf16[8,256,256]{2,1,0:T(8,128)(2,1)S(1)} %multiply_convert_fusion.weights_ref), custom_call_target="tpu_custom_call" | custom-call | tf_op jit(solution)/shard_map/trunk_forward/pallas_call | solution.py:319
  35.6 1.3 copy-done.4
  37.6 1.4 convolution_tanh_fusion.two_ref
  39.0 1.2 convolution_convert_fusion
  41.1 6.0 %project.1 = (f32[64,256]{1,0:T(8,128)S(1)}, bf16[5,64,2048]{2,1,0:T(8,128)(2,1)S(1)}) custom-call(bf16[64,256]{1,0:T(8,128)(2,1)S(1)} %convolution_convert_fusion.1.feats_ref, bf16[5,2048,256]{2,1,0:T(8,128)(2,1)} %get-tuple-element.19.combos_ref, bf16[64,2048]{1,0:T(8,128)(2,1)S(1)} %copy-done.16), custom_call_target="tpu_custom_call" | custom-call | tf_op jit(solution)/shard_map/project/pallas_call | solution.py:339
  47.1 1.1 copy-done.7
  48.8 6.6 %all-to-all-start.1 = ((bf16[8,8,256]{2,1,0:T(8,128)(2,1)}), bf16[8,8,256]{2,1,0:T(8,128)(2,1)}, u32[]{:S(2)}, u32[]{:S(2)}) async-start(bf16[8,8,256]{2,1,0:T(8,128)(2,1)} %convert_bitcast_fusion), calls=%async_computation.1 | async-start | bytes 65536 | tf_op jit(solution)/shard_map/all_to_all | solution.py:441
  55.4 1.2 copy-done.2
  56.6 1.6 %copy-done.5 = f32[2048,256]{1,0:T(8,128)S(1)} copy-done((f32[2048,256]{1,0:T(8,128)S(1)}, f32[2048,256]{1,0:T(8,128)}, u32[]{:S(2)}) %copy-start.5) | copy-done | bytes 2097176
  58.2 1.3 copy-done.8
  61.1 21.3 %trunk_backward.1 = f32[128,8,128]{2,1,0:T(8,128)S(1)} custom-call(f32[2048,256]{1,0:T(8,128)S(1)} %copy-done.5, bf16[4,2048,256]{2,1,0:T(8,128)(2,1)} %get-tuple-element.22.points_ref, f32[8,2048,256]{2,1,0:T(8,128)} %get-tuple-element.23.inner_ref, bf16[5,64,2048]{2,1,0:T(8,128)(2,1)S(1)} %copy-done.8, bf16[64,256]{1,0:T(8,128)(2,1)S(1)} %copy-done.14, ...), custom_call_target="tpu_custom_call" | custom-call | flops 5637144576 | bytes 25165824 | tf_op jit(solution)/shard_map/trunk_backward/pallas_call | solution.py:361
  84.2 10.8 %all-to-all-start.2 = ((bf16[128,8,384]{2,1,0:T(8,128)(2,1)}), bf16[128,8,384]{2,1,0:T(8,128)(2,1)}, u32[]{:S(2)}, u32[]{:S(2)}) async-start(bf16[128,8,384]{2,1,0:T(8,128)(2,1)} %pad_maximum_fusion), calls=%async_computation.2 | async-start | bytes 1572864 | tf_op jit(solution)/shard_map/all_to_all | solution.py:441
  96.0 1.9 %slice_bitcast_fusion.one_ref = bf16[1024,256]{1,0:T(8,128)(2,1)} fusion(bf16[128,8,384]{2,1,0:T(8,128)(2,1)} %all-to-all-done), kind=kLoop, calls=%fused_computation.12 | loop fusion | bytes 1048576 | tf_op jit(solution)/shard_map/reshape | solution.py:495
  97.9 13.7 %all-to-all-done.2.every_ref = bf16[128,8,384]{2,1,0:T(8,128)(2,1)} async-done(((bf16[128,8,384]{2,1,0:T(8,128)(2,1)}), bf16[128,8,384]{2,1,0:T(8,128)(2,1)}, u32[]{:S(2)}, u32[]{:S(2)}) %all-to-all-start.2) | async-done | bytes 786464 | tf_op jit(solution)/shard_map/all_to_all | solution.py:441
  114.4 1.9 %branch_backward.1 = (bf16[1024,256]{1,0:T(8,128)(2,1)S(1)}, bf16[1024,256]{1,0:T(8,128)(2,1)S(1)}, bf16[1024,256]{1,0:T(8,128)(2,1)S(1)}, bf16[72,128]{1,0:T(8,128)(2,1)S(1)}) custom-call(bf16[128,8,384]{2,1,0:T(8,128)(2,1)} %all-to-all-done.2.every_ref, f32[1024,256]{1,0:T(8,128)S(1)} %convolution_tanh_fusion.two_ref, bf16[1024,256]{1,0:T(8,128)(2,1)S(1)} %copy-done.6, ...), custom_call_target="tpu_custom_call" | custom-call | tf_op jit(solution)/shard_map/branch_backward/pallas_call | solution.py:396
  116.5 23.7 %all_to_all.20.mine_ref = bf16[64,72,128]{2,1,0:T(8,128)(2,1)S(1)} all-to-all(bf16[64,72,128]{2,1,0:T(8,128)(2,1)S(1)} %broadcast_in_dim.8), channel_id=1, replica_groups=mesh['pairs'=8,'core'=2,'pts'=8] {'pairs','pts'}, dimensions={0} | all-to-all | bytes 2359296 | tf_op jit(solution)/shard_map/all_to_all | solution.py:441
  140.3 1.7 %collective-permute-start = (bf16[64,72,128]{2,1,0:T(8,128)(2,1)S(1)}, bf16[64,72,128]{2,1,0:T(8,128)(2,1)S(1)}, u32[]{:S(2)}, u32[]{:S(2)}) collective-permute-start(bf16[64,72,128]{2,1,0:T(8,128)(2,1)S(1)} %all_to_all.20.mine_ref), channel_id=1, source_target_pairs={{0,8},{8,0},{1,9},{9,1},{2,10},{10,2},{3,11},{11,3},{4,12},{12,4},... | collective-permute-start | bytes 3538952 | tf_op jit(solution)/shard_map/ppermute | solution.py:537
  143.0 2.1 %fusion.18 = f32[256,256]{1,0:T(8,128)} fusion(bf16[1024,256]{1,0:T(8,128)(2,1)S(1)} %get-tuple-element.27, bf16[128,8,384]{2,1,0:T(8,128)(2,1)} %all-to-all-done), kind=kOutput, calls=%fused_computation.50 | convolution fusion | flops 134217728 | bytes 1310720 | tf_op jit(solution)/shard_map/dot_general | solution.py:28
  146.2 3.9 %spread.1 = (f32[4096,256]{1,0:T(8,128)}, f32[256,256]{1,0:T(8,128)}, f32[2,256]{1,0:T(2,128)}) custom-call(s32[1]{0:T(128)} %bitcast.core_ref, bf16[64,72,128]{2,1,0:T(8,128)(2,1)S(1)} %all_to_all.20.mine_ref, bf16[64,72,128]{2,1,0:T(8,128)(2,1)S(1)} %collective-permute-done.other_ref), custom_call_target="tpu_custom_call" | custom-call | tf_op jit(solution)/shard_map/spread/pallas_call | solution.py:410
  (70 shorter events, 16.8 us)
Async XLA Ops:
  0.6 1.6 %copy-start = (bf16[4096,256]{1,0:T(8,128)(2,1)S(1)}, bf16[4096,256]{1,0:T(8,128)(2,1)}, u32[]{:S(2)}) copy-start(bf16[4096,256]{1,0:T(8,128)(2,1)} %param.12) | copy-start | bytes 6291460
  3.5 12.9 %copy-start.20 = (f32[2,256]{1,0:T(2,128)S(1)}, f32[2,256]{1,0:T(2,128)}, u32[]{:S(2)}) copy-start(f32[2,256]{1,0:T(2,128)} %param.15) | copy-start | bytes 6148
  3.5 13.5 %copy-start.19 = (f32[2,2048]{1,0:T(2,128)S(1)}, f32[2,2048]{1,0:T(2,128)}, u32[]{:S(2)}) copy-start(f32[2,2048]{1,0:T(2,128)} %param.11) | copy-start | bytes 49156
  3.5 14.1 %copy-start.9 = (bf16[256,256]{1,0:T(8,128)(2,1)S(1)}, bf16[256,256]{1,0:T(8,128)(2,1)}, u32[]{:S(2)}) copy-start(bf16[256,256]{1,0:T(8,128)(2,1)} %second_ref.1) | copy-start | bytes 393220
  4.5 33.1 %all-to-all-start = ((bf16[128,8,384]{2,1,0:T(8,128)(2,1)}), bf16[128,8,384]{2,1,0:T(8,128)(2,1)}, u32[]{:S(2)}, u32[]{:S(2)}) async-start(bf16[128,8,384]{2,1,0:T(8,128)(2,1)} %fusion.2), calls=%async_computation | async-start | bytes 1572864 | tf_op jit(solution)/shard_map/all_to_all | solution.py:441
  19.3 16.3 %copy-start.1 = (bf16[8,256,256]{2,1,0:T(8,128)(2,1)}, bf16[8,256,256]{2,1,0:T(8,128)(2,1)S(1)}, u32[]{:S(2)}) copy-start(bf16[8,256,256]{2,1,0:T(8,128)(2,1)S(1)} %multiply_convert_fusion.weights_ref) | copy-start | bytes 3145732
  19.3 3.4 %copy-start.21 = (f32[256,1]{0,1:T(1,128)S(1)}, f32[256,1]{0,1:T(1,128)}, u32[]{:S(2)}) copy-start(f32[256,1]{0,1:T(1,128)} %get-tuple-element.46) | copy-start | bytes 3076
  19.3 3.4 %copy-start.22 = (f32[256,1]{0,1:T(1,128)S(1)}, f32[256,1]{0,1:T(1,128)}, u32[]{:S(2)}) copy-start(f32[256,1]{0,1:T(1,128)} %get-tuple-element.50) | copy-start | bytes 3076
  22.9 1.6 %copy-start.3 = (f32[2048,256]{1,0:T(8,128)S(1)}, f32[2048,256]{1,0:T(8,128)}, u32[]{:S(2)}) copy-start(f32[2048,256]{1,0:T(8,128)} %multiply_add_fusion.values_ref) | copy-start | bytes 6291460
  35.6 1.3 copy-start.4
  36.9 3.3 %copy-start.10 = (bf16[256,256]{1,0:T(8,128)(2,1)S(1)}, bf16[256,256]{1,0:T(8,128)(2,1)}, u32[]{:S(2)}) copy-start(bf16[256,256]{1,0:T(8,128)(2,1)} %third_ref.1) | copy-start | bytes 393220
  37.6 3.4 %copy-start.16 = (bf16[64,2048]{1,0:T(8,128)(2,1)S(1)}, bf16[64,2048]{1,0:T(8,128)(2,1)}, u32[]{:S(2)}) copy-start(bf16[64,2048]{1,0:T(8,128)(2,1)} %forcing_ref.1) | copy-start | bytes 786436
  41.1 6.0 %copy-start.13 = (bf16[64,256]{1,0:T(8,128)(2,1)}, bf16[64,256]{1,0:T(8,128)(2,1)S(1)}, u32[]{:S(2)}) copy-start(bf16[64,256]{1,0:T(8,128)(2,1)S(1)} %convolution_convert_fusion.1.feats_ref) | copy-start | bytes 98308
  47.1 1.1 copy-start.7
  48.8 33.7 %all-to-all-start.1 = ((bf16[8,8,256]{2,1,0:T(8,128)(2,1)}), bf16[8,8,256]{2,1,0:T(8,128)(2,1)}, u32[]{:S(2)}, u32[]{:S(2)}) async-start(bf16[8,8,256]{2,1,0:T(8,128)(2,1)} %convert_bitcast_fusion), calls=%async_computation.1 | async-start | bytes 65536 | tf_op jit(solution)/shard_map/all_to_all | solution.py:441
  55.4 1.2 copy-start.2
  56.6 1.6 %copy-start.5 = (f32[2048,256]{1,0:T(8,128)S(1)}, f32[2048,256]{1,0:T(8,128)}, u32[]{:S(2)}) copy-start(f32[2048,256]{1,0:T(8,128)} %copy-done.4) | copy-start | bytes 6291460
  58.2 1.3 copy-start.8
  84.2 27.3 %all-to-all-start.2 = ((bf16[128,8,384]{2,1,0:T(8,128)(2,1)}), bf16[128,8,384]{2,1,0:T(8,128)(2,1)}, u32[]{:S(2)}, u32[]{:S(2)}) async-start(bf16[128,8,384]{2,1,0:T(8,128)(2,1)} %pad_maximum_fusion), calls=%async_computation.2 | async-start | bytes 1572864 | tf_op jit(solution)/shard_map/all_to_all | solution.py:441
  111.6 1.0 copy-start.6
  112.6 0.9 copy-start.11
  113.5 0.9 copy-start.12
  116.4 25.6 %copy-start.18 = (bf16[1024,256]{1,0:T(8,128)(2,1)S(1)}, bf16[1024,256]{1,0:T(8,128)(2,1)}, u32[]{:S(2)}) copy-start(bf16[1024,256]{1,0:T(8,128)(2,1)} %copy-done.17) | copy-start | bytes 1572868
  140.3 5.9 %collective-permute-start = (bf16[64,72,128]{2,1,0:T(8,128)(2,1)S(1)}, bf16[64,72,128]{2,1,0:T(8,128)(2,1)S(1)}, u32[]{:S(2)}, u32[]{:S(2)}) collective-permute-start(bf16[64,72,128]{2,1,0:T(8,128)(2,1)S(1)} %all_to_all.20.mine_ref), channel_id=1, source_target_pairs={{0,8},{8,0},{1,9},{9,1},{2,10},{10,2},{3,11},{11,3},{4,12},{12,4},... | collective-permute-start | bytes 3538952 | tf_op jit(solution)/shard_map/ppermute | solution.py:537
  (3 other events, 2.4 us)

commit v2 on v1

v2 whole, which is shorter than its diff:
```python
import functools
import math

import jax
import jax.numpy as jnp
from jax import lax
from jax.experimental import pallas as pl
from jax.experimental.pallas import tpu as pltpu
from jax.sharding import PartitionSpec as P

DRAG = 0.5
TILE = 512
ROWS = 16
LANES = 128
F32 = jnp.float32
BF16 = jnp.bfloat16
AXES = ("pairs", "core", "pts")
GROUP = (0, 1, 1, 2, 2, 2, 3, 3)
NT = (((1,), (1,)), ((), ()))
TN = (((0,), (0,)), ((), ()))
PARAMS = pltpu.CompilerParams(
    dimension_semantics=("arbitrary",), vmem_limit_bytes=40 * 1024 * 1024
)
SMALL = pltpu.CompilerParams(vmem_limit_bytes=16 * 1024 * 1024)


def dot(left, right, dims=(((1,), (0,)), ((), ()))):
    return lax.dot_general(left, right, dims, preferred_element_type=F32)


def slopes(squash):
    square = squash * squash
    one = 1.0 - square
    two = -2.0 * (squash * one)
    three = one * (4.0 * square - 2.0 * one)
    return square, one, two, three


def chunks(shape, body, unroll):
    def one(index, carry):
        start = pl.multiple_of(index * ROWS, ROWS)
        for lane in range(0, shape[1], LANES):
            body(pl.ds(start, ROWS), pl.ds(lane, LANES))
        return carry

    lax.fori_loop(0, shape[0] // ROWS, one, 0, unroll=unroll)


def constants(first):
    a, b = first[0:1], first[1:2]
    one, zero = jnp.ones_like(a), jnp.zeros_like(a)
    square = a * a + b * b
    consts = [one, a, b, -square, b * b - a * a, -2.0 * a * b, -a * square, -b * square]
    by_a = [zero, one, zero, -2.0 * a, -2.0 * a, -2.0 * b, -(3.0 * a * a + b * b), -2.0 * a * b]
    by_b = [zero, zero, one, -2.0 * b, 2.0 * b, -2.0 * a, -2.0 * a * b, -(a * a + 3.0 * b * b)]
    return jnp.concatenate(consts + by_a + by_b, axis=0).T


def thirds(value):
    parts = []
    for _ in range(3):
        part = value.astype(BF16).astype(F32)
        parts.append(part)
        value = value - part
    return parts


def forward_kernel(
    coords_ref,
    first_ref,
    second_ref,
    squash_ref,
    points_ref,
    inner_ref,
    combos_ref,
    weights_ref,
    values_ref,
):
    @pl.when(pl.program_id(0) == 0)
    def _():
        consts = constants(first_ref[...])
        second = second_ref[...].astype(F32)
        for part in range(8):
            weights_ref[part] = (consts[:, part : part + 1] * second).astype(BF16)

    left, right = thirds(coords_ref[...]), thirds(first_ref[...])
    pairs = ((0, 0), (0, 1), (1, 0), (0, 2), (2, 0), (1, 1))
    left = [left[i] for i, _ in pairs] + [jnp.zeros_like(left[0])] * 2
    right = [right[j] for _, j in pairs] + [jnp.zeros_like(right[0])] * 2
    values_ref[...] = dot(
        jnp.concatenate(left, axis=0).astype(BF16), jnp.concatenate(right, axis=0).astype(BF16), TN
    )

    def layer_one(rows, lanes):
        squash = jnp.tanh(values_ref[rows, lanes])
        _, one, two, three = slopes(squash)
        squash_ref[rows, lanes] = squash
        for group, part in enumerate((squash, one, two, three)):
            points_ref[group, rows, lanes] = part.astype(BF16)

    chunks(values_ref.shape, layer_one, 4)
    for part, group in enumerate(GROUP):
        inner_ref[part] = dot(points_ref[group], weights_ref[part])

    def layer_two(rows, lanes):
        z, zx, zy, lap, dif, mix, px, py = (inner_ref[part, rows, lanes] for part in range(8))
        squash = jnp.tanh(z)
        inner_ref[0, rows, lanes] = squash
        _, one, two, three = slopes(squash)
        radius = zx * zx + zy * zy
        twice = lap + lap
        bend = three * radius
        along = zx * (twice + dif) + zy * mix
        across = zy * (twice - dif) + zx * mix
        combos = (
            one * zx,
            one * zy,
            one * lap - two * radius,
            one * px + two * along - bend * zx,
            one * py + two * across - bend * zy,
        )
        for k, combo in enumerate(combos):
            combos_ref[k, rows, lanes] = combo.astype(BF16)

    chunks(values_ref.shape, layer_two, 4)


def project_kernel(
    weight,
    scale,
    pair_ref,
    got_ref,
    branch_second_ref,
    branch_third_ref,
    third_ref,
    combos_ref,
    forcing_ref,
    u_ref,
    cots_ref,
    feats_ref,
):
    @pl.when(pl.program_id(0) == 0)
    def _():
        u_ref[...] = jnp.zeros_like(u_ref)
        width = third_ref.shape[0]
        one = got_ref[:, :, 0:width].astype(F32).reshape(-1, width).astype(BF16)
        two = jnp.tanh(dot(one, branch_second_ref[...])).astype(BF16)
        features = dot(two, branch_third_ref[...]).astype(BF16)
        feats_ref[...] = dot(features, third_ref[...], NT).astype(BF16)

    feats = feats_ref[...]
    px, py, om, omx, omy = (dot(feats, combos_ref[k], NT) * scale for k in range(5))
    slope = (py * omx - px * omy + DRAG * om - forcing_ref[...].astype(F32)) * weight
    total = u_ref[...]
    parts = (-slope * omy, slope * omx, DRAG * slope, slope * py, -slope * px)
    for k, part in enumerate(parts):
        cot = part.astype(BF16)
        cots_ref[k] = cot
        total += dot(cot, combos_ref[k])
    u_ref[...] = total


def backward_kernel(
    scale,
    squash_ref,
    points_ref,
    inner_ref,
    cots_ref,
    feats_ref,
    coords_ref,
    weights_ref,
    first_ref,
    second_ref,
    pieces_ref,
    back_ref,
    inner_back_ref,
    ones_ref,
    one_back_ref,
    grads_ref,
    value_ref,
):
    step = pl.program_id(0)
    last = pl.num_programs(0) - 1
    width = second_ref.shape[0]

    @pl.when(step == 0)
    def _():
        grads_ref[...] = jnp.zeros_like(grads_ref)
        value_ref[...] = jnp.zeros_like(value_ref)

    feats = feats_ref[...]
    for k in range(5):
        back_ref[k] = dot(cots_ref[k], feats, TN) * scale

    def layer_two_back(rows, lanes):
        squash, zx, zy, lap, dif, mix, px, py = (inner_ref[part, rows, lanes] for part in range(8))
        gx, gy, gl, gp, gq = (back_ref[k, rows, lanes] for k in range(5))
        square, one, two, three = slopes(squash)
        four = two * (4.0 * square - 8.0 * one)
        radius = zx * zx + zy * zy
        twice = lap + lap
        plus, minus = twice + dif, twice - dif
        along = zx * plus + zy * mix
        across = zy * minus + zx * mix
        pull = gp * zx + gq * zy
        one_bar = gx * zx + gy * zy + gl * lap + gp * px + gq * py
        two_bar = gp * along + gq * across - gl * radius
        three_bar = pull * radius
        along_bar, across_bar = two * gp, two * gq
        turn = -2.0 * (two * gl + three * pull)
        bend = three * radius
        xa, yc = zx * along_bar, zy * across_bar
        parts = (
            two * one_bar + three * two_bar - four * three_bar,
            one * gx - bend * gp + zx * turn + along_bar * plus + across_bar * mix,
            one * gy - bend * gq + zy * turn + across_bar * minus + along_bar * mix,
            one * gl + 2.0 * (xa + yc),
            xa - yc,
            zy * along_bar + zx * across_bar,
            one * gp,
            one * gq,
        )
        for part, value in enumerate(parts):
            inner_back_ref[part, rows, lanes] = value.astype(BF16)

    chunks(squash_ref.shape, layer_two_back, 4)
    for part, group in enumerate(GROUP):
        grads_ref[part] += dot(points_ref[group], inner_back_ref[part], TN)
    for group in range(4):
        total = None
        for part in range(8):
            if GROUP[part] == group:
                term = dot(inner_back_ref[part], weights_ref[part], NT)
                total = term if total is None else total + term
        ones_ref[group] = total

    def layer_one_back(rows, lanes):
        square, one, two, three = slopes(squash_ref[rows, lanes])
        four = two * (4.0 * square - 8.0 * one)
        back = (
            one * ones_ref[0, rows, lanes]
            + two * ones_ref[1, rows, lanes]
            + three * ones_ref[2, rows, lanes]
            + four * ones_ref[3, rows, lanes]
        )
        one_back_ref[rows, lanes] = back.astype(BF16)

    chunks(squash_ref.shape, layer_one_back, 4)
    coords = jnp.concatenate(thirds(coords_ref[...]) + [jnp.zeros_like(coords_ref)] * 5, axis=0)
    value_ref[...] += dot(coords.astype(BF16), one_back_ref[...])

    @pl.when(step == last)
    def _():
        second = second_ref[...].astype(F32)
        consts = constants(first_ref[...])
        total = jnp.zeros((width, width), F32)
        first = [jnp.zeros((width, 1), F32)] * 2
        for part in range(8):
            grad = grads_ref[part]
            total += consts[:, part : part + 1] * grad
            row = jnp.sum(second * grad, axis=1, keepdims=True)
            for axis in range(2):
                column = 8 * (axis + 1) + part
                first[axis] = first[axis] + consts[:, column : column + 1] * row
        lane = lax.broadcasted_iota(jnp.int32, (width, LANES), 1)
        both = jnp.where(lane == 0, first[0], 0.0) + jnp.where(lane == 1, first[1], 0.0)
        first_grad = value_ref[0:2] + value_ref[2:4] + value_ref[4:6] + both.T[0:2]
        count, own, _ = pieces_ref.shape
        strips = width // LANES
        part = count // strips
        for strip in range(strips):
            block = total[:, strip * LANES : (strip + 1) * LANES]
            pieces_ref[strip * part : (strip + 1) * part, :, 0:LANES] = block.reshape(
                part, own, LANES
            )
        rows = [
            first_grad[axis : axis + 1, strip * LANES : (strip + 1) * LANES]
            for axis in range(2)
            for strip in range(strips)
        ]
        rows.append(jnp.zeros((own - len(rows), LANES), F32))
        told = jnp.concatenate(rows, axis=0)
        pieces_ref[:, :, LANES:] = jnp.broadcast_to(told[None], (count, own, LANES))


def hidden_kernel(
    core_ref,
    mine_ref,
    other_ref,
    branch_second_ref,
    branch_third_ref,
    one_ref,
    wide_ref,
    two_ref,
    features_ref,
    columns_ref,
):
    core = core_ref[0]
    width = branch_second_ref.shape[0]
    half, fields = one_ref.shape[0] // 2, columns_ref.shape[1]
    for place, from_ref in ((core, mine_ref), (1 - core, other_ref)):
        rows = pl.ds(pl.multiple_of(place * half, half), half)
        got = from_ref[...].astype(F32).reshape(half, -1)
        one_ref[rows, :] = got[:, 0:width].astype(BF16)
        columns_ref[rows, :] = jnp.where(
            core == 0,
            got[:, width : width + fields],
            got[:, width + fields : width + 2 * fields],
        ).astype(BF16)
    wide = jnp.tanh(dot(one_ref[...], branch_second_ref[...]))
    wide_ref[...] = wide
    two = wide.astype(BF16)
    two_ref[...] = two
    features_ref[...] = dot(two, branch_third_ref[...]).astype(BF16)


def branch_kernel(
    scale,
    core_ref,
    mine_ref,
    other_ref,
    two_ref,
    one_ref,
    columns_ref,
    third_ref,
    branch_third_ref,
    branch_second_ref,
    u_ref,
    feature_back_ref,
    back_two_ref,
    rows_ref,
    first_ref,
):
    core = core_ref[0]
    width = third_ref.shape[0]
    half = u_ref.shape[0] // 2
    total = None
    for place, from_ref in ((core, mine_ref), (1 - core, other_ref)):
        rows = pl.ds(pl.multiple_of(place * half, half), half)
        u_ref[rows, :] = from_ref[:, :, 0:width].astype(F32).reshape(half, width).astype(BF16)
        part = jnp.sum(from_ref[:, :, width:].astype(F32), axis=0)
        total = part if total is None else total + part
    feature_back = (dot(u_ref[...], third_ref[...]) * scale).astype(BF16)
    feature_back_ref[...] = feature_back
    two = two_ref[...]
    back_two = (dot(feature_back, branch_third_ref[...], NT) * (1.0 - two * two)).astype(BF16)
    back_two_ref[...] = back_two
    one = one_ref[...].astype(F32)
    back_one = (dot(back_two, branch_second_ref[...], NT) * (1.0 - one * one)).astype(BF16)
    rows = dot(columns_ref[...], back_one, TN)
    parts = [rows[:, lane : lane + LANES] for lane in range(0, width, LANES)]
    rows_ref[...] = jnp.concatenate(parts + [total[:, 0:LANES]], axis=0).astype(BF16)
    strips = width // LANES
    for axis in range(2):
        for strip in range(strips):
            first_ref[axis : axis + 1, strip * LANES : (strip + 1) * LANES] = total[
                axis * strips + strip : axis * strips + strip + 1, LANES:
            ]


def gradient_kernel(
    scale,
    u_ref,
    features_ref,
    two_ref,
    feature_back_ref,
    one_ref,
    back_two_ref,
    trunk_ref,
    third_ref,
    second_ref,
):
    trunk_ref[...] = dot(u_ref[...], features_ref[...], TN) * scale
    third_ref[...] = dot(two_ref[...], feature_back_ref[...], TN)
    second_ref[...] = dot(one_ref[...], back_two_ref[...], TN)


def spread_kernel(core_ref, mine_ref, other_ref, grad_ref, second_ref):
    first = core_ref[0] == 0
    step = pl.program_id(0)
    count = mine_ref.shape[0]
    fields = grad_ref.shape[0] // (2 * count)
    mine, other = mine_ref[...].astype(F32), other_ref[...].astype(F32)
    for lane in range(grad_ref.shape[1] // LANES):
        parts = [got[:, lane * fields : (lane + 1) * fields] for got in (mine, other)]
        block = jnp.stack(
            [jnp.where(first, parts[0], parts[1]), jnp.where(first, parts[1], parts[0])], axis=1
        )
        grad_ref[:, lane * LANES : (lane + 1) * LANES] = block.reshape(-1, LANES)
    tail = mine[:, -8:].reshape(-1, LANES)
    width = second_ref.shape[0]
    for now in range(width * width // tail.size):

        @pl.when(step == now)
        def _():
            strip, row = divmod(now * tail.shape[0], width)
            second_ref[row : row + tail.shape[0], strip * LANES : (strip + 1) * LANES] = tail


def whole(*shape):
    return pl.BlockSpec(shape, lambda i: (0,) * len(shape))


def there(value):
    return pltpu.with_memory_space_constraint(value, pltpu.HBM)


SCALAR = pl.BlockSpec(memory_space=pltpu.SMEM)
LOCAL = pl.BlockSpec(memory_space=pltpu.VMEM)


def tiles(points):
    tile = min(TILE, points)
    deep = lambda n, width: pl.BlockSpec((n, tile, width), lambda i: (0, i, 0))
    return tile, deep


def forward_call(coords, first, second):
    points, width = coords.shape[1], first.shape[1]
    tile, deep = tiles(points)
    flat = pl.BlockSpec((tile, width), lambda i: (i, 0))
    return pl.pallas_call(
        forward_kernel,
        grid=(points // tile,),
        in_specs=[
            pl.BlockSpec((2, tile), lambda i: (0, i)),
            whole(2, width),
            whole(width, width),
        ],
        out_specs=[flat, deep(4, width), deep(8, width), deep(5, width), whole(8, width, width)],
        out_shape=[
            pltpu.HBM((points, width), F32),
            pltpu.HBM((4, points, width), BF16),
            pltpu.HBM((8, points, width), F32),
            pltpu.HBM((5, points, width), BF16),
            pltpu.HBM((8, width, width), BF16),
        ],
        scratch_shapes=[pltpu.VMEM((tile, width), F32)],
        compiler_params=PARAMS,
        name="trunk_forward",
    )(coords, first, second)


def project_call(
    pair, got, branch_second, branch_third, third, combos, forcing, pts_size, weight, scale
):
    funcs, points = forcing.shape
    width = third.shape[0]
    tile, _ = tiles(points)
    flat = lambda *shape: pl.BlockSpec(shape, lambda i, p: (0,) * len(shape))
    return pl.pallas_call(
        functools.partial(project_kernel, weight, scale),
        grid_spec=pltpu.PrefetchScalarGridSpec(
            num_scalar_prefetch=1,
            grid=(points // tile,),
            in_specs=[
                pl.BlockSpec((pts_size, *got.shape[1:]), lambda i, p: (p[0], 0, 0)),
                flat(width, width),
                flat(width, width),
                flat(width, width),
                pl.BlockSpec((5, tile, width), lambda i, p: (0, i, 0)),
                pl.BlockSpec((funcs, tile), lambda i, p: (0, i)),
            ],
            out_specs=[
                flat(funcs, width),
                pl.BlockSpec((5, funcs, tile), lambda i, p: (0, 0, i)),
                flat(funcs, width),
            ],
        ),
        out_shape=[
            jax.ShapeDtypeStruct((funcs, width), F32),
            pltpu.HBM((5, funcs, points), BF16),
            pltpu.HBM((funcs, width), BF16),
        ],
        compiler_params=PARAMS,
        name="project",
    )(pair, there(got), branch_second, branch_third, third, there(combos), there(forcing))


def backward_call(
    squash, points_all, inner, cots, feats, coords, weights, first, second, pieces, scale
):
    points, width = squash.shape
    funcs = feats.shape[0]
    tile, deep = tiles(points)
    return pl.pallas_call(
        functools.partial(backward_kernel, scale),
        grid=(points // tile,),
        in_specs=[
            pl.BlockSpec((tile, width), lambda i: (i, 0)),
            deep(4, width),
            deep(8, width),
            pl.BlockSpec((5, funcs, tile), lambda i: (0, 0, i)),
            whole(funcs, width),
            pl.BlockSpec((2, tile), lambda i: (0, i)),
            whole(8, width, width),
            whole(2, width),
            whole(width, width),
        ],
        out_specs=whole(*pieces),
        out_shape=jax.ShapeDtypeStruct(pieces, F32),
        scratch_shapes=[
            pltpu.VMEM((5, tile, width), F32),
            pltpu.VMEM((8, tile, width), BF16),
            pltpu.VMEM((4, tile, width), F32),
            pltpu.VMEM((tile, width), BF16),
            pltpu.VMEM((8, width, width), F32),
            pltpu.VMEM((16, width), F32),
        ],
        compiler_params=PARAMS,
        cost_estimate=pl.CostEstimate(
            flops=42 * points * width * width, bytes_accessed=48 * points * width, transcendentals=0
        ),
        name="trunk_backward",
    )(
        there(squash),
        there(points_all),
        there(inner),
        there(cots),
        there(feats),
        coords,
        there(weights),
        first,
        second,
    )


def hidden_call(core, mine, other, branch_second, branch_third, fields):
    rows, width = 2 * mine.shape[0] * mine.shape[1], branch_second.shape[0]
    return pl.pallas_call(
        hidden_kernel,
        in_specs=[SCALAR] + [LOCAL] * 4,
        out_shape=[
            jax.ShapeDtypeStruct((rows, width), BF16),
            jax.ShapeDtypeStruct((rows, width), F32),
            jax.ShapeDtypeStruct((rows, width), BF16),
            jax.ShapeDtypeStruct((rows, width), BF16),
            jax.ShapeDtypeStruct((rows, fields), BF16),
        ],
        compiler_params=SMALL,
        name="branch_hidden",
    )(core, mine, other, branch_second, branch_third)


def branch_call(core, mine, other, two, one, columns, third, branch_third, branch_second, scale):
    shape = one.shape
    rows = columns.shape[1] * (shape[1] // LANES) + mine.shape[1]
    return pl.pallas_call(
        functools.partial(branch_kernel, scale),
        in_specs=[SCALAR] + [LOCAL] * 8,
        out_shape=[jax.ShapeDtypeStruct(shape, BF16)] * 3
        + [jax.ShapeDtypeStruct((rows, LANES), BF16), jax.ShapeDtypeStruct((2, shape[1]), F32)],
        compiler_params=SMALL,
        name="branch_backward",
    )(core, mine, other, two, one, columns, third, branch_third, branch_second)


def gradient_call(u, features, two, feature_back, one, back_two, scale):
    shape = (u.shape[1], features.shape[1])
    return pl.pallas_call(
        functools.partial(gradient_kernel, scale),
        in_specs=[LOCAL] * 6,
        out_shape=[jax.ShapeDtypeStruct(shape, F32)] * 3,
        compiler_params=SMALL,
        name="branch_gradients",
    )(u, features, two, feature_back, one, back_two)


def spread_call(core, mine, other, shape, width):
    steps = 4
    block = (mine.shape[0] // steps, *mine.shape[1:])
    piece = pl.BlockSpec(block, lambda j: (j, 0, 0))
    return pl.pallas_call(
        spread_kernel,
        grid=(steps,),
        in_specs=[SCALAR, piece, piece],
        out_specs=[
            pl.BlockSpec((shape[0] // steps, shape[1]), lambda j: (j, 0)),
            whole(width, width),
        ],
        out_shape=[jax.ShapeDtypeStruct(shape, F32), jax.ShapeDtypeStruct((width, width), F32)],
        compiler_params=PARAMS,
        name="spread",
    )(core, mine, other)


def swap(parts, axes):
    return lax.all_to_all(parts, axes, split_axis=0, concat_axis=0, tiled=True)


def across_chip(value):
    return lax.ppermute(value, "core", [(0, 1), (1, 0)])


def per_device(
    sensors,
    forcing,
    coords,
    branch_first,
    branch_second,
    branch_third,
    trunk_first,
    trunk_second,
    trunk_third,
):
    pairs, pts_size = lax.axis_size("pairs"), lax.axis_size("pts")
    func_size = 2 * pairs
    chips = pairs * pts_size
    core = lax.axis_index("core").reshape(1)
    pair = lax.axis_index("pairs").reshape(1)
    funcs = forcing.shape[0]
    weight = 1.0 / math.sqrt(funcs * func_size * forcing.shape[1] * pts_size)
    width_out = trunk_third.shape[1]
    width = trunk_second.shape[0]
    scale = width_out ** (-0.5)
    own = sensors.shape[0]
    fields = sensors.shape[1] // chips

    own_one = jnp.tanh(dot(sensors, branch_first)).astype(BF16)
    blocks = sensors.reshape(own, chips, fields).transpose(1, 0, 2)
    sent = jnp.concatenate(
        [
            jnp.broadcast_to(own_one[None], (chips, own, width)),
            jnp.pad(blocks, ((0, 0), (0, 0), (0, -fields % LANES))),
        ],
        axis=2,
    )
    got = swap(sent, ("pairs", "pts"))
    squash, points_all, inner, combos, weights = forward_call(coords, trunk_first, trunk_second)
    u_part, cots, feats = project_call(
        pair,
        got,
        branch_second,
        branch_third,
        trunk_third,
        combos,
        forcing,
        pts_size,
        weight,
        scale,
    )
    got_other = across_chip(got)

    u_blocks = swap(u_part.astype(BF16).reshape(pts_size, own, width), "pts")
    u_own = u_blocks.astype(F32).sum(0).astype(BF16)
    second_pieces = backward_call(
        squash,
        points_all,
        inner,
        cots,
        feats,
        coords,
        weights,
        trunk_first,
        trunk_second,
        (chips, own, 2 * LANES),
        scale,
    )
    pieces = jnp.concatenate(
        [jnp.broadcast_to(u_own[None], (chips, own, width)), second_pieces.astype(BF16)], axis=2
    )
    every = swap(pieces, ("pairs", "pts"))
    every_other = across_chip(every)

    one, wide, two, features, columns = hidden_call(
        core, got, got_other, branch_second, branch_third, fields // 2
    )
    u, feature_back, back_two, rows, grad_t1 = branch_call(
        core,
        every,
        every_other,
        wide,
        one,
        columns,
        trunk_third,
        branch_third,
        branch_second,
        scale,
    )
    mine = swap(jnp.broadcast_to(rows[None], (chips, *rows.shape)), ("pairs", "pts"))
    other = across_chip(mine)
    grad_t3, grad_b3, grad_b2 = gradient_call(
        u, features, two, feature_back, one, back_two, scale
    )
    grad_b1, grad_t2 = spread_call(core, mine, other, branch_first.shape, width)
    return (grad_b1, grad_b2, grad_b3, grad_t1, grad_t2, grad_t3)


def solution(mesh):
    func_size, pts_size = mesh.devices.shape
    cores = jax.sharding.Mesh(mesh.devices.reshape(func_size // 2, 2, pts_size), AXES)
    return jax.shard_map(
        per_device,
        mesh=cores,
        in_specs=(
            P(AXES, None),
            P(("pairs", "core"), "pts"),
            P(None, "pts"),
            P(),
            P(),
            P(),
            P(),
            P(),
            P(),
        ),
        out_specs=(P(), P(), P(), P(), P(), P()),
        check_vma=False,
    )
```

time: 151 us -> 128 us (0.85)
  blocking collectives: 23.7 us -> 44.8 us
  local copies, waits for them, and re-layouts: 19.4 us -> 2.67 us
  waiting for transfers between devices: 13.7 us -> 3.32 us
  starting transfers between devices: 31 us -> 23.3 us
  other arithmetic: 8.93 us -> 1.48 us
  matrix products: 8.15 us -> 1.3 us
  Pallas kernels: 44.3 us -> 49.7 us
    all_to_all x1 -> x2, blocking collectives: 23.7 us -> 44.8 us  [swap(): return lax.all_to_all(parts, axes, split_axis=0, concat_axis=0, tiled=True)]
    all_to_all x3 -> x2, waiting for transfers between devices: 13.7 us -> 0.01 us  [swap(): return lax.all_to_all(parts, axes, split_axis=0, concat_axis=0, tiled=True)]
    unnamed x46 -> x18, local copies, waits for them, and re-layouts: 13.4 us -> 1.21 us
    all_to_all x3 -> x2, starting transfers between devices: 29.3 us -> 18.2 us  [swap(): return lax.all_to_all(parts, axes, split_axis=0, concat_axis=0, tiled=True)]
    dot_general x7 -> x1, matrix products: 8.15 us -> 1.3 us  [dot(): return lax.dot_general(left, right, dims, preferred_element_type=F32)]
    pallas_call x4 -> x6, Pallas kernels: 23 us -> 28 us  [the longest x1 13.1 us: forward_call(): pl.pallas_call(forward_kernel, grid=(points // tile,), in_specs=[pl.Block...]
    ppermute x1 -> x3, starting transfers between devices: 1.73 us -> 5.13 us  [across_chip(): return lax.ppermute(value, 'core', [(0, 1), (1, 0)])]
    ppermute x1 -> x3, waiting for transfers between devices: 0.01 us -> 3.32 us  [across_chip(): return lax.ppermute(value, 'core', [(0, 1), (1, 0)])]
  transfers between devices with their start and end apart: 4 -> 5, of which waited for: 1 -> 2; matrix products, arithmetic and copies ran while one was open for 9% -> 0% of each run, Pallas kernels for 22% -> 30%
where the time goes in v2:
time: 128 us; the launch traced here: 127 us
  Pallas kernels  49.7 us (39%)
  blocking collectives  44.8 us (35%)
  starting transfers between devices  23.3 us (18%)
  waiting for transfers between devices  3.32 us (3%)
  local copies, waits for them, and re-layouts  2.67 us (2%)
  other arithmetic  1.48 us (1%)
  matrix products  1.3 us (1%)
    all_to_all x2, blocking collectives, swap(): return lax.all_to_all(parts, axes, split_axis=0, concat_axis=0, tiled=True)  44.8 us
    pallas_call x1, Pallas kernels, backward_call(): pl.pallas_call(functools.partial(backward_kernel, scale), grid=(points //...  21.6 us
    all_to_all x2, starting transfers between devices, swap(): return lax.all_to_all(parts, axes, split_axis=0, concat_axis=0, tiled=True)  18.2 us
    pallas_call x1, Pallas kernels, forward_call(): pl.pallas_call(forward_kernel, grid=(points // tile,), in_specs=[pl.Block...  13.1 us
    pallas_call x1, Pallas kernels, project_call(): pl.pallas_call(functools.partial(project_kernel, weight, scale), grid_spe...  7.07 us
    ppermute x3, starting transfers between devices, across_chip(): return lax.ppermute(value, 'core', [(0, 1), (1, 0)])  5.13 us
    ppermute x3, waiting for transfers between devices, across_chip(): return lax.ppermute(value, 'core', [(0, 1), (1, 0)])  3.32 us
  transfers between devices with their start and end apart: 5, of which 2 were waited for; matrix products, arithmetic and copies ran while one was open for 0% of the time, Pallas kernels for 30%

profile of v2, /device:TPU:1, one launch (start us, length us, event | category | flops | bytes accessed | tf_op | source)
XLA Modules:
  0.0 127.4 jit_solution(15996508363393456637)
XLA Ops:
  0.6 0.0 copy-start
  0.6 1.2 reshape.29
  1.8 0.4 copy-done
  2.3 1.3 %fusion = bf16[8,256]{1,0:T(8,128)(2,1)S(1)} fusion(bf16[8,4096]{1,0:T(8,128)(2,1)} %param.9, bf16[4096,256]{1,0:T(8,128)(2,1)S(1)} %copy-done), kind=kOutput, calls=%fused_computation.1 | convolution fusion | flops 16779264 | bytes 2166784 | tf_op jit(solution)/shard_map/dot_general | solution.py:28
  3.6 0.1 copy.17
  3.7 0.8 fusion.2
  4.5 12.0 %all-to-all-start = ((bf16[64,8,384]{2,1,0:T(8,128)(2,1)}), bf16[64,8,384]{2,1,0:T(8,128)(2,1)S(1)}, u32[]{:S(2)}, u32[]{:S(2)}) async-start(bf16[64,8,384]{2,1,0:T(8,128)(2,1)} %fusion.2), calls=%async_computation | async-start | bytes 786432 | tf_op jit(solution)/shard_map/all_to_all | solution.py:588
  16.5 13.1 %trunk_forward.1 = (f32[2048,256]{1,0:T(8,128)}, bf16[4,2048,256]{2,1,0:T(8,128)(2,1)}, f32[8,2048,256]{2,1,0:T(8,128)}, bf16[5,2048,256]{2,1,0:T(8,128)(2,1)}, bf16[8,256,256]{2,1,0:T(8,128)(2,1)}) custom-call(f32[2,2048]{1,0:T(2,128)S(1)} %copy-done.7, f32[2,256]{1,0:T(2,128)S(1)} %copy-done.8, bf16[256,256]{1,0:T(8,128)(2,1)S(1)} %copy-done.5), custom_call_target="tpu_custom_call" | custom-call | tf_op jit(solution)/shard_map/trunk_forward/pallas_call | solution.py:422
  29.7 0.7 copy-done.1
  30.4 7.1 %project.1 = (f32[64,256]{1,0:T(8,128)S(1)}, bf16[5,64,2048]{2,1,0:T(8,128)(2,1)}, bf16[64,256]{1,0:T(8,128)(2,1)}) custom-call(s32[1]{0:T(128)} %bitcast.1.pair_ref, bf16[64,8,384]{2,1,0:T(8,128)(2,1)} %copy-done.1, bf16[256,256]{1,0:T(8,128)(2,1)S(1)} %copy-done.3, bf16[256,256]{1,0:T(8,128)(2,1)S(1)} %copy-done.4, bf16[256,256]{1,0:T(8,128)(2,1)S(1)} %copy-done.6, ...), custom_call_target="tpu_custom_call" | custom-call | tf_op jit(solution)/shard_map/project/pallas_call | solution.py:451
  37.5 0.6 convert_bitcast_fusion
  38.1 6.2 %all-to-all-start.1 = ((bf16[8,8,256]{2,1,0:T(8,128)(2,1)}), bf16[8,8,256]{2,1,0:T(8,128)(2,1)S(1)}, u32[]{:S(2)}, u32[]{:S(2)}) async-start(bf16[8,8,256]{2,1,0:T(8,128)(2,1)} %convert_bitcast_fusion), calls=%async_computation.1 | async-start | bytes 65536 | tf_op jit(solution)/shard_map/all_to_all | solution.py:588
  44.3 21.6 %trunk_backward.1 = f32[64,8,256]{2,1,0:T(8,128)S(1)} custom-call(f32[2048,256]{1,0:T(8,128)} %get-tuple-element.31.squash_ref, bf16[4,2048,256]{2,1,0:T(8,128)(2,1)} %get-tuple-element.32.points_ref, f32[8,2048,256]{2,1,0:T(8,128)} %get-tuple-element.33.inner_ref, bf16[5,64,2048]{2,1,0:T(8,128)(2,1)} %get-tuple-element.34.cots_ref, ...), custom_call_target="tpu_custom_call" | custom-call | flops 5637144576 | bytes 25165824 | tf_op jit(solution)/shard_map/trunk_backward/pallas_call | solution.py:486
  66.1 21.0 %all_to_all.20.mine_ref = bf16[64,8,512]{2,1,0:T(8,128)(2,1)S(1)} all-to-all(bf16[64,8,512]{2,1,0:T(8,128)(2,1)S(1)} %pad_maximum_fusion), channel_id=1, replica_groups=mesh['pairs'=8,'core'=2,'pts'=8] {'pairs','pts'}, dimensions={0} | all-to-all | bytes 1048576 | tf_op jit(solution)/shard_map/all_to_all | solution.py:588
  87.1 3.2 %collective-permute-start = (bf16[64,8,512]{2,1,0:T(8,128)(2,1)S(1)}, bf16[64,8,512]{2,1,0:T(8,128)(2,1)}, u32[]{:S(2)}, u32[]{:S(2)}) collective-permute-start(bf16[64,8,512]{2,1,0:T(8,128)(2,1)S(1)} %all_to_all.20.mine_ref), channel_id=1, source_target_pairs={{0,8},{8,0},{1,9},{9,1},{2,10},{10,2},{3,11},{11,3},{4,12},{12,4},... | collective-permute-start | bytes 1572872 | tf_op jit(solution)/shard_map/ppermute | solution.py:592
  90.4 2.2 %collective-permute-done.1.other_ref = bf16[64,8,384]{2,1,0:T(8,128)(2,1)} collective-permute-done((bf16[64,8,384]{2,1,0:T(8,128)(2,1)S(1)}, bf16[64,8,384]{2,1,0:T(8,128)(2,1)}, u32[]{:S(2)}, u32[]{:S(2)}) %collective-permute-start.1) | collective-permute-done | bytes 393248 | tf_op jit(solution)/shard_map/ppermute | solution.py:592
  92.6 1.5 %branch_hidden.1 = (bf16[1024,256]{1,0:T(8,128)(2,1)S(1)}, f32[1024,256]{1,0:T(8,128)S(1)}, bf16[1024,256]{1,0:T(8,128)(2,1)S(1)}, bf16[1024,256]{1,0:T(8,128)(2,1)S(1)}, bf16[1024,32]{1,0:T(8,128)(2,1)S(1)}) custom-call(s32[1]{0:T(128)} %bitcast.core_ref, bf16[64,8,384]{2,1,0:T(8,128)(2,1)S(1)} %copy-done.2, ...), custom_call_target="tpu_custom_call" | custom-call | tf_op jit(solution)/shard_map/branch_hidden/pallas_call | solution.py:530
  94.2 2.4 %branch_backward.1 = (bf16[1024,256]{1,0:T(8,128)(2,1)S(1)}, bf16[1024,256]{1,0:T(8,128)(2,1)S(1)}, bf16[1024,256]{1,0:T(8,128)(2,1)S(1)}, bf16[72,128]{1,0:T(8,128)(2,1)S(1)}, f32[2,256]{1,0:T(2,128)}) custom-call(s32[1]{0:T(128)} %bitcast.core_ref, bf16[64,8,512]{2,1,0:T(8,128)(2,1)S(1)} %all_to_all.20.mine_ref, ...), custom_call_target="tpu_custom_call" | custom-call | tf_op jit(solution)/shard_map/branch_backward/pallas_call | solution.py:548
  96.6 0.2 broadcast_in_dim.8
  96.7 23.8 %all_to_all.21.mine_ref = bf16[64,72,128]{2,1,0:T(8,128)(2,1)S(1)} all-to-all(bf16[64,72,128]{2,1,0:T(8,128)(2,1)S(1)} %broadcast_in_dim.8), channel_id=1, replica_groups=mesh['pairs'=8,'core'=2,'pts'=8] {'pairs','pts'}, dimensions={0} | all-to-all | bytes 2359296 | tf_op jit(solution)/shard_map/all_to_all | solution.py:588
  120.5 1.9 %collective-permute-start.2 = (bf16[64,72,128]{2,1,0:T(8,128)(2,1)S(1)}, bf16[64,72,128]{2,1,0:T(8,128)(2,1)S(1)}, u32[]{:S(2)}, u32[]{:S(2)}) collective-permute-start(bf16[64,72,128]{2,1,0:T(8,128)(2,1)S(1)} %all_to_all.21.mine_ref), channel_id=1, source_target_pairs={{0,8},{8,0},{1,9},{9,1},{2,10},{10,2},{3,11},{11,3},{4,12},{12,4},... | collective-permute-start | bytes 3538952 | tf_op jit(solution)/shard_map/ppermute | solution.py:592
  122.4 1.4 %branch_gradients.1 = (f32[256,256]{1,0:T(8,128)}, f32[256,256]{1,0:T(8,128)}, f32[256,256]{1,0:T(8,128)}) custom-call(bf16[1024,256]{1,0:T(8,128)(2,1)S(1)} %get-tuple-element.42.u_ref, bf16[1024,256]{1,0:T(8,128)(2,1)S(1)} %get-tuple-element.43.features_ref, bf16[1024,256]{1,0:T(8,128)(2,1)S(1)} %get-tuple-element.44.two_ref, ...), custom_call_target="tpu_custom_call" | custom-call | tf_op jit(solution)/shard_map/branch_gradients/pallas_call | solution.py:560
  123.7 1.1 collective-permute-done.2.other_ref
  124.8 2.6 %spread.1 = (f32[4096,256]{1,0:T(8,128)}, f32[256,256]{1,0:T(8,128)}) custom-call(s32[1]{0:T(128)} %bitcast.core_ref, bf16[64,72,128]{2,1,0:T(8,128)(2,1)S(1)} %all_to_all.21.mine_ref, bf16[64,72,128]{2,1,0:T(8,128)(2,1)S(1)} %collective-permute-done.2.other_ref), custom_call_target="tpu_custom_call" | custom-call | tf_op jit(solution)/shard_map/spread/pallas_call | solution.py:573
  (24 shorter events, 0.2 us)
Async XLA Ops:
  0.6 1.6 %copy-start = (bf16[4096,256]{1,0:T(8,128)(2,1)S(1)}, bf16[4096,256]{1,0:T(8,128)(2,1)}, u32[]{:S(2)}) copy-start(bf16[4096,256]{1,0:T(8,128)(2,1)} %param.12) | copy-start | bytes 6291460
  2.3 14.2 %copy-start.5 = (bf16[256,256]{1,0:T(8,128)(2,1)S(1)}, bf16[256,256]{1,0:T(8,128)(2,1)}, u32[]{:S(2)}) copy-start(bf16[256,256]{1,0:T(8,128)(2,1)} %second_ref.3) | copy-start | bytes 393220
  2.3 14.2 %copy-start.7 = (f32[2,2048]{1,0:T(2,128)S(1)}, f32[2,2048]{1,0:T(2,128)}, u32[]{:S(2)}) copy-start(f32[2,2048]{1,0:T(2,128)} %coords_ref.3) | copy-start | bytes 49156
  2.3 14.2 %copy-start.8 = (f32[2,256]{1,0:T(2,128)S(1)}, f32[2,256]{1,0:T(2,128)}, u32[]{:S(2)}) copy-start(f32[2,256]{1,0:T(2,128)} %first_ref.3) | copy-start | bytes 6148
  2.3 28.1 %copy-start.3 = (bf16[256,256]{1,0:T(8,128)(2,1)S(1)}, bf16[256,256]{1,0:T(8,128)(2,1)}, u32[]{:S(2)}) copy-start(bf16[256,256]{1,0:T(8,128)(2,1)} %branch_second_ref.5) | copy-start | bytes 393220
  2.3 28.1 %copy-start.4 = (bf16[256,256]{1,0:T(8,128)(2,1)S(1)}, bf16[256,256]{1,0:T(8,128)(2,1)}, u32[]{:S(2)}) copy-start(bf16[256,256]{1,0:T(8,128)(2,1)} %branch_third_ref.5) | copy-start | bytes 393220
  2.3 28.1 %copy-start.6 = (bf16[256,256]{1,0:T(8,128)(2,1)S(1)}, bf16[256,256]{1,0:T(8,128)(2,1)}, u32[]{:S(2)}) copy-start(bf16[256,256]{1,0:T(8,128)(2,1)} %third_ref.3) | copy-start | bytes 393220
  4.5 25.1 %all-to-all-start = ((bf16[64,8,384]{2,1,0:T(8,128)(2,1)}), bf16[64,8,384]{2,1,0:T(8,128)(2,1)S(1)}, u32[]{:S(2)}, u32[]{:S(2)}) async-start(bf16[64,8,384]{2,1,0:T(8,128)(2,1)} %fusion.2), calls=%async_computation | async-start | bytes 786432 | tf_op jit(solution)/shard_map/all_to_all | solution.py:588
  29.6 0.7 copy-start.1
  38.1 27.9 %all-to-all-start.1 = ((bf16[8,8,256]{2,1,0:T(8,128)(2,1)}), bf16[8,8,256]{2,1,0:T(8,128)(2,1)S(1)}, u32[]{:S(2)}, u32[]{:S(2)}) async-start(bf16[8,8,256]{2,1,0:T(8,128)(2,1)} %convert_bitcast_fusion), calls=%async_computation.1 | async-start | bytes 65536 | tf_op jit(solution)/shard_map/all_to_all | solution.py:588
  65.9 24.4 %copy-start.2 = (bf16[64,8,384]{2,1,0:T(8,128)(2,1)S(1)}, bf16[64,8,384]{2,1,0:T(8,128)(2,1)}, u32[]{:S(2)}) copy-start(bf16[64,8,384]{2,1,0:T(8,128)(2,1)} %copy-done.1) | copy-start | bytes 1179652
  87.1 7.0 %collective-permute-start = (bf16[64,8,512]{2,1,0:T(8,128)(2,1)S(1)}, bf16[64,8,512]{2,1,0:T(8,128)(2,1)}, u32[]{:S(2)}, u32[]{:S(2)}) collective-permute-start(bf16[64,8,512]{2,1,0:T(8,128)(2,1)S(1)} %all_to_all.20.mine_ref), channel_id=1, source_target_pairs={{0,8},{8,0},{1,9},{9,1},{2,10},{10,2},{3,11},{11,3},{4,12},{12,4},... | collective-permute-start | bytes 1572872 | tf_op jit(solution)/shard_map/ppermute | solution.py:592
  90.4 2.2 %collective-permute-start.1 = (bf16[64,8,384]{2,1,0:T(8,128)(2,1)S(1)}, bf16[64,8,384]{2,1,0:T(8,128)(2,1)}, u32[]{:S(2)}, u32[]{:S(2)}) collective-permute-start(bf16[64,8,384]{2,1,0:T(8,128)(2,1)S(1)} %copy-done.2), channel_id=1, source_target_pairs={{0,8},{8,0},{1,9},{9,1},{2,10},{10,2},{3,11},{11,3},{4,12},{12,4},... | collective-permute-start | bytes 1179656 | tf_op jit(solution)/shard_map/ppermute | solution.py:592
  120.5 4.4 %collective-permute-start.2 = (bf16[64,72,128]{2,1,0:T(8,128)(2,1)S(1)}, bf16[64,72,128]{2,1,0:T(8,128)(2,1)S(1)}, u32[]{:S(2)}, u32[]{:S(2)}) collective-permute-start(bf16[64,72,128]{2,1,0:T(8,128)(2,1)S(1)} %all_to_all.21.mine_ref), channel_id=1, source_target_pairs={{0,8},{8,0},{1,9},{9,1},{2,10},{10,2},{3,11},{11,3},{4,12},{12,4},... | collective-permute-start | bytes 3538952 | tf_op jit(solution)/shard_map/ppermute | solution.py:592

commit v3 on v2

--- a/solution.py
+++ b/solution.py
@@ -10,7 +10,10 @@
 
 DRAG = 0.5
 TILE = 512
+PROJECT = 1024
 ROWS = 16
+PARTS = 2
+CHUNK = 256
 LANES = 128
 F32 = jnp.float32
 BF16 = jnp.bfloat16
@@ -21,7 +24,7 @@
 PARAMS = pltpu.CompilerParams(
     dimension_semantics=("arbitrary",), vmem_limit_bytes=40 * 1024 * 1024
 )
-SMALL = pltpu.CompilerParams(vmem_limit_bytes=16 * 1024 * 1024)
+SMALL = pltpu.CompilerParams(vmem_limit_bytes=24 * 1024 * 1024)
 
 
 def dot(left, right, dims=(((1,), (0,)), ((), ()))):
@@ -36,14 +39,10 @@
     return square, one, two, three
 
 
-def chunks(shape, body, unroll):
-    def one(index, carry):
-        start = pl.multiple_of(index * ROWS, ROWS)
-        for lane in range(0, shape[1], LANES):
+def chunks(rows, width, body):
+    for start in range(*rows, ROWS):
+        for lane in range(0, width, LANES):
             body(pl.ds(start, ROWS), pl.ds(lane, LANES))
-        return carry
-
-    lax.fori_loop(0, shape[0] // ROWS, one, 0, unroll=unroll)
 
 
 def constants(first):
@@ -69,12 +68,13 @@
     coords_ref,
     first_ref,
     second_ref,
+    points_ref,
     squash_ref,
-    points_ref,
     inner_ref,
     combos_ref,
     weights_ref,
     values_ref,
+    wide_ref,
 ):
     @pl.when(pl.program_id(0) == 0)
     def _():
@@ -94,18 +94,16 @@
     def layer_one(rows, lanes):
         squash = jnp.tanh(values_ref[rows, lanes])
         _, one, two, three = slopes(squash)
-        squash_ref[rows, lanes] = squash
         for group, part in enumerate((squash, one, two, three)):
             points_ref[group, rows, lanes] = part.astype(BF16)
 
-    chunks(values_ref.shape, layer_one, 4)
-    for part, group in enumerate(GROUP):
-        inner_ref[part] = dot(points_ref[group], weights_ref[part])
 
     def layer_two(rows, lanes):
-        z, zx, zy, lap, dif, mix, px, py = (inner_ref[part, rows, lanes] for part in range(8))
+        z, zx, zy, lap, dif, mix, px, py = (wide_ref[part, rows, lanes] for part in range(8))
         squash = jnp.tanh(z)
-        inner_ref[0, rows, lanes] = squash
+        squash_ref[rows, lanes] = squash
+        for part, value in enumerate((zx, zy, lap, dif, mix, px, py)):
+            inner_ref[part, rows, lanes] = value.astype(BF16)
         _, one, two, three = slopes(squash)
         radius = zx * zx + zy * zy
         twice = lap + lap
@@ -122,42 +120,58 @@
         for k, combo in enumerate(combos):
             combos_ref[k, rows, lanes] = combo.astype(BF16)
 
-    chunks(values_ref.shape, layer_two, 4)
+    tile, width = values_ref.shape
+    part_rows = tile // max(1, min(PARTS, tile // LANES))
+    for start in range(0, tile, part_rows):
+        rows = (start, start + part_rows)
+        chunks(rows, width, layer_one)
+        span = pl.ds(start, part_rows)
+        for part, group in enumerate(GROUP):
+            wide_ref[part, span] = dot(points_ref[group, span], weights_ref[part])
+    for start in range(0, tile, part_rows):
+        chunks((start, start + part_rows), width, layer_two)
 
 
 def project_kernel(
     weight,
     scale,
-    pair_ref,
-    got_ref,
+    ones_ref,
     branch_second_ref,
     branch_third_ref,
     third_ref,
     combos_ref,
     forcing_ref,
-    u_ref,
     cots_ref,
     feats_ref,
+    shares_ref,
+    u_ref,
 ):
     @pl.when(pl.program_id(0) == 0)
     def _():
         u_ref[...] = jnp.zeros_like(u_ref)
-        width = third_ref.shape[0]
-        one = got_ref[:, :, 0:width].astype(F32).reshape(-1, width).astype(BF16)
+        one = ones_ref[...].astype(F32).reshape(u_ref.shape).astype(BF16)
         two = jnp.tanh(dot(one, branch_second_ref[...])).astype(BF16)
         features = dot(two, branch_third_ref[...]).astype(BF16)
         feats_ref[...] = dot(features, third_ref[...], NT).astype(BF16)
 
     feats = feats_ref[...]
-    px, py, om, omx, omy = (dot(feats, combos_ref[k], NT) * scale for k in range(5))
-    slope = (py * omx - px * omy + DRAG * om - forcing_ref[...].astype(F32)) * weight
+    tile = forcing_ref.shape[1]
+    for start in range(0, tile, min(CHUNK, tile)):
+        span = pl.ds(start, min(CHUNK, tile))
+        px, py, om, omx, omy = (dot(feats, combos_ref[k, span], NT) * scale for k in range(5))
+        residual = py * omx - px * omy + DRAG * om - forcing_ref[:, span].astype(F32)
+        slope = residual * weight
+        parts = (-slope * omy, slope * omx, DRAG * slope, slope * py, -slope * px)
+        for k, part in enumerate(parts):
+            cots_ref[k, :, span] = part.astype(BF16)
     total = u_ref[...]
-    parts = (-slope * omy, slope * omx, DRAG * slope, slope * py, -slope * px)
-    for k, part in enumerate(parts):
-        cot = part.astype(BF16)
-        cots_ref[k] = cot
-        total += dot(cot, combos_ref[k])
+    for k in range(5):
+        total += dot(cots_ref[k], combos_ref[k])
     u_ref[...] = total
+
+    @pl.when(pl.program_id(0) == pl.num_programs(0) - 1)
+    def _():
+        shares_ref[...] = u_ref[...].reshape(shares_ref.shape).astype(BF16)
 
 
 def backward_kernel(
@@ -189,11 +203,12 @@
         value_ref[...] = jnp.zeros_like(value_ref)
 
     feats = feats_ref[...]
-    for k in range(5):
-        back_ref[k] = dot(cots_ref[k], feats, TN) * scale
 
     def layer_two_back(rows, lanes):
-        squash, zx, zy, lap, dif, mix, px, py = (inner_ref[part, rows, lanes] for part in range(8))
+        squash = squash_ref[rows, lanes]
+        zx, zy, lap, dif, mix, px, py = (
+            inner_ref[part, rows, lanes].astype(F32) for part in range(7)
+        )
         gx, gy, gl, gp, gq = (back_ref[k, rows, lanes] for k in range(5))
         square, one, two, three = slopes(squash)
         four = two * (4.0 * square - 8.0 * one)
@@ -223,20 +238,9 @@
         for part, value in enumerate(parts):
             inner_back_ref[part, rows, lanes] = value.astype(BF16)
 
-    chunks(squash_ref.shape, layer_two_back, 4)
-    for part, group in enumerate(GROUP):
-        grads_ref[part] += dot(points_ref[group], inner_back_ref[part], TN)
-    for group in range(4):
-        total = None
-        for part in range(8):
-            if GROUP[part] == group:
-                term = dot(inner_back_ref[part], weights_ref[part], NT)
-                total = term if total is None else total + term
-        ones_ref[group] = total
-
     def layer_one_back(rows, lanes):
-        square, one, two, three = slopes(squash_ref[rows, lanes])
-        four = two * (4.0 * square - 8.0 * one)
+        squash, one, two, three = (points_ref[part, rows, lanes].astype(F32) for part in range(4))
+        four = two * (4.0 * (squash * squash) - 8.0 * one)
         back = (
             one * ones_ref[0, rows, lanes]
             + two * ones_ref[1, rows, lanes]
@@ -245,7 +249,25 @@
         )
         one_back_ref[rows, lanes] = back.astype(BF16)
 
-    chunks(squash_ref.shape, layer_one_back, 4)
+    tile = squash_ref.shape[0]
+    part_rows = tile // max(1, min(PARTS, tile // LANES))
+    spans = [(start, start + part_rows) for start in range(0, tile, part_rows)]
+    for start, stop in spans:
+        for k in range(5):
+            back_ref[k, start:stop] = dot(cots_ref[k, :, start:stop], feats, TN) * scale
+    for start, stop in spans:
+        chunks((start, stop), width, layer_two_back)
+        for group in range(4):
+            total = None
+            for part in range(8):
+                if GROUP[part] == group:
+                    term = dot(inner_back_ref[part, start:stop], weights_ref[part], NT)
+                    total = term if total is None else total + term
+            ones_ref[group, start:stop] = total
+    for part, group in enumerate(GROUP):
+        grads_ref[part] += dot(points_ref[group], inner_back_ref[part], TN)
+    for start, stop in spans:
+        chunks((start, stop), width, layer_one_back)
     coords = jnp.concatenate(thirds(coords_ref[...]) + [jnp.zeros_like(coords_ref)] * 5, axis=0)
     value_ref[...] += dot(coords.astype(BF16), one_back_ref[...])
 
@@ -253,15 +275,15 @@
     def _():
         second = second_ref[...].astype(F32)
         consts = constants(first_ref[...])
-        total = jnp.zeros((width, width), F32)
-        first = [jnp.zeros((width, 1), F32)] * 2
-        for part in range(8):
-            grad = grads_ref[part]
-            total += consts[:, part : part + 1] * grad
-            row = jnp.sum(second * grad, axis=1, keepdims=True)
-            for axis in range(2):
-                column = 8 * (axis + 1) + part
-                first[axis] = first[axis] + consts[:, column : column + 1] * row
+        g = [grads_ref[part] for part in range(8)]
+        column = lambda part: consts[:, part : part + 1]
+        total = g[0]
+        for part in range(1, 8):
+            total += column(part) * g[part]
+        both, less = g[3] + g[4], g[3] - g[4]
+        by_a = g[1] + column(11) * both + column(13) * g[5] + column(14) * g[6] + column(15) * g[7]
+        by_b = g[2] + column(19) * less + column(21) * g[5] + column(22) * g[6] + column(23) * g[7]
+        first = [jnp.sum(second * by, axis=1, keepdims=True) for by in (by_a, by_b)]
         lane = lax.broadcasted_iota(jnp.int32, (width, LANES), 1)
         both = jnp.where(lane == 0, first[0], 0.0) + jnp.where(lane == 1, first[1], 0.0)
         first_grad = value_ref[0:2] + value_ref[2:4] + value_ref[4:6] + both.T[0:2]
@@ -273,45 +295,14 @@
             pieces_ref[strip * part : (strip + 1) * part, :, 0:LANES] = block.reshape(
                 part, own, LANES
             )
+        across = 2 * width // own
         rows = [
-            first_grad[axis : axis + 1, strip * LANES : (strip + 1) * LANES]
+            first_grad[axis : axis + 1, lane : lane + across]
             for axis in range(2)
-            for strip in range(strips)
+            for lane in range(0, width, across)
         ]
-        rows.append(jnp.zeros((own - len(rows), LANES), F32))
         told = jnp.concatenate(rows, axis=0)
-        pieces_ref[:, :, LANES:] = jnp.broadcast_to(told[None], (count, own, LANES))
-
-
-def hidden_kernel(
-    core_ref,
-    mine_ref,
-    other_ref,
-    branch_second_ref,
-    branch_third_ref,
-    one_ref,
-    wide_ref,
-    two_ref,
-    features_ref,
-    columns_ref,
-):
-    core = core_ref[0]
-    width = branch_second_ref.shape[0]
-    half, fields = one_ref.shape[0] // 2, columns_ref.shape[1]
-    for place, from_ref in ((core, mine_ref), (1 - core, other_ref)):
-        rows = pl.ds(pl.multiple_of(place * half, half), half)
-        got = from_ref[...].astype(F32).reshape(half, -1)
-        one_ref[rows, :] = got[:, 0:width].astype(BF16)
-        columns_ref[rows, :] = jnp.where(
-            core == 0,
-            got[:, width : width + fields],
-            got[:, width + fields : width + 2 * fields],
-        ).astype(BF16)
-    wide = jnp.tanh(dot(one_ref[...], branch_second_ref[...]))
-    wide_ref[...] = wide
-    two = wide.astype(BF16)
-    two_ref[...] = two
-    features_ref[...] = dot(two, branch_third_ref[...]).astype(BF16)
+        pieces_ref[:, :, LANES:] = jnp.broadcast_to(told[None], (count, *told.shape))
 
 
 def branch_kernel(
@@ -319,42 +310,55 @@
     core_ref,
     mine_ref,
     other_ref,
-    two_ref,
-    one_ref,
-    columns_ref,
     third_ref,
     branch_third_ref,
     branch_second_ref,
     u_ref,
+    features_ref,
+    two_ref,
     feature_back_ref,
+    one_ref,
     back_two_ref,
     rows_ref,
     first_ref,
+    columns_ref,
 ):
     core = core_ref[0]
     width = third_ref.shape[0]
-    half = u_ref.shape[0] // 2
+    half, fields = u_ref.shape[0] // 2, columns_ref.shape[1]
+    across = 2 * width // mine_ref.shape[1]
+    here = width + LANES + across
     total = None
     for place, from_ref in ((core, mine_ref), (1 - core, other_ref)):
         rows = pl.ds(pl.multiple_of(place * half, half), half)
-        u_ref[rows, :] = from_ref[:, :, 0:width].astype(F32).reshape(half, width).astype(BF16)
-        part = jnp.sum(from_ref[:, :, width:].astype(F32), axis=0)
+        got = from_ref[...].astype(F32)
+        part = jnp.sum(got[:, :, width : width + 2 * LANES], axis=0)
         total = part if total is None else total + part
+        got = got.reshape(half, -1)
+        u_ref[rows, :] = got[:, 0:width].astype(BF16)
+        one_ref[rows, :] = got[:, width + 2 * LANES :].astype(BF16)
+        columns_ref[rows, :] = jnp.where(
+            core == 0,
+            got[:, here : here + fields],
+            got[:, here + fields : here + 2 * fields],
+        ).astype(BF16)
+    wide = jnp.tanh(dot(one_ref[...], branch_second_ref[...]))
+    two_ref[...] = wide.astype(BF16)
+    features_ref[...] = dot(two_ref[...], branch_third_ref[...]).astype(BF16)
     feature_back = (dot(u_ref[...], third_ref[...]) * scale).astype(BF16)
     feature_back_ref[...] = feature_back
-    two = two_ref[...]
-    back_two = (dot(feature_back, branch_third_ref[...], NT) * (1.0 - two * two)).astype(BF16)
+    back_two = (dot(feature_back, branch_third_ref[...], NT) * (1.0 - wide * wide)).astype(BF16)
     back_two_ref[...] = back_two
     one = one_ref[...].astype(F32)
     back_one = (dot(back_two, branch_second_ref[...], NT) * (1.0 - one * one)).astype(BF16)
     rows = dot(columns_ref[...], back_one, TN)
     parts = [rows[:, lane : lane + LANES] for lane in range(0, width, LANES)]
     rows_ref[...] = jnp.concatenate(parts + [total[:, 0:LANES]], axis=0).astype(BF16)
-    strips = width // LANES
+    deep = width // across
     for axis in range(2):
-        for strip in range(strips):
-            first_ref[axis : axis + 1, strip * LANES : (strip + 1) * LANES] = total[
-                axis * strips + strip : axis * strips + strip + 1, LANES:
+        for strip in range(deep):
+            first_ref[axis : axis + 1, strip * across : (strip + 1) * across] = total[
+                axis * deep + strip : axis * deep + strip + 1, LANES : LANES + across
             ]
 
 
@@ -427,54 +431,49 @@
             whole(2, width),
             whole(width, width),
         ],
-        out_specs=[flat, deep(4, width), deep(8, width), deep(5, width), whole(8, width, width)],
+        out_specs=[deep(4, width), flat, deep(7, width), deep(5, width), whole(8, width, width)],
         out_shape=[
+            pltpu.HBM((4, points, width), BF16),
             pltpu.HBM((points, width), F32),
-            pltpu.HBM((4, points, width), BF16),
-            pltpu.HBM((8, points, width), F32),
+            pltpu.HBM((7, points, width), BF16),
             pltpu.HBM((5, points, width), BF16),
             pltpu.HBM((8, width, width), BF16),
         ],
-        scratch_shapes=[pltpu.VMEM((tile, width), F32)],
+        scratch_shapes=[pltpu.VMEM((tile, width), F32), pltpu.VMEM((8, tile, width), F32)],
         compiler_params=PARAMS,
         name="trunk_forward",
     )(coords, first, second)
 
 
-def project_call(
-    pair, got, branch_second, branch_third, third, combos, forcing, pts_size, weight, scale
-):
+def project_call(ones, branch_second, branch_third, third, combos, forcing, weight, scale):
     funcs, points = forcing.shape
     width = third.shape[0]
-    tile, _ = tiles(points)
-    flat = lambda *shape: pl.BlockSpec(shape, lambda i, p: (0,) * len(shape))
+    tile = min(PROJECT, points)
     return pl.pallas_call(
         functools.partial(project_kernel, weight, scale),
-        grid_spec=pltpu.PrefetchScalarGridSpec(
-            num_scalar_prefetch=1,
-            grid=(points // tile,),
-            in_specs=[
-                pl.BlockSpec((pts_size, *got.shape[1:]), lambda i, p: (p[0], 0, 0)),
-                flat(width, width),
-                flat(width, width),
-                flat(width, width),
-                pl.BlockSpec((5, tile, width), lambda i, p: (0, i, 0)),
-                pl.BlockSpec((funcs, tile), lambda i, p: (0, i)),
-            ],
-            out_specs=[
-                flat(funcs, width),
-                pl.BlockSpec((5, funcs, tile), lambda i, p: (0, 0, i)),
-                flat(funcs, width),
-            ],
-        ),
+        grid=(points // tile,),
+        in_specs=[
+            whole(*ones.shape),
+            whole(width, width),
+            whole(width, width),
+            whole(width, width),
+            pl.BlockSpec((5, tile, width), lambda i: (0, i, 0)),
+            pl.BlockSpec((funcs, tile), lambda i: (0, i)),
+        ],
+        out_specs=[
+            pl.BlockSpec((5, funcs, tile), lambda i: (0, 0, i)),
+            whole(funcs, width),
+            whole(*ones.shape),
+        ],
         out_shape=[
-            jax.ShapeDtypeStruct((funcs, width), F32),
             pltpu.HBM((5, funcs, points), BF16),
             pltpu.HBM((funcs, width), BF16),
-        ],
+            jax.ShapeDtypeStruct(ones.shape, BF16),
+        ],
+        scratch_shapes=[pltpu.VMEM((funcs, width), F32)],
         compiler_params=PARAMS,
         name="project",
-    )(pair, there(got), branch_second, branch_third, third, there(combos), there(forcing))
+    )(ones, branch_second, branch_third, third, there(combos), there(forcing))
 
 
 def backward_call(
@@ -489,7 +488,7 @@
         in_specs=[
             pl.BlockSpec((tile, width), lambda i: (i, 0)),
             deep(4, width),
-            deep(8, width),
+            deep(7, width),
             pl.BlockSpec((5, funcs, tile), lambda i: (0, 0, i)),
             whole(funcs, width),
             pl.BlockSpec((2, tile), lambda i: (0, i)),
@@ -525,34 +524,18 @@
     )
 
 
-def hidden_call(core, mine, other, branch_second, branch_third, fields):
-    rows, width = 2 * mine.shape[0] * mine.shape[1], branch_second.shape[0]
-    return pl.pallas_call(
-        hidden_kernel,
-        in_specs=[SCALAR] + [LOCAL] * 4,
-        out_shape=[
-            jax.ShapeDtypeStruct((rows, width), BF16),
-            jax.ShapeDtypeStruct((rows, width), F32),
-            jax.ShapeDtypeStruct((rows, width), BF16),
-            jax.ShapeDtypeStruct((rows, width), BF16),
-            jax.ShapeDtypeStruct((rows, fields), BF16),
-        ],
-        compiler_params=SMALL,
-        name="branch_hidden",
-    )(core, mine, other, branch_second, branch_third)
-
-
-def branch_call(core, mine, other, two, one, columns, third, branch_third, branch_second, scale):
-    shape = one.shape
-    rows = columns.shape[1] * (shape[1] // LANES) + mine.shape[1]
+def branch_call(core, mine, other, third, branch_third, branch_second, fields, scale):
+    count, width = 2 * mine.shape[0] * mine.shape[1], third.shape[0]
+    rows = fields * (width // LANES) + mine.shape[1]
     return pl.pallas_call(
         functools.partial(branch_kernel, scale),
-        in_specs=[SCALAR] + [LOCAL] * 8,
-        out_shape=[jax.ShapeDtypeStruct(shape, BF16)] * 3
-        + [jax.ShapeDtypeStruct((rows, LANES), BF16), jax.ShapeDtypeStruct((2, shape[1]), F32)],
+        in_specs=[SCALAR] + [LOCAL] * 5,
+        out_shape=[jax.ShapeDtypeStruct((count, width), BF16)] * 6
+        + [jax.ShapeDtypeStruct((rows, LANES), BF16), jax.ShapeDtypeStruct((2, width), F32)],
+        scratch_shapes=[pltpu.VMEM((count, fields), BF16)],
         compiler_params=SMALL,
         name="branch_backward",
-    )(core, mine, other, two, one, columns, third, branch_third, branch_second)
+    )(core, mine, other, third, branch_third, branch_second)
 
 
 def gradient_call(u, features, two, feature_back, one, back_two, scale):
@@ -607,7 +590,6 @@
     func_size = 2 * pairs
     chips = pairs * pts_size
     core = lax.axis_index("core").reshape(1)
-    pair = lax.axis_index("pairs").reshape(1)
     funcs = forcing.shape[0]
     weight = 1.0 / math.sqrt(funcs * func_size * forcing.shape[1] * pts_size)
     width_out = trunk_third.shape[1]
@@ -617,32 +599,20 @@
     fields = sensors.shape[1] // chips
 
     own_one = jnp.tanh(dot(sensors, branch_first)).astype(BF16)
+    ones = swap(jnp.broadcast_to(own_one[None], (pts_size, own, width)), "pts")
     blocks = sensors.reshape(own, chips, fields).transpose(1, 0, 2)
-    sent = jnp.concatenate(
-        [
-            jnp.broadcast_to(own_one[None], (chips, own, width)),
-            jnp.pad(blocks, ((0, 0), (0, 0), (0, -fields % LANES))),
-        ],
-        axis=2,
-    )
-    got = swap(sent, ("pairs", "pts"))
-    squash, points_all, inner, combos, weights = forward_call(coords, trunk_first, trunk_second)
-    u_part, cots, feats = project_call(
-        pair,
-        got,
+    points_all, squash, inner, combos, weights = forward_call(coords, trunk_first, trunk_second)
+    cots, feats, shares = project_call(
+        ones,
         branch_second,
         branch_third,
         trunk_third,
         combos,
         forcing,
-        pts_size,
         weight,
         scale,
     )
-    got_other = across_chip(got)
-
-    u_blocks = swap(u_part.astype(BF16).reshape(pts_size, own, width), "pts")
-    u_own = u_blocks.astype(F32).sum(0).astype(BF16)
+    u_own = swap(shares, "pts").astype(F32).sum(0).astype(BF16)
     second_pieces = backward_call(
         squash,
         points_all,
@@ -653,31 +623,25 @@
         weights,
         trunk_first,
         trunk_second,
-        (chips, own, 2 * LANES),
+        (chips, own, LANES + 2 * width // own),
         scale,
     )
+    told = lambda part: jnp.broadcast_to(part[None], (chips, *part.shape))
     pieces = jnp.concatenate(
-        [jnp.broadcast_to(u_own[None], (chips, own, width)), second_pieces.astype(BF16)], axis=2
+        [
+            told(u_own),
+            second_pieces.astype(BF16),
+            blocks,
+            told(own_one),
+        ],
+        axis=2,
     )
     every = swap(pieces, ("pairs", "pts"))
     every_other = across_chip(every)
-
-    one, wide, two, features, columns = hidden_call(
-        core, got, got_other, branch_second, branch_third, fields // 2
-    )
-    u, feature_back, back_two, rows, grad_t1 = branch_call(
-        core,
-        every,
-        every_other,
-        wide,
-        one,
-        columns,
-        trunk_third,
-        branch_third,
-        branch_second,
-        scale,
-    )
-    mine = swap(jnp.broadcast_to(rows[None], (chips, *rows.shape)), ("pairs", "pts"))
+    u, features, two, feature_back, one, back_two, rows, grad_t1 = branch_call(
+        core, every, every_other, trunk_third, branch_third, branch_second, fields // 2, scale
+    )
+    mine = swap(told(rows), ("pairs", "pts"))
     other = across_chip(mine)
     grad_t3, grad_b3, grad_b2 = gradient_call(
         u, features, two, feature_back, one, back_two, scale

time: 128 us -> 117 us (0.914)
  Pallas kernels: 49.7 us -> 41 us
  starting transfers between devices: 23.3 us -> 19.2 us
  blocking collectives: 44.8 us -> 48.6 us
    pallas_call x1, Pallas kernels: 21.6 us -> 17 us  [backward_call(): pl.pallas_call(functools.partial(backward_kernel, scale), grid=(points //...]
    all_to_all x2, starting transfers between devices: 18.2 us -> 14.1 us  [swap(): return lax.all_to_all(parts, axes, split_axis=0, concat_axis=0, tiled=True)]
    all_to_all x2, blocking collectives: 44.8 us -> 48.6 us  [swap(): return lax.all_to_all(parts, axes, split_axis=0, concat_axis=0, tiled=True)]
    pallas_call x1, Pallas kernels: 13.1 us -> 10.1 us  [forward_call(): pl.pallas_call(forward_kernel, grid=(points // tile,), in_specs=[pl.Block...]
    pallas_call x2 -> x1, Pallas kernels: 8.62 us -> 7.08 us  [project_call(): pl.pallas_call(functools.partial(project_kernel, weight, scale), grid=(po...]
    ppermute x3 -> x2, waiting for transfers between devices: 3.32 us -> 3.13 us  [across_chip(): return lax.ppermute(value, 'core', [(0, 1), (1, 0)])]
    ppermute x3 -> x2, starting transfers between devices: 5.13 us -> 5.03 us  [across_chip(): return lax.ppermute(value, 'core', [(0, 1), (1, 0)])]
  transfers between devices with their start and end apart: 5 -> 4, of which waited for: 2 -> 2; matrix products, arithmetic and copies ran while one was open for 0% -> 0% of each run, Pallas kernels for 30% -> 24%
where the time goes in v3:
time: 117 us
  blocking collectives  48.6 us (42%)
  Pallas kernels  41 us (35%)
  starting transfers between devices  19.2 us (16%)
  waiting for transfers between devices  3.14 us (3%)
  local copies, waits for them, and re-layouts  2.65 us (2%)
  matrix products  1.25 us (1%)
    all_to_all x2, blocking collectives, swap(): return lax.all_to_all(parts, axes, split_axis=0, concat_axis=0, tiled=True)  48.6 us
    pallas_call x1, Pallas kernels, backward_call(): pl.pallas_call(functools.partial(backward_kernel, scale), grid=(points //...  17 us
    all_to_all x2, starting transfers between devices, swap(): return lax.all_to_all(parts, axes, split_axis=0, concat_axis=0, tiled=True)  14.1 us
    pallas_call x1, Pallas kernels, forward_call(): pl.pallas_call(forward_kernel, grid=(points // tile,), in_specs=[pl.Block...  10.1 us
    pallas_call x1, Pallas kernels, project_call(): pl.pallas_call(functools.partial(project_kernel, weight, scale), grid=(po...  7.08 us
    ppermute x2, starting transfers between devices, across_chip(): return lax.ppermute(value, 'core', [(0, 1), (1, 0)])  5.03 us
    ppermute x2, waiting for transfers between devices, across_chip(): return lax.ppermute(value, 'core', [(0, 1), (1, 0)])  3.13 us
    pallas_call x1, Pallas kernels, branch_call(): pl.pallas_call(functools.partial(branch_kernel, scale), in_specs=[SCALAR]...  2.82 us
  transfers between devices with their start and end apart: 4, of which 2 were waited for; matrix products, arithmetic and copies ran while one was open for 0% of the time, Pallas kernels for 24%

profile of v3, /device:TPU:1, one launch (start us, length us, event | category | flops | bytes accessed | tf_op | source)
XLA Modules:
  0.0 116.8 jit_solution(15729534963212662720)
XLA Ops:
  0.6 0.0 copy-start
  0.7 1.5 %copy-done = bf16[4096,256]{1,0:T(8,128)(2,1)S(1)} copy-done((bf16[4096,256]{1,0:T(8,128)(2,1)S(1)}, bf16[4096,256]{1,0:T(8,128)(2,1)}, u32[]{:S(2)}) %copy-start) | copy-done | bytes 2097176
  2.2 1.3 %fusion = bf16[8,256]{1,0:T(8,128)(2,1)S(1)} fusion(bf16[8,4096]{1,0:T(8,128)(2,1)} %param.9, bf16[4096,256]{1,0:T(8,128)(2,1)S(1)} %copy-done), kind=kOutput, calls=%fused_computation.1 | convolution fusion | flops 16779264 | bytes 2166784 | tf_op jit(solution)/shard_map/dot_general | solution.py:31
  3.5 0.6 broadcast_in_dim.8
  4.1 7.5 %all-to-all-start = ((bf16[8,8,256]{2,1,0:T(8,128)(2,1)}), bf16[8,8,256]{2,1,0:T(8,128)(2,1)S(1)}, u32[]{:S(2)}, u32[]{:S(2)}) async-start(bf16[8,8,256]{2,1,0:T(8,128)(2,1)} %broadcast_in_dim.8), calls=%async_computation | async-start | bytes 65536 | tf_op jit(solution)/shard_map/all_to_all | solution.py:571
  11.6 0.2 reshape.22
  11.8 0.1 copy.17
  11.9 10.1 %trunk_forward.1 = (bf16[4,2048,256]{2,1,0:T(8,128)(2,1)}, f32[2048,256]{1,0:T(8,128)}, bf16[7,2048,256]{2,1,0:T(8,128)(2,1)}, bf16[5,2048,256]{2,1,0:T(8,128)(2,1)}, bf16[8,256,256]{2,1,0:T(8,128)(2,1)}) custom-call(f32[2,2048]{1,0:T(2,128)S(1)} %copy-done.5, f32[2,256]{1,0:T(2,128)S(1)} %copy-done.6, bf16[256,256]{1,0:T(8,128)(2,1)S(1)} %copy-done.4), custom_call_target="tpu_custom_call" | custom-call | tf_op jit(solution)/shard_map/trunk_forward/pallas_call | solution.py:426
  22.0 0.0 all-to-all-done.ones_ref
  22.1 7.1 %project.1 = (bf16[5,64,2048]{2,1,0:T(8,128)(2,1)}, bf16[64,256]{1,0:T(8,128)(2,1)}, bf16[8,8,256]{2,1,0:T(8,128)(2,1)}) custom-call(bf16[8,8,256]{2,1,0:T(8,128)(2,1)S(1)} %all-to-all-done.ones_ref, bf16[256,256]{1,0:T(8,128)(2,1)S(1)} %copy-done.1, bf16[256,256]{1,0:T(8,128)(2,1)S(1)} %copy-done.2, bf16[256,256]{1,0:T(8,128)(2,1)S(1)} %copy-done.3, ...), custom_call_target="tpu_custom_call" | custom-call | tf_op jit(solution)/shard_map/project/pallas_call | solution.py:452
  29.2 6.6 %all-to-all-start.1 = ((bf16[8,8,256]{2,1,0:T(8,128)(2,1)}), bf16[8,8,256]{2,1,0:T(8,128)(2,1)S(1)}, u32[]{:S(2)}, u32[]{:S(2)}) async-start(bf16[8,8,256]{2,1,0:T(8,128)(2,1)} %get-tuple-element.28), calls=%async_computation.1 | async-start | bytes 65536 | tf_op jit(solution)/shard_map/all_to_all | solution.py:571
  35.8 17.0 %trunk_backward.1 = f32[64,8,192]{2,1,0:T(8,128)S(1)} custom-call(f32[2048,256]{1,0:T(8,128)} %get-tuple-element.29.squash_ref, bf16[4,2048,256]{2,1,0:T(8,128)(2,1)} %get-tuple-element.30.points_ref, bf16[7,2048,256]{2,1,0:T(8,128)(2,1)} %get-tuple-element.31.inner_ref, bf16[5,64,2048]{2,1,0:T(8,128)(2,1)} %get-tuple-element.32.cots_ref, ...), custom_call_target="tpu_custom_call" | custom-call | flops 5637144576 | bytes 25165824 | tf_op jit(solution)/shard_map/trunk_backward/pallas_call | solution.py:485
  52.9 0.0 all-to-all-done.1
  52.9 0.2 pad_maximum_fusion
  53.1 24.8 %all_to_all.20.mine_ref = bf16[64,8,768]{2,1,0:T(8,128)(2,1)S(1)} all-to-all(bf16[64,8,768]{2,1,0:T(8,128)(2,1)S(1)} %pad_maximum_fusion), channel_id=1, replica_groups=mesh['pairs'=8,'core'=2,'pts'=8] {'pairs','pts'}, dimensions={0} | all-to-all | bytes 1572864 | tf_op jit(solution)/shard_map/all_to_all | solution.py:571
  77.9 3.1 %collective-permute-start = (bf16[64,8,768]{2,1,0:T(8,128)(2,1)S(1)}, bf16[64,8,768]{2,1,0:T(8,128)(2,1)}, u32[]{:S(2)}, u32[]{:S(2)}) collective-permute-start(bf16[64,8,768]{2,1,0:T(8,128)(2,1)S(1)} %all_to_all.20.mine_ref), channel_id=1, source_target_pairs={{0,8},{8,0},{1,9},{9,1},{2,10},{10,2},{3,11},{11,3},{4,12},{12,4},... | collective-permute-start | bytes 2359304 | tf_op jit(solution)/shard_map/ppermute | solution.py:575
  81.0 2.0 %collective-permute-done.other_ref = bf16[64,8,768]{2,1,0:T(8,128)(2,1)} collective-permute-done((bf16[64,8,768]{2,1,0:T(8,128)(2,1)S(1)}, bf16[64,8,768]{2,1,0:T(8,128)(2,1)}, u32[]{:S(2)}, u32[]{:S(2)}) %collective-permute-start) | collective-permute-done | bytes 786464 | tf_op jit(solution)/shard_map/ppermute | solution.py:575
  83.1 2.8 %branch_backward.1 = (bf16[1024,256]{1,0:T(8,128)(2,1)S(1)}, bf16[1024,256]{1,0:T(8,128)(2,1)S(1)}, bf16[1024,256]{1,0:T(8,128)(2,1)S(1)}, bf16[1024,256]{1,0:T(...) custom-call(s32[1]{0:T(128)} %bitcast.core_ref, ...), custom_call_target="tpu_custom_call" | custom-call | tf_op jit(solution)/shard_map/branch_backward/pallas_call | solution.py:530
  85.9 0.2 broadcast_in_dim.11
  86.1 23.8 %all_to_all.21.mine_ref = bf16[64,72,128]{2,1,0:T(8,128)(2,1)S(1)} all-to-all(bf16[64,72,128]{2,1,0:T(8,128)(2,1)S(1)} %broadcast_in_dim.11), channel_id=1, replica_groups=mesh['pairs'=8,'core'=2,'pts'=8] {'pairs','pts'}, dimensions={0} | all-to-all | bytes 2359296 | tf_op jit(solution)/shard_map/all_to_all | solution.py:571
  109.9 1.9 %collective-permute-start.1 = (bf16[64,72,128]{2,1,0:T(8,128)(2,1)S(1)}, bf16[64,72,128]{2,1,0:T(8,128)(2,1)S(1)}, u32[]{:S(2)}, u32[]{:S(2)}) collective-permute-start(bf16[64,72,128]{2,1,0:T(8,128)(2,1)S(1)} %all_to_all.21.mine_ref), channel_id=1, source_target_pairs={{0,8},{8,0},{1,9},{9,1},{2,10},{10,2},{3,11},{11,3},{4,12},{12,4},... | collective-permute-start | bytes 3538952 | tf_op jit(solution)/shard_map/ppermute | solution.py:575
  111.8 1.4 %branch_gradients.1 = (f32[256,256]{1,0:T(8,128)}, f32[256,256]{1,0:T(8,128)}, f32[256,256]{1,0:T(8,128)}) custom-call(bf16[1024,256]{1,0:T(8,128)(2,1)S(1)} %get-tuple-element.37.u_ref, bf16[1024,256]{1,0:T(8,128)(2,1)S(1)} %get-tuple-element.38.features_ref, bf16[1024,256]{1,0:T(8,128)(2,1)S(1)} %get-tuple-element.39.two_ref, ...), custom_call_target="tpu_custom_call" | custom-call | tf_op jit(solution)/shard_map/branch_gradients/pallas_call | solution.py:543
  113.2 1.1 collective-permute-done.1.other_ref
  114.3 2.6 %spread.1 = (f32[4096,256]{1,0:T(8,128)}, f32[256,256]{1,0:T(8,128)}) custom-call(s32[1]{0:T(128)} %bitcast.core_ref, bf16[64,72,128]{2,1,0:T(8,128)(2,1)S(1)} %all_to_all.21.mine_ref, bf16[64,72,128]{2,1,0:T(8,128)(2,1)S(1)} %collective-permute-done.1.other_ref), custom_call_target="tpu_custom_call" | custom-call | tf_op jit(solution)/shard_map/spread/pallas_call | solution.py:556
  (18 shorter events, 0.1 us)
Async XLA Ops:
  0.6 1.6 %copy-start = (bf16[4096,256]{1,0:T(8,128)(2,1)S(1)}, bf16[4096,256]{1,0:T(8,128)(2,1)}, u32[]{:S(2)}) copy-start(bf16[4096,256]{1,0:T(8,128)(2,1)} %param.12) | copy-start | bytes 6291460
  0.6 11.0 %copy-start.7 = (bf16[8,4096]{1,0:T(8,128)(2,1)S(1)}, bf16[8,4096]{1,0:T(8,128)(2,1)}, u32[]{:S(2)}) copy-start(bf16[8,4096]{1,0:T(8,128)(2,1)} %param.9) | copy-start | bytes 196612
  0.7 11.2 %copy-start.5 = (f32[2,2048]{1,0:T(2,128)S(1)}, f32[2,2048]{1,0:T(2,128)}, u32[]{:S(2)}) copy-start(f32[2,2048]{1,0:T(2,128)} %coords_ref.3) | copy-start | bytes 49156
  0.7 11.2 %copy-start.6 = (f32[2,256]{1,0:T(2,128)S(1)}, f32[2,256]{1,0:T(2,128)}, u32[]{:S(2)}) copy-start(f32[2,256]{1,0:T(2,128)} %first_ref.3) | copy-start | bytes 6148
  0.7 11.2 %copy-start.4 = (bf16[256,256]{1,0:T(8,128)(2,1)S(1)}, bf16[256,256]{1,0:T(8,128)(2,1)}, u32[]{:S(2)}) copy-start(bf16[256,256]{1,0:T(8,128)(2,1)} %second_ref.3) | copy-start | bytes 393220
  0.7 21.4 %copy-start.1 = (bf16[256,256]{1,0:T(8,128)(2,1)S(1)}, bf16[256,256]{1,0:T(8,128)(2,1)}, u32[]{:S(2)}) copy-start(bf16[256,256]{1,0:T(8,128)(2,1)} %branch_second_ref.3) | copy-start | bytes 393220
  0.7 21.4 %copy-start.2 = (bf16[256,256]{1,0:T(8,128)(2,1)S(1)}, bf16[256,256]{1,0:T(8,128)(2,1)}, u32[]{:S(2)}) copy-start(bf16[256,256]{1,0:T(8,128)(2,1)} %branch_third_ref.3) | copy-start | bytes 393220
  2.2 19.8 %copy-start.3 = (bf16[256,256]{1,0:T(8,128)(2,1)S(1)}, bf16[256,256]{1,0:T(8,128)(2,1)}, u32[]{:S(2)}) copy-start(bf16[256,256]{1,0:T(8,128)(2,1)} %third_ref.3) | copy-start | bytes 393220
  4.1 17.9 %all-to-all-start = ((bf16[8,8,256]{2,1,0:T(8,128)(2,1)}), bf16[8,8,256]{2,1,0:T(8,128)(2,1)S(1)}, u32[]{:S(2)}, u32[]{:S(2)}) async-start(bf16[8,8,256]{2,1,0:T(8,128)(2,1)} %broadcast_in_dim.8), calls=%async_computation | async-start | bytes 65536 | tf_op jit(solution)/shard_map/all_to_all | solution.py:571
  29.2 23.7 %all-to-all-start.1 = ((bf16[8,8,256]{2,1,0:T(8,128)(2,1)}), bf16[8,8,256]{2,1,0:T(8,128)(2,1)S(1)}, u32[]{:S(2)}, u32[]{:S(2)}) async-start(bf16[8,8,256]{2,1,0:T(8,128)(2,1)} %get-tuple-element.28), calls=%async_computation.1 | async-start | bytes 65536 | tf_op jit(solution)/shard_map/all_to_all | solution.py:571
  77.9 5.2 %collective-permute-start = (bf16[64,8,768]{2,1,0:T(8,128)(2,1)S(1)}, bf16[64,8,768]{2,1,0:T(8,128)(2,1)}, u32[]{:S(2)}, u32[]{:S(2)}) collective-permute-start(bf16[64,8,768]{2,1,0:T(8,128)(2,1)S(1)} %all_to_all.20.mine_ref), channel_id=1, source_target_pairs={{0,8},{8,0},{1,9},{9,1},{2,10},{10,2},{3,11},{11,3},{4,12},{12,4},... | collective-permute-start | bytes 2359304 | tf_op jit(solution)/shard_map/ppermute | solution.py:575
  109.9 4.4 %collective-permute-start.1 = (bf16[64,72,128]{2,1,0:T(8,128)(2,1)S(1)}, bf16[64,72,128]{2,1,0:T(8,128)(2,1)S(1)}, u32[]{:S(2)}, u32[]{:S(2)}) collective-permute-start(bf16[64,72,128]{2,1,0:T(8,128)(2,1)S(1)} %all_to_all.21.mine_ref), channel_id=1, source_target_pairs={{0,8},{8,0},{1,9},{9,1},{2,10},{10,2},{3,11},{11,3},{4,12},{12,4},... | collective-permute-start | bytes 3538952 | tf_op jit(solution)/shard_map/ppermute | solution.py:575

commit v4 on v3

--- a/solution.py
+++ b/solution.py
@@ -35,7 +35,7 @@
     square = squash * squash
     one = 1.0 - square
     two = -2.0 * (squash * one)
-    three = one * (4.0 * square - 2.0 * one)
+    three = one * (6.0 * square - 2.0)
     return square, one, two, three
 
 
@@ -152,13 +152,13 @@
         one = ones_ref[...].astype(F32).reshape(u_ref.shape).astype(BF16)
         two = jnp.tanh(dot(one, branch_second_ref[...])).astype(BF16)
         features = dot(two, branch_third_ref[...]).astype(BF16)
-        feats_ref[...] = dot(features, third_ref[...], NT).astype(BF16)
+        feats_ref[...] = (dot(features, third_ref[...], NT) * scale).astype(BF16)
 
     feats = feats_ref[...]
     tile = forcing_ref.shape[1]
     for start in range(0, tile, min(CHUNK, tile)):
         span = pl.ds(start, min(CHUNK, tile))
-        px, py, om, omx, omy = (dot(feats, combos_ref[k, span], NT) * scale for k in range(5))
+        px, py, om, omx, omy = (dot(feats, combos_ref[k, span], NT) for k in range(5))
         residual = py * omx - px * omy + DRAG * om - forcing_ref[:, span].astype(F32)
         slope = residual * weight
         parts = (-slope * omy, slope * omx, DRAG * slope, slope * py, -slope * px)
@@ -175,7 +175,6 @@
 
 
 def backward_kernel(
-    scale,
     squash_ref,
     points_ref,
     inner_ref,
@@ -211,7 +210,7 @@
         )
         gx, gy, gl, gp, gq = (back_ref[k, rows, lanes] for k in range(5))
         square, one, two, three = slopes(squash)
-        four = two * (4.0 * square - 8.0 * one)
+        four = two * (12.0 * square - 8.0)
         radius = zx * zx + zy * zy
         twice = lap + lap
         plus, minus = twice + dif, twice - dif
@@ -240,7 +239,7 @@
 
     def layer_one_back(rows, lanes):
         squash, one, two, three = (points_ref[part, rows, lanes].astype(F32) for part in range(4))
-        four = two * (4.0 * (squash * squash) - 8.0 * one)
+        four = two * (4.0 - 12.0 * one)
         back = (
             one * ones_ref[0, rows, lanes]
             + two * ones_ref[1, rows, lanes]
@@ -254,7 +253,7 @@
     spans = [(start, start + part_rows) for start in range(0, tile, part_rows)]
     for start, stop in spans:
         for k in range(5):
-            back_ref[k, start:stop] = dot(cots_ref[k, :, start:stop], feats, TN) * scale
+            back_ref[k, start:stop] = dot(cots_ref[k, :, start:stop], feats, TN)
     for start, stop in spans:
         chunks((start, stop), width, layer_two_back)
         for group in range(4):
@@ -379,19 +378,19 @@
     second_ref[...] = dot(one_ref[...], back_two_ref[...], TN)
 
 
-def spread_kernel(core_ref, mine_ref, other_ref, grad_ref, second_ref):
-    first = core_ref[0] == 0
+def spread_rows(from_ref, grad_ref):
+    got = from_ref[...].astype(F32)
+    fields = grad_ref.shape[2]
+    for lane in range(grad_ref.shape[3] // LANES):
+        grad_ref[:, 0, :, lane * LANES : (lane + 1) * LANES] = got[
+            :, lane * fields : (lane + 1) * fields
+        ]
+    return got
+
+
+def mine_kernel(core_ref, mine_ref, grad_ref, second_ref):
     step = pl.program_id(0)
-    count = mine_ref.shape[0]
-    fields = grad_ref.shape[0] // (2 * count)
-    mine, other = mine_ref[...].astype(F32), other_ref[...].astype(F32)
-    for lane in range(grad_ref.shape[1] // LANES):
-        parts = [got[:, lane * fields : (lane + 1) * fields] for got in (mine, other)]
-        block = jnp.stack(
-            [jnp.where(first, parts[0], parts[1]), jnp.where(first, parts[1], parts[0])], axis=1
-        )
-        grad_ref[:, lane * LANES : (lane + 1) * LANES] = block.reshape(-1, LANES)
-    tail = mine[:, -8:].reshape(-1, LANES)
+    tail = spread_rows(mine_ref, grad_ref)[:, -8:].reshape(-1, LANES)
     width = second_ref.shape[0]
     for now in range(width * width // tail.size):
 
@@ -399,6 +398,10 @@
         def _():
             strip, row = divmod(now * tail.shape[0], width)
             second_ref[row : row + tail.shape[0], strip * LANES : (strip + 1) * LANES] = tail
+
+
+def other_kernel(core_ref, other_ref, kept_ref, grad_ref):
+    spread_rows(other_ref, grad_ref)
 
 
 def whole(*shape):
@@ -477,13 +480,13 @@
 
 
 def backward_call(
-    squash, points_all, inner, cots, feats, coords, weights, first, second, pieces, scale
+    squash, points_all, inner, cots, feats, coords, weights, first, second, pieces
 ):
     points, width = squash.shape
     funcs = feats.shape[0]
     tile, deep = tiles(points)
     return pl.pallas_call(
-        functools.partial(backward_kernel, scale),
+        backward_kernel,
         grid=(points // tile,),
         in_specs=[
             pl.BlockSpec((tile, width), lambda i: (i, 0)),
@@ -549,22 +552,49 @@
     )(u, features, two, feature_back, one, back_two)
 
 
-def spread_call(core, mine, other, shape, width):
+def spread_specs(got, shape, side):
     steps = 4
-    block = (mine.shape[0] // steps, *mine.shape[1:])
-    piece = pl.BlockSpec(block, lambda j: (j, 0, 0))
+    part = got.shape[0] // steps
+    fields = shape[0] // (2 * got.shape[0])
+    return (
+        steps,
+        pl.BlockSpec((part, *got.shape[1:]), lambda j, c: (j, 0, 0)),
+        pl.BlockSpec((part, 1, fields, shape[1]), lambda j, c: (j, side(c[0]), 0, 0)),
+        jax.ShapeDtypeStruct((got.shape[0], 2, fields, shape[1]), F32),
+    )
+
+
+def mine_call(core, mine, shape, width):
+    steps, piece, place, out = spread_specs(mine, shape, lambda c: c)
     return pl.pallas_call(
-        spread_kernel,
-        grid=(steps,),
-        in_specs=[SCALAR, piece, piece],
-        out_specs=[
-            pl.BlockSpec((shape[0] // steps, shape[1]), lambda j: (j, 0)),
-            whole(width, width),
-        ],
-        out_shape=[jax.ShapeDtypeStruct(shape, F32), jax.ShapeDtypeStruct((width, width), F32)],
+        mine_kernel,
+        grid_spec=pltpu.PrefetchScalarGridSpec(
+            num_scalar_prefetch=1,
+            grid=(steps,),
+            in_specs=[piece],
+            out_specs=[place, pl.BlockSpec((width, width), lambda j, c: (0, 0))],
+        ),
+        out_shape=[out, jax.ShapeDtypeStruct((width, width), F32)],
         compiler_params=PARAMS,
-        name="spread",
-    )(core, mine, other)
+        name="spread_mine",
+    )(core, mine)
+
+
+def other_call(core, other, kept, shape):
+    steps, piece, place, out = spread_specs(other, shape, lambda c: 1 - c)
+    return pl.pallas_call(
+        other_kernel,
+        grid_spec=pltpu.PrefetchScalarGridSpec(
+            num_scalar_prefetch=1,
+            grid=(steps,),
+            in_specs=[piece, pl.BlockSpec(memory_space=pl.ANY)],
+            out_specs=place,
+        ),
+        out_shape=out,
+        input_output_aliases={2: 0},
+        compiler_params=PARAMS,
+        name="spread_other",
+    )(core, other, kept)
 
 
 def swap(parts, axes):
@@ -624,7 +654,6 @@
         trunk_first,
         trunk_second,
         (chips, own, LANES + 2 * width // own),
-        scale,
     )
     told = lambda part: jnp.broadcast_to(part[None], (chips, *part.shape))
     pieces = jnp.concatenate(
@@ -646,7 +675,8 @@
     grad_t3, grad_b3, grad_b2 = gradient_call(
         u, features, two, feature_back, one, back_two, scale
     )
-    grad_b1, grad_t2 = spread_call(core, mine, other, branch_first.shape, width)
+    kept, grad_t2 = mine_call(core, mine, branch_first.shape, width)
+    grad_b1 = other_call(core, other, kept, branch_first.shape).reshape(branch_first.shape)
     return (grad_b1, grad_b2, grad_b3, grad_t1, grad_t2, grad_t3)
 
 

time: 117 us -> 117 us (level)
    pallas_call x2 -> x3, Pallas kernels: 19.6 us -> 20.5 us  [the longest x1 16.7 us: backward_call(): pl.pallas_call(backward_kernel, grid=(points // tile,), in_specs=[pl.Bloc...]
  transfers between devices with their start and end apart: 4 -> 4, of which waited for: 2 -> 1; matrix products, arithmetic and copies ran while one was open for 0% -> 0% of each run, Pallas kernels for 24% -> 26%
where the time goes in v4:
time: 117 us
  blocking collectives  48.6 us (42%)
  Pallas kernels  41.8 us (36%)
  starting transfers between devices  19.2 us (16%)
  local copies, waits for them, and re-layouts  2.65 us (2%)
  waiting for transfers between devices  2.05 us (2%)
  matrix products  1.25 us (1%)
    all_to_all x2, blocking collectives, swap(): return lax.all_to_all(parts, axes, split_axis=0, concat_axis=0, tiled=True)  48.6 us
    pallas_call x1, Pallas kernels, backward_call(): pl.pallas_call(backward_kernel, grid=(points // tile,), in_specs=[pl.Bloc...  16.7 us
    all_to_all x2, starting transfers between devices, swap(): return lax.all_to_all(parts, axes, split_axis=0, concat_axis=0, tiled=True)  14.1 us
    pallas_call x1, Pallas kernels, forward_call(): pl.pallas_call(forward_kernel, grid=(points // tile,), in_specs=[pl.Block...  9.97 us
    pallas_call x1, Pallas kernels, project_call(): pl.pallas_call(functools.partial(project_kernel, weight, scale), grid=(po...  7.07 us
    ppermute x2, starting transfers between devices, across_chip(): return lax.ppermute(value, 'core', [(0, 1), (1, 0)])  5.04 us
    pallas_call x1, Pallas kernels, branch_call(): pl.pallas_call(functools.partial(branch_kernel, scale), in_specs=[SCALAR]...  2.84 us
  transfers between devices with their start and end apart: 4, of which 1 were waited for; matrix products, arithmetic and copies ran while one was open for 0% of the time, Pallas kernels for 26%

profile of v4, /device:TPU:1, one launch (start us, length us, event | category | flops | bytes accessed | tf_op | source)
XLA Modules:
  0.0 116.5 jit_solution(4661604013280623226)
XLA Ops:
  0.6 0.0 copy-start
  0.7 1.5 %copy-done = bf16[4096,256]{1,0:T(8,128)(2,1)S(1)} copy-done((bf16[4096,256]{1,0:T(8,128)(2,1)S(1)}, bf16[4096,256]{1,0:T(8,128)(2,1)}, u32[]{:S(2)}) %copy-start) | copy-done | bytes 2097176
  2.2 1.3 %fusion = bf16[8,256]{1,0:T(8,128)(2,1)S(1)} fusion(bf16[8,4096]{1,0:T(8,128)(2,1)} %param.9, bf16[4096,256]{1,0:T(8,128)(2,1)S(1)} %copy-done), kind=kOutput, calls=%fused_computation.1 | convolution fusion | flops 16779264 | bytes 2166784 | tf_op jit(solution)/shard_map/dot_general | solution.py:31
  3.5 0.6 broadcast_in_dim.8
  4.1 7.5 %all-to-all-start = ((bf16[8,8,256]{2,1,0:T(8,128)(2,1)}), bf16[8,8,256]{2,1,0:T(8,128)(2,1)S(1)}, u32[]{:S(2)}, u32[]{:S(2)}) async-start(bf16[8,8,256]{2,1,0:T(8,128)(2,1)} %broadcast_in_dim.8), calls=%async_computation | async-start | bytes 65536 | tf_op jit(solution)/shard_map/all_to_all | solution.py:601
  11.6 0.2 reshape.25
  11.8 0.1 copy.18
  11.9 10.0 %trunk_forward.1 = (bf16[4,2048,256]{2,1,0:T(8,128)(2,1)}, f32[2048,256]{1,0:T(8,128)}, bf16[7,2048,256]{2,1,0:T(8,128)(2,1)}, bf16[5,2048,256]{2,1,0:T(8,128)(2,1)}, bf16[8,256,256]{2,1,0:T(8,128)(2,1)}) custom-call(f32[2,2048]{1,0:T(2,128)S(1)} %copy-done.5, f32[2,256]{1,0:T(2,128)S(1)} %copy-done.6, bf16[256,256]{1,0:T(8,128)(2,1)S(1)} %copy-done.4), custom_call_target="tpu_custom_call" | custom-call | tf_op jit(solution)/shard_map/trunk_forward/pallas_call | solution.py:429
  21.9 0.0 all-to-all-done.ones_ref
  21.9 7.1 %project.1 = (bf16[5,64,2048]{2,1,0:T(8,128)(2,1)}, bf16[64,256]{1,0:T(8,128)(2,1)}, bf16[8,8,256]{2,1,0:T(8,128)(2,1)}) custom-call(bf16[8,8,256]{2,1,0:T(8,128)(2,1)S(1)} %all-to-all-done.ones_ref, bf16[256,256]{1,0:T(8,128)(2,1)S(1)} %copy-done.1, bf16[256,256]{1,0:T(8,128)(2,1)S(1)} %copy-done.2, bf16[256,256]{1,0:T(8,128)(2,1)S(1)} %copy-done.3, ...), custom_call_target="tpu_custom_call" | custom-call | tf_op jit(solution)/shard_map/project/pallas_call | solution.py:455
  29.0 6.6 %all-to-all-start.1 = ((bf16[8,8,256]{2,1,0:T(8,128)(2,1)}), bf16[8,8,256]{2,1,0:T(8,128)(2,1)S(1)}, u32[]{:S(2)}, u32[]{:S(2)}) async-start(bf16[8,8,256]{2,1,0:T(8,128)(2,1)} %get-tuple-element.28), calls=%async_computation.1 | async-start | bytes 65536 | tf_op jit(solution)/shard_map/all_to_all | solution.py:601
  35.6 16.7 %trunk_backward.1 = f32[64,8,192]{2,1,0:T(8,128)S(1)} custom-call(f32[2048,256]{1,0:T(8,128)} %get-tuple-element.29.squash_ref, bf16[4,2048,256]{2,1,0:T(8,128)(2,1)} %get-tuple-element.30.points_ref, bf16[7,2048,256]{2,1,0:T(8,128)(2,1)} %get-tuple-element.31.inner_ref, bf16[5,64,2048]{2,1,0:T(8,128)(2,1)} %get-tuple-element.32.cots_ref, ...), custom_call_target="tpu_custom_call" | custom-call | flops 5637144576 | bytes 25165824 | tf_op jit(solution)/shard_map/trunk_backward/pallas_call | solution.py:488
  52.5 0.2 pad_maximum_fusion
  52.7 24.8 %all_to_all.20.mine_ref = bf16[64,8,768]{2,1,0:T(8,128)(2,1)S(1)} all-to-all(bf16[64,8,768]{2,1,0:T(8,128)(2,1)S(1)} %pad_maximum_fusion), channel_id=1, replica_groups=mesh['pairs'=8,'core'=2,'pts'=8] {'pairs','pts'}, dimensions={0} | all-to-all | bytes 1572864 | tf_op jit(solution)/shard_map/all_to_all | solution.py:601
  77.5 3.1 %collective-permute-start = (bf16[64,8,768]{2,1,0:T(8,128)(2,1)S(1)}, bf16[64,8,768]{2,1,0:T(8,128)(2,1)}, u32[]{:S(2)}, u32[]{:S(2)}) collective-permute-start(bf16[64,8,768]{2,1,0:T(8,128)(2,1)S(1)} %all_to_all.20.mine_ref), channel_id=1, source_target_pairs={{0,8},{8,0},{1,9},{9,1},{2,10},{10,2},{3,11},{11,3},{4,12},{12,4},... | collective-permute-start | bytes 2359304 | tf_op jit(solution)/shard_map/ppermute | solution.py:605
  80.6 2.0 %collective-permute-done.other_ref = bf16[64,8,768]{2,1,0:T(8,128)(2,1)} collective-permute-done((bf16[64,8,768]{2,1,0:T(8,128)(2,1)S(1)}, bf16[64,8,768]{2,1,0:T(8,128)(2,1)}, u32[]{:S(2)}, u32[]{:S(2)}) %collective-permute-start) | collective-permute-done | bytes 786464 | tf_op jit(solution)/shard_map/ppermute | solution.py:605
  82.7 2.8 %branch_backward.1 = (bf16[1024,256]{1,0:T(8,128)(2,1)S(1)}, bf16[1024,256]{1,0:T(8,128)(2,1)S(1)}, bf16[1024,256]{1,0:T(8,128)(2,1)S(1)}, bf16[1024,256]{1,0:T(...) custom-call(s32[1]{0:T(128)} %bitcast.core_ref, ...), custom_call_target="tpu_custom_call" | custom-call | tf_op jit(solution)/shard_map/branch_backward/pallas_call | solution.py:533
  85.5 0.2 broadcast_in_dim.11
  85.7 23.8 %all_to_all.21.mine_ref = bf16[64,72,128]{2,1,0:T(8,128)(2,1)S(1)} all-to-all(bf16[64,72,128]{2,1,0:T(8,128)(2,1)S(1)} %broadcast_in_dim.11), channel_id=1, replica_groups=mesh['pairs'=8,'core'=2,'pts'=8] {'pairs','pts'}, dimensions={0} | all-to-all | bytes 2359296 | tf_op jit(solution)/shard_map/all_to_all | solution.py:601
  109.5 1.9 %collective-permute-start.1 = (bf16[64,72,128]{2,1,0:T(8,128)(2,1)S(1)}, bf16[64,72,128]{2,1,0:T(8,128)(2,1)S(1)}, u32[]{:S(2)}, u32[]{:S(2)}) collective-permute-start(bf16[64,72,128]{2,1,0:T(8,128)(2,1)S(1)} %all_to_all.21.mine_ref), channel_id=1, source_target_pairs={{0,8},{8,0},{1,9},{9,1},{2,10},{10,2},{3,11},{11,3},{4,12},{12,4},... | collective-permute-start | bytes 3538952 | tf_op jit(solution)/shard_map/ppermute | solution.py:605
  111.4 1.4 %branch_gradients.1 = (f32[256,256]{1,0:T(8,128)}, f32[256,256]{1,0:T(8,128)}, f32[256,256]{1,0:T(8,128)}) custom-call(bf16[1024,256]{1,0:T(8,128)(2,1)S(1)} %get-tuple-element.37.u_ref, bf16[1024,256]{1,0:T(8,128)(2,1)S(1)} %get-tuple-element.38.features_ref, bf16[1024,256]{1,0:T(8,128)(2,1)S(1)} %get-tuple-element.39.two_ref, ...), custom_call_target="tpu_custom_call" | custom-call | tf_op jit(solution)/shard_map/branch_gradients/pallas_call | solution.py:546
  112.8 1.9 %spread_mine.1 = (f32[64,2,32,256]{3,2,1,0:T(8,128)}, f32[256,256]{1,0:T(8,128)}) custom-call(s32[1]{0:T(128)} %bitcast.core_ref, bf16[64,72,128]{2,1,0:T(8,128)(2,1)S(1)} %all_to_all.21.mine_ref), custom_call_target="tpu_custom_call" | custom-call | tf_op jit(solution)/shard_map/spread_mine/pallas_call | solution.py:569
  114.7 0.0 collective-permute-done.1.other_ref
  114.7 1.8 %spread_other.1 = f32[64,2,32,256]{3,2,1,0:T(8,128)} custom-call(s32[1]{0:T(128)} %bitcast.core_ref, bf16[64,72,128]{2,1,0:T(8,128)(2,1)S(1)} %collective-permute-done.1.other_ref, f32[64,2,32,256]{3,2,1,0:T(8,128)} %get-tuple-element.36.kept_ref), custom_call_target="tpu_custom_call", output_to_operand_aliasing={{}: (2, {})} | custom-call | tf_op jit(solution)/shard_map/spread_other/pallas_call | solution.py:585
  (19 shorter events, 0.1 us)
Async XLA Ops:
  0.6 1.6 %copy-start = (bf16[4096,256]{1,0:T(8,128)(2,1)S(1)}, bf16[4096,256]{1,0:T(8,128)(2,1)}, u32[]{:S(2)}) copy-start(bf16[4096,256]{1,0:T(8,128)(2,1)} %param.12) | copy-start | bytes 6291460
  0.6 11.0 %copy-start.7 = (bf16[8,4096]{1,0:T(8,128)(2,1)S(1)}, bf16[8,4096]{1,0:T(8,128)(2,1)}, u32[]{:S(2)}) copy-start(bf16[8,4096]{1,0:T(8,128)(2,1)} %param.9) | copy-start | bytes 196612
  0.7 11.2 %copy-start.5 = (f32[2,2048]{1,0:T(2,128)S(1)}, f32[2,2048]{1,0:T(2,128)}, u32[]{:S(2)}) copy-start(f32[2,2048]{1,0:T(2,128)} %coords_ref.3) | copy-start | bytes 49156
  0.7 11.2 %copy-start.6 = (f32[2,256]{1,0:T(2,128)S(1)}, f32[2,256]{1,0:T(2,128)}, u32[]{:S(2)}) copy-start(f32[2,256]{1,0:T(2,128)} %first_ref.3) | copy-start | bytes 6148
  0.7 11.2 %copy-start.4 = (bf16[256,256]{1,0:T(8,128)(2,1)S(1)}, bf16[256,256]{1,0:T(8,128)(2,1)}, u32[]{:S(2)}) copy-start(bf16[256,256]{1,0:T(8,128)(2,1)} %second_ref.3) | copy-start | bytes 393220
  0.7 21.2 %copy-start.1 = (bf16[256,256]{1,0:T(8,128)(2,1)S(1)}, bf16[256,256]{1,0:T(8,128)(2,1)}, u32[]{:S(2)}) copy-start(bf16[256,256]{1,0:T(8,128)(2,1)} %branch_second_ref.3) | copy-start | bytes 393220
  0.7 21.2 %copy-start.2 = (bf16[256,256]{1,0:T(8,128)(2,1)S(1)}, bf16[256,256]{1,0:T(8,128)(2,1)}, u32[]{:S(2)}) copy-start(bf16[256,256]{1,0:T(8,128)(2,1)} %branch_third_ref.3) | copy-start | bytes 393220
  2.2 19.7 %copy-start.3 = (bf16[256,256]{1,0:T(8,128)(2,1)S(1)}, bf16[256,256]{1,0:T(8,128)(2,1)}, u32[]{:S(2)}) copy-start(bf16[256,256]{1,0:T(8,128)(2,1)} %third_ref.3) | copy-start | bytes 393220
  4.1 17.8 %all-to-all-start = ((bf16[8,8,256]{2,1,0:T(8,128)(2,1)}), bf16[8,8,256]{2,1,0:T(8,128)(2,1)S(1)}, u32[]{:S(2)}, u32[]{:S(2)}) async-start(bf16[8,8,256]{2,1,0:T(8,128)(2,1)} %broadcast_in_dim.8), calls=%async_computation | async-start | bytes 65536 | tf_op jit(solution)/shard_map/all_to_all | solution.py:601
  29.0 23.4 %all-to-all-start.1 = ((bf16[8,8,256]{2,1,0:T(8,128)(2,1)}), bf16[8,8,256]{2,1,0:T(8,128)(2,1)S(1)}, u32[]{:S(2)}, u32[]{:S(2)}) async-start(bf16[8,8,256]{2,1,0:T(8,128)(2,1)} %get-tuple-element.28), calls=%async_computation.1 | async-start | bytes 65536 | tf_op jit(solution)/shard_map/all_to_all | solution.py:601
  77.5 5.2 %collective-permute-start = (bf16[64,8,768]{2,1,0:T(8,128)(2,1)S(1)}, bf16[64,8,768]{2,1,0:T(8,128)(2,1)}, u32[]{:S(2)}, u32[]{:S(2)}) collective-permute-start(bf16[64,8,768]{2,1,0:T(8,128)(2,1)S(1)} %all_to_all.20.mine_ref), channel_id=1, source_target_pairs={{0,8},{8,0},{1,9},{9,1},{2,10},{10,2},{3,11},{11,3},{4,12},{12,4},... | collective-permute-start | bytes 2359304 | tf_op jit(solution)/shard_map/ppermute | solution.py:605
  109.5 5.2 %collective-permute-start.1 = (bf16[64,72,128]{2,1,0:T(8,128)(2,1)S(1)}, bf16[64,72,128]{2,1,0:T(8,128)(2,1)S(1)}, u32[]{:S(2)}, u32[]{:S(2)}) collective-permute-start(bf16[64,72,128]{2,1,0:T(8,128)(2,1)S(1)} %all_to_all.21.mine_ref), channel_id=1, source_target_pairs={{0,8},{8,0},{1,9},{9,1},{2,10},{10,2},{3,11},{11,3},{4,12},{12,4},... | collective-permute-start | bytes 3538952 | tf_op jit(solution)/shard_map/ppermute | solution.py:605

commit v5 on v4

--- a/solution.py
+++ b/solution.py
@@ -14,6 +14,7 @@
 ROWS = 16
 PARTS = 2
 CHUNK = 256
+STEPS = 2
 LANES = 128
 F32 = jnp.float32
 BF16 = jnp.bfloat16
@@ -41,8 +42,7 @@
 
 def chunks(rows, width, body):
     for start in range(*rows, ROWS):
-        for lane in range(0, width, LANES):
-            body(pl.ds(start, ROWS), pl.ds(lane, LANES))
+        body(pl.ds(start, ROWS), pl.ds(0, width))
 
 
 def constants(first):
@@ -62,6 +62,22 @@
         parts.append(part)
         value = value - part
     return parts
+
+
+def first_kernel(sensors_ref, first_ref, own_ref, told_ref, total_ref):
+    step = pl.program_id(0)
+
+    @pl.when(step == 0)
+    def _():
+        total_ref[...] = jnp.zeros_like(total_ref)
+
+    total_ref[...] += dot(sensors_ref[...], first_ref[...])
+
+    @pl.when(step == pl.num_programs(0) - 1)
+    def _():
+        one = jnp.tanh(total_ref[...])
+        own_ref[...] = one.astype(BF16)
+        told_ref[...] = jnp.broadcast_to(one[None], told_ref.shape).astype(BF16)
 
 
 def forward_kernel(
@@ -422,6 +438,28 @@
     return tile, deep
 
 
+def first_call(sensors, first, count):
+    own, depth = sensors.shape
+    width = first.shape[1]
+    part = depth // STEPS
+    return pl.pallas_call(
+        first_kernel,
+        grid=(STEPS,),
+        in_specs=[
+            pl.BlockSpec((own, part), lambda i: (0, i)),
+            pl.BlockSpec((part, width), lambda i: (i, 0)),
+        ],
+        out_specs=[whole(own, width), whole(count, own, width)],
+        out_shape=[
+            jax.ShapeDtypeStruct((own, width), BF16),
+            jax.ShapeDtypeStruct((count, own, width), BF16),
+        ],
+        scratch_shapes=[pltpu.VMEM((own, width), F32)],
+        compiler_params=PARAMS,
+        name="branch_first",
+    )(there(sensors), there(first))
+
+
 def forward_call(coords, first, second):
     points, width = coords.shape[1], first.shape[1]
     tile, deep = tiles(points)
@@ -553,7 +591,7 @@
 
 
 def spread_specs(got, shape, side):
-    steps = 4
+    steps = STEPS
     part = got.shape[0] // steps
     fields = shape[0] // (2 * got.shape[0])
     return (
@@ -628,8 +666,8 @@
     own = sensors.shape[0]
     fields = sensors.shape[1] // chips
 
-    own_one = jnp.tanh(dot(sensors, branch_first)).astype(BF16)
-    ones = swap(jnp.broadcast_to(own_one[None], (pts_size, own, width)), "pts")
+    own_one, told_one = first_call(sensors, branch_first, pts_size)
+    ones = swap(told_one, "pts")
     blocks = sensors.reshape(own, chips, fields).transpose(1, 0, 2)
     points_all, squash, inner, combos, weights = forward_call(coords, trunk_first, trunk_second)
     cots, feats, shares = project_call(

time: 117 us -> 113 us (0.966)
  local copies, waits for them, and re-layouts: 2.65 us -> 0.49 us
  matrix products: 1.25 us -> 0 us
    pallas_call x0 -> x1, Pallas kernels: none -> 2.57 us  [first_call(): pl.pallas_call(first_kernel, grid=(STEPS,), in_specs=[pl.BlockSpec((own,...]
    unnamed x16 -> x14, local copies, waits for them, and re-layouts: 1.56 us -> 0.03 us
    dot_general x1 -> x0, matrix products: 1.25 us -> none  [dot(): return lax.dot_general(left, right, dims, preferred_element_type=F32)]
  transfers between devices with their start and end apart: 4 -> 4, of which waited for: 1 -> 1; matrix products, arithmetic and copies ran while one was open for 0% -> 0% of each run, Pallas kernels for 26% -> 25%
where the time goes in v5:
time: 113 us; the launch traced here: 112 us
  blocking collectives  48.6 us (43%)
  Pallas kernels  41.2 us (36%)
  starting transfers between devices  19.2 us (17%)
  waiting for transfers between devices  1.92 us (2%)
    all_to_all x2, blocking collectives, swap(): return lax.all_to_all(parts, axes, split_axis=0, concat_axis=0, tiled=True)  48.6 us
    pallas_call x1, Pallas kernels, backward_call(): pl.pallas_call(backward_kernel, grid=(points // tile,), in_specs=[pl.Bloc...  16.3 us
    all_to_all x2, starting transfers between devices, swap(): return lax.all_to_all(parts, axes, split_axis=0, concat_axis=0, tiled=True)  14.1 us
    pallas_call x1, Pallas kernels, forward_call(): pl.pallas_call(forward_kernel, grid=(points // tile,), in_specs=[pl.Block...  9.32 us
    pallas_call x1, Pallas kernels, project_call(): pl.pallas_call(functools.partial(project_kernel, weight, scale), grid=(po...  7.07 us
    ppermute x2, starting transfers between devices, across_chip(): return lax.ppermute(value, 'core', [(0, 1), (1, 0)])  5.03 us
    pallas_call x1, Pallas kernels, first_call(): pl.pallas_call(first_kernel, grid=(STEPS,), in_specs=[pl.BlockSpec((own,...  2.57 us
  transfers between devices with their start and end apart: 4, of which 1 were waited for; matrix products, arithmetic and copies ran while one was open for 0% of the time, Pallas kernels for 25%

profile of v5, /device:TPU:1, one launch (start us, length us, event | category | flops | bytes accessed | tf_op | source)
XLA Modules:
  0.0 112.5 jit_solution(1045076724992904997)
XLA Ops:
  0.6 0.0 copy-start.6
  0.6 0.0 copy-start.4
  0.7 2.6 %branch_first.1 = (bf16[8,256]{1,0:T(8,128)(2,1)S(1)}, bf16[8,8,256]{2,1,0:T(8,128)(2,1)}) custom-call(bf16[8,4096]{1,0:T(8,128)(2,1)} %sensors_ref.1, bf16[4096,256]{1,0:T(8,128)(2,1)} %first_ref.3), custom_call_target="tpu_custom_call" | custom-call | tf_op jit(solution)/shard_map/branch_first/pallas_call | solution.py:445
  3.3 7.5 %all-to-all-start = ((bf16[8,8,256]{2,1,0:T(8,128)(2,1)}), bf16[8,8,256]{2,1,0:T(8,128)(2,1)S(1)}, u32[]{:S(2)}, u32[]{:S(2)}) async-start(bf16[8,8,256]{2,1,0:T(8,128)(2,1)} %get-tuple-element.29), calls=%async_computation | async-start | bytes 65536 | tf_op jit(solution)/shard_map/all_to_all | solution.py:639
  10.8 0.2 reshape.25
  10.9 0.1 copy.18
  11.1 9.3 %trunk_forward.1 = (bf16[4,2048,256]{2,1,0:T(8,128)(2,1)}, f32[2048,256]{1,0:T(8,128)}, bf16[7,2048,256]{2,1,0:T(8,128)(2,1)}, bf16[5,2048,256]{2,1,0:T(8,128)(2,1)}, bf16[8,256,256]{2,1,0:T(8,128)(2,1)}) custom-call(f32[2,2048]{1,0:T(2,128)S(1)} %copy-done.4, f32[2,256]{1,0:T(2,128)S(1)} %copy-done.5, bf16[256,256]{1,0:T(8,128)(2,1)S(1)} %copy-done.3), custom_call_target="tpu_custom_call" | custom-call | tf_op jit(solution)/shard_map/trunk_forward/pallas_call | solution.py:467
  20.4 0.0 all-to-all-done.ones_ref
  20.4 7.1 %project.1 = (bf16[5,64,2048]{2,1,0:T(8,128)(2,1)}, bf16[64,256]{1,0:T(8,128)(2,1)}, bf16[8,8,256]{2,1,0:T(8,128)(2,1)}) custom-call(bf16[8,8,256]{2,1,0:T(8,128)(2,1)S(1)} %all-to-all-done.ones_ref, bf16[256,256]{1,0:T(8,128)(2,1)S(1)} %copy-done, bf16[256,256]{1,0:T(8,128)(2,1)S(1)} %copy-done.1, bf16[256,256]{1,0:T(8,128)(2,1)S(1)} %copy-done.2, ...), custom_call_target="tpu_custom_call" | custom-call | tf_op jit(solution)/shard_map/project/pallas_call | solution.py:493
  27.5 6.6 %all-to-all-start.1 = ((bf16[8,8,256]{2,1,0:T(8,128)(2,1)}), bf16[8,8,256]{2,1,0:T(8,128)(2,1)S(1)}, u32[]{:S(2)}, u32[]{:S(2)}) async-start(bf16[8,8,256]{2,1,0:T(8,128)(2,1)} %get-tuple-element.31), calls=%async_computation.1 | async-start | bytes 65536 | tf_op jit(solution)/shard_map/all_to_all | solution.py:639
  34.1 16.3 %trunk_backward.1 = f32[64,8,192]{2,1,0:T(8,128)S(1)} custom-call(f32[2048,256]{1,0:T(8,128)} %get-tuple-element.32.squash_ref, bf16[4,2048,256]{2,1,0:T(8,128)(2,1)} %get-tuple-element.33.points_ref, bf16[7,2048,256]{2,1,0:T(8,128)(2,1)} %get-tuple-element.34.inner_ref, bf16[5,64,2048]{2,1,0:T(8,128)(2,1)} %get-tuple-element.35.cots_ref, ...), custom_call_target="tpu_custom_call" | custom-call | flops 5637144576 | bytes 25165824 | tf_op jit(solution)/shard_map/trunk_backward/pallas_call | solution.py:526
  50.5 0.0 all-to-all-done.1
  50.6 0.2 pad_maximum_fusion
  50.8 24.8 %all_to_all.20.mine_ref = bf16[64,8,768]{2,1,0:T(8,128)(2,1)S(1)} all-to-all(bf16[64,8,768]{2,1,0:T(8,128)(2,1)S(1)} %pad_maximum_fusion), channel_id=1, replica_groups=mesh['pairs'=8,'core'=2,'pts'=8] {'pairs','pts'}, dimensions={0} | all-to-all | bytes 1572864 | tf_op jit(solution)/shard_map/all_to_all | solution.py:639
  75.6 3.1 %collective-permute-start = (bf16[64,8,768]{2,1,0:T(8,128)(2,1)S(1)}, bf16[64,8,768]{2,1,0:T(8,128)(2,1)S(1)}, u32[]{:S(2)}, u32[]{:S(2)}) collective-permute-start(bf16[64,8,768]{2,1,0:T(8,128)(2,1)S(1)} %all_to_all.20.mine_ref), channel_id=1, source_target_pairs={{0,8},{8,0},{1,9},{9,1},{2,10},{10,2},{3,11},{11,3},{4,12},{12,4},... | collective-permute-start | bytes 2359304 | tf_op jit(solution)/shard_map/ppermute | solution.py:643
  78.7 1.9 %collective-permute-done.other_ref = bf16[64,8,768]{2,1,0:T(8,128)(2,1)S(1)} collective-permute-done((bf16[64,8,768]{2,1,0:T(8,128)(2,1)S(1)}, bf16[64,8,768]{2,1,0:T(8,128)(2,1)S(1)}, u32[]{:S(2)}, u32[]{:S(2)}) %collective-permute-start) | collective-permute-done | bytes 786464 | tf_op jit(solution)/shard_map/ppermute | solution.py:643
  80.6 1.7 %branch_backward.1 = (bf16[1024,256]{1,0:T(8,128)(2,1)S(1)}, bf16[1024,256]{1,0:T(8,128)(2,1)S(1)}, bf16[1024,256]{1,0:T(8,128)(2,1)S(1)}, bf16[1024,256]{1,0:T(...) custom-call(s32[1]{0:T(128)} %bitcast.core_ref, ...), custom_call_target="tpu_custom_call" | custom-call | tf_op jit(solution)/shard_map/branch_backward/pallas_call | solution.py:571
  82.4 0.2 broadcast_in_dim.8
  82.5 23.8 %all_to_all.21.mine_ref = bf16[64,72,128]{2,1,0:T(8,128)(2,1)S(1)} all-to-all(bf16[64,72,128]{2,1,0:T(8,128)(2,1)S(1)} %broadcast_in_dim.8), channel_id=1, replica_groups=mesh['pairs'=8,'core'=2,'pts'=8] {'pairs','pts'}, dimensions={0} | all-to-all | bytes 2359296 | tf_op jit(solution)/shard_map/all_to_all | solution.py:639
  106.3 1.9 %collective-permute-start.1 = (bf16[64,72,128]{2,1,0:T(8,128)(2,1)S(1)}, bf16[64,72,128]{2,1,0:T(8,128)(2,1)S(1)}, u32[]{:S(2)}, u32[]{:S(2)}) collective-permute-start(bf16[64,72,128]{2,1,0:T(8,128)(2,1)S(1)} %all_to_all.21.mine_ref), channel_id=1, source_target_pairs={{0,8},{8,0},{1,9},{9,1},{2,10},{10,2},{3,11},{11,3},{4,12},{12,4},... | collective-permute-start | bytes 3538952 | tf_op jit(solution)/shard_map/ppermute | solution.py:643
  108.2 1.4 %branch_gradients.1 = (f32[256,256]{1,0:T(8,128)}, f32[256,256]{1,0:T(8,128)}, f32[256,256]{1,0:T(8,128)}) custom-call(bf16[1024,256]{1,0:T(8,128)(2,1)S(1)} %get-tuple-element.41.u_ref, bf16[1024,256]{1,0:T(8,128)(2,1)S(1)} %get-tuple-element.42.features_ref, bf16[1024,256]{1,0:T(8,128)(2,1)S(1)} %get-tuple-element.43.two_ref, ...), custom_call_target="tpu_custom_call" | custom-call | tf_op jit(solution)/shard_map/branch_gradients/pallas_call | solution.py:584
  109.6 1.5 %spread_mine.1 = (f32[64,2,32,256]{3,2,1,0:T(8,128)}, f32[256,256]{1,0:T(8,128)}) custom-call(s32[1]{0:T(128)} %bitcast.core_ref, bf16[64,72,128]{2,1,0:T(8,128)(2,1)S(1)} %all_to_all.21.mine_ref), custom_call_target="tpu_custom_call" | custom-call | tf_op jit(solution)/shard_map/spread_mine/pallas_call | solution.py:607
  111.1 0.0 collective-permute-done.1.other_ref
  111.1 1.4 %spread_other.1 = f32[64,2,32,256]{3,2,1,0:T(8,128)} custom-call(s32[1]{0:T(128)} %bitcast.core_ref, bf16[64,72,128]{2,1,0:T(8,128)(2,1)S(1)} %collective-permute-done.1.other_ref, f32[64,2,32,256]{3,2,1,0:T(8,128)} %get-tuple-element.40.kept_ref), custom_call_target="tpu_custom_call", output_to_operand_aliasing={{}: (2, {})} | custom-call | tf_op jit(solution)/shard_map/spread_other/pallas_call | solution.py:623
  (16 shorter events, 0.1 us)
Async XLA Ops:
  0.6 10.1 %copy-start.6 = (bf16[8,4096]{1,0:T(8,128)(2,1)S(1)}, bf16[8,4096]{1,0:T(8,128)(2,1)}, u32[]{:S(2)}) copy-start(bf16[8,4096]{1,0:T(8,128)(2,1)} %sensors_ref.1) | copy-start | bytes 196612
  0.6 10.4 %copy-start.4 = (f32[2,2048]{1,0:T(2,128)S(1)}, f32[2,2048]{1,0:T(2,128)}, u32[]{:S(2)}) copy-start(f32[2,2048]{1,0:T(2,128)} %coords_ref.3) | copy-start | bytes 49156
  0.7 10.4 %copy-start.5 = (f32[2,256]{1,0:T(2,128)S(1)}, f32[2,256]{1,0:T(2,128)}, u32[]{:S(2)}) copy-start(f32[2,256]{1,0:T(2,128)} %first_ref.5) | copy-start | bytes 6148
  0.7 10.4 %copy-start.3 = (bf16[256,256]{1,0:T(8,128)(2,1)S(1)}, bf16[256,256]{1,0:T(8,128)(2,1)}, u32[]{:S(2)}) copy-start(bf16[256,256]{1,0:T(8,128)(2,1)} %second_ref.3) | copy-start | bytes 393220
  0.7 19.7 %copy-start = (bf16[256,256]{1,0:T(8,128)(2,1)S(1)}, bf16[256,256]{1,0:T(8,128)(2,1)}, u32[]{:S(2)}) copy-start(bf16[256,256]{1,0:T(8,128)(2,1)} %branch_second_ref.3) | copy-start | bytes 393220
  0.7 19.7 %copy-start.1 = (bf16[256,256]{1,0:T(8,128)(2,1)S(1)}, bf16[256,256]{1,0:T(8,128)(2,1)}, u32[]{:S(2)}) copy-start(bf16[256,256]{1,0:T(8,128)(2,1)} %branch_third_ref.3) | copy-start | bytes 393220
  0.7 19.7 %copy-start.2 = (bf16[256,256]{1,0:T(8,128)(2,1)S(1)}, bf16[256,256]{1,0:T(8,128)(2,1)}, u32[]{:S(2)}) copy-start(bf16[256,256]{1,0:T(8,128)(2,1)} %third_ref.3) | copy-start | bytes 393220
  3.3 17.1 %all-to-all-start = ((bf16[8,8,256]{2,1,0:T(8,128)(2,1)}), bf16[8,8,256]{2,1,0:T(8,128)(2,1)S(1)}, u32[]{:S(2)}, u32[]{:S(2)}) async-start(bf16[8,8,256]{2,1,0:T(8,128)(2,1)} %get-tuple-element.29), calls=%async_computation | async-start | bytes 65536 | tf_op jit(solution)/shard_map/all_to_all | solution.py:639
  27.5 23.0 %all-to-all-start.1 = ((bf16[8,8,256]{2,1,0:T(8,128)(2,1)}), bf16[8,8,256]{2,1,0:T(8,128)(2,1)S(1)}, u32[]{:S(2)}, u32[]{:S(2)}) async-start(bf16[8,8,256]{2,1,0:T(8,128)(2,1)} %get-tuple-element.31), calls=%async_computation.1 | async-start | bytes 65536 | tf_op jit(solution)/shard_map/all_to_all | solution.py:639
  75.6 5.1 %collective-permute-start = (bf16[64,8,768]{2,1,0:T(8,128)(2,1)S(1)}, bf16[64,8,768]{2,1,0:T(8,128)(2,1)S(1)}, u32[]{:S(2)}, u32[]{:S(2)}) collective-permute-start(bf16[64,8,768]{2,1,0:T(8,128)(2,1)S(1)} %all_to_all.20.mine_ref), channel_id=1, source_target_pairs={{0,8},{8,0},{1,9},{9,1},{2,10},{10,2},{3,11},{11,3},{4,12},{12,4},... | collective-permute-start | bytes 2359304 | tf_op jit(solution)/shard_map/ppermute | solution.py:643
  106.3 4.8 %collective-permute-start.1 = (bf16[64,72,128]{2,1,0:T(8,128)(2,1)S(1)}, bf16[64,72,128]{2,1,0:T(8,128)(2,1)S(1)}, u32[]{:S(2)}, u32[]{:S(2)}) collective-permute-start(bf16[64,72,128]{2,1,0:T(8,128)(2,1)S(1)} %all_to_all.21.mine_ref), channel_id=1, source_target_pairs={{0,8},{8,0},{1,9},{9,1},{2,10},{10,2},{3,11},{11,3},{4,12},{12,4},... | collective-permute-start | bytes 3538952 | tf_op jit(solution)/shard_map/ppermute | solution.py:643

commit v6 on v5

--- a/solution.py
+++ b/solution.py
@@ -322,51 +322,49 @@
 
 def branch_kernel(
     scale,
+    fields,
     core_ref,
-    mine_ref,
-    other_ref,
+    from_ref,
     third_ref,
     branch_third_ref,
     branch_second_ref,
-    u_ref,
-    features_ref,
-    two_ref,
-    feature_back_ref,
-    one_ref,
-    back_two_ref,
-    rows_ref,
-    first_ref,
-    columns_ref,
+    *refs,
 ):
+    first = len(refs) == 8
+    sums = () if first else refs[:2]
+    u_ref, features_ref, two_ref, feature_back_ref, one_ref, back_two_ref = refs[-8:-2]
     core = core_ref[0]
     width = third_ref.shape[0]
-    half, fields = u_ref.shape[0] // 2, columns_ref.shape[1]
-    across = 2 * width // mine_ref.shape[1]
+    half = u_ref.shape[0]
+    across = 2 * width // from_ref.shape[1]
     here = width + LANES + across
-    total = None
-    for place, from_ref in ((core, mine_ref), (1 - core, other_ref)):
-        rows = pl.ds(pl.multiple_of(place * half, half), half)
-        got = from_ref[...].astype(F32)
-        part = jnp.sum(got[:, :, width : width + 2 * LANES], axis=0)
-        total = part if total is None else total + part
-        got = got.reshape(half, -1)
-        u_ref[rows, :] = got[:, 0:width].astype(BF16)
-        one_ref[rows, :] = got[:, width + 2 * LANES :].astype(BF16)
-        columns_ref[rows, :] = jnp.where(
-            core == 0,
-            got[:, here : here + fields],
-            got[:, here + fields : here + 2 * fields],
-        ).astype(BF16)
+    got = from_ref[...].astype(F32)
+    total = jnp.sum(got[:, :, width : width + 2 * LANES], axis=0)
+    got = got.reshape(half, -1)
+    u = got[:, 0:width].astype(BF16)
+    one = got[:, width + 2 * LANES :]
+    columns = jnp.where(
+        core == 0,
+        got[:, here : here + fields],
+        got[:, here + fields : here + 2 * fields],
+    ).astype(BF16)
+    u_ref[...] = u
+    one_ref[...] = one.astype(BF16)
     wide = jnp.tanh(dot(one_ref[...], branch_second_ref[...]))
     two_ref[...] = wide.astype(BF16)
     features_ref[...] = dot(two_ref[...], branch_third_ref[...]).astype(BF16)
-    feature_back = (dot(u_ref[...], third_ref[...]) * scale).astype(BF16)
+    feature_back = (dot(u, third_ref[...]) * scale).astype(BF16)
     feature_back_ref[...] = feature_back
     back_two = (dot(feature_back, branch_third_ref[...], NT) * (1.0 - wide * wide)).astype(BF16)
     back_two_ref[...] = back_two
-    one = one_ref[...].astype(F32)
     back_one = (dot(back_two, branch_second_ref[...], NT) * (1.0 - one * one)).astype(BF16)
-    rows = dot(columns_ref[...], back_one, TN)
+    rows = dot(columns, back_one, TN)
+    if first:
+        refs[-2][...] = rows
+        refs[-1][...] = total
+        return
+    rows_ref, first_ref = refs[-2:]
+    rows, total = rows + sums[0][...], total + sums[1][...]
     parts = [rows[:, lane : lane + LANES] for lane in range(0, width, LANES)]
     rows_ref[...] = jnp.concatenate(parts + [total[:, 0:LANES]], axis=0).astype(BF16)
     deep = width // across
@@ -377,21 +375,12 @@
             ]
 
 
-def gradient_kernel(
-    scale,
-    u_ref,
-    features_ref,
-    two_ref,
-    feature_back_ref,
-    one_ref,
-    back_two_ref,
-    trunk_ref,
-    third_ref,
-    second_ref,
-):
-    trunk_ref[...] = dot(u_ref[...], features_ref[...], TN) * scale
-    third_ref[...] = dot(two_ref[...], feature_back_ref[...], TN)
-    second_ref[...] = dot(one_ref[...], back_two_ref[...], TN)
+def gradient_kernel(scale, *refs):
+    mine, other, outs = refs[:6], refs[6:12], refs[12:]
+    for out_ref, (left, right), by in zip(outs, ((0, 1), (2, 3), (4, 5)), (scale, None, None)):
+        parts = [dot(half[left][...], half[right][...], TN) for half in (mine, other)]
+        total = parts[0] + parts[1]
+        out_ref[...] = total if by is None else total * by
 
 
 def spread_rows(from_ref, grad_ref):
@@ -565,29 +554,30 @@
     )
 
 
-def branch_call(core, mine, other, third, branch_third, branch_second, fields, scale):
-    count, width = 2 * mine.shape[0] * mine.shape[1], third.shape[0]
-    rows = fields * (width // LANES) + mine.shape[1]
+def branch_call(core, got, third, branch_third, branch_second, fields, scale, sums=()):
+    count, own, width = got.shape[0] * got.shape[1], got.shape[1], third.shape[0]
+    rows = fields * (width // LANES) + own
+    last = [jax.ShapeDtypeStruct((fields, width), F32), jax.ShapeDtypeStruct((own, 2 * LANES), F32)]
+    if sums:
+        last = [jax.ShapeDtypeStruct((rows, LANES), BF16), jax.ShapeDtypeStruct((2, width), F32)]
     return pl.pallas_call(
-        functools.partial(branch_kernel, scale),
-        in_specs=[SCALAR] + [LOCAL] * 5,
-        out_shape=[jax.ShapeDtypeStruct((count, width), BF16)] * 6
-        + [jax.ShapeDtypeStruct((rows, LANES), BF16), jax.ShapeDtypeStruct((2, width), F32)],
-        scratch_shapes=[pltpu.VMEM((count, fields), BF16)],
+        functools.partial(branch_kernel, scale, fields),
+        in_specs=[SCALAR] + [LOCAL] * (4 + len(sums)),
+        out_shape=[jax.ShapeDtypeStruct((count, width), BF16)] * 6 + last,
         compiler_params=SMALL,
-        name="branch_backward",
-    )(core, mine, other, third, branch_third, branch_second)
-
-
-def gradient_call(u, features, two, feature_back, one, back_two, scale):
-    shape = (u.shape[1], features.shape[1])
+        name="branch_other" if sums else "branch_mine",
+    )(core, got, third, branch_third, branch_second, *sums)
+
+
+def gradient_call(mine, other, scale):
+    shape = (mine[0].shape[1], mine[1].shape[1])
     return pl.pallas_call(
         functools.partial(gradient_kernel, scale),
-        in_specs=[LOCAL] * 6,
+        in_specs=[LOCAL] * 12,
         out_shape=[jax.ShapeDtypeStruct(shape, F32)] * 3,
         compiler_params=SMALL,
         name="branch_gradients",
-    )(u, features, two, feature_back, one, back_two)
+    )(*mine, *other)
 
 
 def spread_specs(got, shape, side):
@@ -705,14 +695,20 @@
     )
     every = swap(pieces, ("pairs", "pts"))
     every_other = across_chip(every)
-    u, features, two, feature_back, one, back_two, rows, grad_t1 = branch_call(
-        core, every, every_other, trunk_third, branch_third, branch_second, fields // 2, scale
+    branch = functools.partial(
+        branch_call,
+        core,
+        third=trunk_third,
+        branch_third=branch_third,
+        branch_second=branch_second,
+        fields=fields // 2,
+        scale=scale,
     )
+    *half_mine, rows, total = branch(got=every)
+    *half_other, rows, grad_t1 = branch(got=every_other, sums=(rows, total))
     mine = swap(told(rows), ("pairs", "pts"))
     other = across_chip(mine)
-    grad_t3, grad_b3, grad_b2 = gradient_call(
-        u, features, two, feature_back, one, back_two, scale
-    )
+    grad_t3, grad_b3, grad_b2 = gradient_call(half_mine, half_other, scale)
     kept, grad_t2 = mine_call(core, mine, branch_first.shape, width)
     grad_b1 = other_call(core, other, kept, branch_first.shape).reshape(branch_first.shape)
     return (grad_b1, grad_b2, grad_b3, grad_t1, grad_t2, grad_t3)

time: 113 us -> 112 us (level)
  transfers between devices with their start and end apart: 4 -> 4, of which waited for: 1 -> 1; matrix products, arithmetic and copies ran while one was open for 0% -> 0% of each run, Pallas kernels for 25% -> 26%
where the time goes in v6:
time: 112 us
  blocking collectives  48.6 us (43%)
  Pallas kernels  41.6 us (37%)
  starting transfers between devices  19.2 us (17%)
  waiting for transfers between devices  1.12 us (1%)
    all_to_all x2, blocking collectives, swap(): return lax.all_to_all(parts, axes, split_axis=0, concat_axis=0, tiled=True)  48.6 us
    pallas_call x1, Pallas kernels, backward_call(): pl.pallas_call(backward_kernel, grid=(points // tile,), in_specs=[pl.Bloc...  16.3 us
    all_to_all x2, starting transfers between devices, swap(): return lax.all_to_all(parts, axes, split_axis=0, concat_axis=0, tiled=True)  14.1 us
    pallas_call x1, Pallas kernels, forward_call(): pl.pallas_call(forward_kernel, grid=(points // tile,), in_specs=[pl.Block...  9.31 us
    pallas_call x1, Pallas kernels, project_call(): pl.pallas_call(functools.partial(project_kernel, weight, scale), grid=(po...  7.02 us
    ppermute x2, starting transfers between devices, across_chip(): return lax.ppermute(value, 'core', [(0, 1), (1, 0)])  5.03 us
    pallas_call x1, Pallas kernels, first_call(): pl.pallas_call(first_kernel, grid=(STEPS,), in_specs=[pl.BlockSpec((own,...  2.57 us
  transfers between devices with their start and end apart: 4, of which 1 were waited for; matrix products, arithmetic and copies ran while one was open for 0% of the time, Pallas kernels for 26%

profile of v6, /device:TPU:1, one launch (start us, length us, event | category | flops | bytes accessed | tf_op | source)
XLA Modules:
  0.0 112.0 jit_solution(18062532336565038121)
XLA Ops:
  0.6 0.0 copy-start.6
  0.7 2.6 %branch_first.1 = (bf16[8,256]{1,0:T(8,128)(2,1)S(1)}, bf16[8,8,256]{2,1,0:T(8,128)(2,1)}) custom-call(bf16[8,4096]{1,0:T(8,128)(2,1)} %sensors_ref.1, bf16[4096,256]{1,0:T(8,128)(2,1)} %first_ref.3), custom_call_target="tpu_custom_call" | custom-call | tf_op jit(solution)/shard_map/branch_first/pallas_call | solution.py:434
  3.3 7.5 %all-to-all-start = ((bf16[8,8,256]{2,1,0:T(8,128)(2,1)}), bf16[8,8,256]{2,1,0:T(8,128)(2,1)S(1)}, u32[]{:S(2)}, u32[]{:S(2)}) async-start(bf16[8,8,256]{2,1,0:T(8,128)(2,1)} %get-tuple-element.37), calls=%async_computation | async-start | bytes 65536 | tf_op jit(solution)/shard_map/all_to_all | solution.py:629
  10.8 0.2 reshape.25
  10.9 0.1 copy.18
  11.1 9.3 %trunk_forward.1 = (bf16[4,2048,256]{2,1,0:T(8,128)(2,1)}, f32[2048,256]{1,0:T(8,128)}, bf16[7,2048,256]{2,1,0:T(8,128)(2,1)}, bf16[5,2048,256]{2,1,0:T(8,128)(2,1)}, bf16[8,256,256]{2,1,0:T(8,128)(2,1)}) custom-call(f32[2,2048]{1,0:T(2,128)S(1)} %copy-done.4, f32[2,256]{1,0:T(2,128)S(1)} %copy-done.5, bf16[256,256]{1,0:T(8,128)(2,1)S(1)} %copy-done.3), custom_call_target="tpu_custom_call" | custom-call | tf_op jit(solution)/shard_map/trunk_forward/pallas_call | solution.py:456
  20.4 0.0 all-to-all-done.ones_ref
  20.4 7.0 %project.1 = (bf16[5,64,2048]{2,1,0:T(8,128)(2,1)}, bf16[64,256]{1,0:T(8,128)(2,1)}, bf16[8,8,256]{2,1,0:T(8,128)(2,1)}) custom-call(bf16[8,8,256]{2,1,0:T(8,128)(2,1)S(1)} %all-to-all-done.ones_ref, bf16[256,256]{1,0:T(8,128)(2,1)S(1)} %copy-done, bf16[256,256]{1,0:T(8,128)(2,1)S(1)} %copy-done.1, bf16[256,256]{1,0:T(8,128)(2,1)S(1)} %copy-done.2, ...), custom_call_target="tpu_custom_call" | custom-call | tf_op jit(solution)/shard_map/project/pallas_call | solution.py:482
  27.4 6.6 %all-to-all-start.1 = ((bf16[8,8,256]{2,1,0:T(8,128)(2,1)}), bf16[8,8,256]{2,1,0:T(8,128)(2,1)S(1)}, u32[]{:S(2)}, u32[]{:S(2)}) async-start(bf16[8,8,256]{2,1,0:T(8,128)(2,1)} %get-tuple-element.39), calls=%async_computation.1 | async-start | bytes 65536 | tf_op jit(solution)/shard_map/all_to_all | solution.py:629
  34.1 16.3 %trunk_backward.1 = f32[64,8,192]{2,1,0:T(8,128)S(1)} custom-call(f32[2048,256]{1,0:T(8,128)} %get-tuple-element.40.squash_ref, bf16[4,2048,256]{2,1,0:T(8,128)(2,1)} %get-tuple-element.41.points_ref, bf16[7,2048,256]{2,1,0:T(8,128)(2,1)} %get-tuple-element.42.inner_ref, bf16[5,64,2048]{2,1,0:T(8,128)(2,1)} %get-tuple-element.43.cots_ref, ...), custom_call_target="tpu_custom_call" | custom-call | flops 5637144576 | bytes 25165824 | tf_op jit(solution)/shard_map/trunk_backward/pallas_call | solution.py:515
  50.5 0.0 all-to-all-done.1
  50.6 0.2 pad_maximum_fusion
  50.8 24.8 %all_to_all.20.from_ref = bf16[64,8,768]{2,1,0:T(8,128)(2,1)S(1)} all-to-all(bf16[64,8,768]{2,1,0:T(8,128)(2,1)S(1)} %pad_maximum_fusion), channel_id=1, replica_groups=mesh['pairs'=8,'core'=2,'pts'=8] {'pairs','pts'}, dimensions={0} | all-to-all | bytes 1572864 | tf_op jit(solution)/shard_map/all_to_all | solution.py:629
  75.5 3.1 %collective-permute-start = (bf16[64,8,768]{2,1,0:T(8,128)(2,1)S(1)}, bf16[64,8,768]{2,1,0:T(8,128)(2,1)S(1)}, u32[]{:S(2)}, u32[]{:S(2)}) collective-permute-start(bf16[64,8,768]{2,1,0:T(8,128)(2,1)S(1)} %all_to_all.20.from_ref), channel_id=1, source_target_pairs={{0,8},{8,0},{1,9},{9,1},{2,10},{10,2},{3,11},{11,3},{4,12},{12,4},... | collective-permute-start | bytes 2359304 | tf_op jit(solution)/shard_map/ppermute | solution.py:633
  78.7 0.8 branch_mine.1
  79.5 1.1 collective-permute-done.from_ref
  80.6 1.3 %branch_other.1 = (bf16[512,256]{1,0:T(8,128)(2,1)S(1)}, bf16[512,256]{1,0:T(8,128)(2,1)S(1)}, bf16[512,256]{1,0:T(8,128)(2,1)S(1)}, bf16[512,256]{1,0:T(8,128)(...) custom-call(s32[1]{0:T(128)} %bitcast.core_ref, ...), custom_call_target="tpu_custom_call" | custom-call | tf_op jit(solution)/shard_map/branch_other/pallas_call | solution.py:563
  81.9 0.2 broadcast_in_dim.8
  82.0 23.8 %all_to_all.21.mine_ref = bf16[64,72,128]{2,1,0:T(8,128)(2,1)S(1)} all-to-all(bf16[64,72,128]{2,1,0:T(8,128)(2,1)S(1)} %broadcast_in_dim.8), channel_id=1, replica_groups=mesh['pairs'=8,'core'=2,'pts'=8] {'pairs','pts'}, dimensions={0} | all-to-all | bytes 2359296 | tf_op jit(solution)/shard_map/all_to_all | solution.py:629
  105.9 1.9 %collective-permute-start.1 = (bf16[64,72,128]{2,1,0:T(8,128)(2,1)S(1)}, bf16[64,72,128]{2,1,0:T(8,128)(2,1)S(1)}, u32[]{:S(2)}, u32[]{:S(2)}) collective-permute-start(bf16[64,72,128]{2,1,0:T(8,128)(2,1)S(1)} %all_to_all.21.mine_ref), channel_id=1, source_target_pairs={{0,8},{8,0},{1,9},{9,1},{2,10},{10,2},{3,11},{11,3},{4,12},{12,4},... | collective-permute-start | bytes 3538952 | tf_op jit(solution)/shard_map/ppermute | solution.py:633
  107.7 1.4 %branch_gradients.1 = (f32[256,256]{1,0:T(8,128)}, f32[256,256]{1,0:T(8,128)}, f32[256,256]{1,0:T(8,128)}) custom-call(bf16[512,256]{1,0:T(8,128)(2,1)S(1)} %get-tuple-element.51.refs_0_, bf16[512,256]{1,0:T(8,128)(2,1)S(1)} %get-tuple-element.52.refs_1_, bf16[512,256]{1,0:T(8,128)(2,1)S(1)} %get-tuple-element.53.refs_2_, ...), custom_call_target="tpu_custom_call" | custom-call | tf_op jit(solution)/shard_map/branch_gradients/pallas_call | solution.py:574
  109.1 1.5 %spread_mine.1 = (f32[64,2,32,256]{3,2,1,0:T(8,128)}, f32[256,256]{1,0:T(8,128)}) custom-call(s32[1]{0:T(128)} %bitcast.core_ref, bf16[64,72,128]{2,1,0:T(8,128)(2,1)S(1)} %all_to_all.21.mine_ref), custom_call_target="tpu_custom_call" | custom-call | tf_op jit(solution)/shard_map/spread_mine/pallas_call | solution.py:597
  110.6 0.0 collective-permute-done.1.other_ref
  110.6 1.4 %spread_other.1 = f32[64,2,32,256]{3,2,1,0:T(8,128)} custom-call(s32[1]{0:T(128)} %bitcast.core_ref, bf16[64,72,128]{2,1,0:T(8,128)(2,1)S(1)} %collective-permute-done.1.other_ref, f32[64,2,32,256]{3,2,1,0:T(8,128)} %get-tuple-element.50.kept_ref), custom_call_target="tpu_custom_call", output_to_operand_aliasing={{}: (2, {})} | custom-call | tf_op jit(solution)/shard_map/spread_other/pallas_call | solution.py:613
  (17 shorter events, 0.1 us)
Async XLA Ops:
  0.6 10.1 %copy-start.6 = (bf16[8,4096]{1,0:T(8,128)(2,1)S(1)}, bf16[8,4096]{1,0:T(8,128)(2,1)}, u32[]{:S(2)}) copy-start(bf16[8,4096]{1,0:T(8,128)(2,1)} %sensors_ref.1) | copy-start | bytes 196612
  0.6 10.4 %copy-start.4 = (f32[2,2048]{1,0:T(2,128)S(1)}, f32[2,2048]{1,0:T(2,128)}, u32[]{:S(2)}) copy-start(f32[2,2048]{1,0:T(2,128)} %coords_ref.3) | copy-start | bytes 49156
  0.7 10.4 %copy-start.5 = (f32[2,256]{1,0:T(2,128)S(1)}, f32[2,256]{1,0:T(2,128)}, u32[]{:S(2)}) copy-start(f32[2,256]{1,0:T(2,128)} %first_ref.5) | copy-start | bytes 6148
  0.7 10.4 %copy-start.3 = (bf16[256,256]{1,0:T(8,128)(2,1)S(1)}, bf16[256,256]{1,0:T(8,128)(2,1)}, u32[]{:S(2)}) copy-start(bf16[256,256]{1,0:T(8,128)(2,1)} %second_ref.3) | copy-start | bytes 393220
  0.7 19.7 %copy-start = (bf16[256,256]{1,0:T(8,128)(2,1)S(1)}, bf16[256,256]{1,0:T(8,128)(2,1)}, u32[]{:S(2)}) copy-start(bf16[256,256]{1,0:T(8,128)(2,1)} %branch_second_ref.5) | copy-start | bytes 393220
  0.7 19.7 %copy-start.1 = (bf16[256,256]{1,0:T(8,128)(2,1)S(1)}, bf16[256,256]{1,0:T(8,128)(2,1)}, u32[]{:S(2)}) copy-start(bf16[256,256]{1,0:T(8,128)(2,1)} %branch_third_ref.5) | copy-start | bytes 393220
  0.7 19.7 %copy-start.2 = (bf16[256,256]{1,0:T(8,128)(2,1)S(1)}, bf16[256,256]{1,0:T(8,128)(2,1)}, u32[]{:S(2)}) copy-start(bf16[256,256]{1,0:T(8,128)(2,1)} %third_ref.5) | copy-start | bytes 393220
  3.3 17.1 %all-to-all-start = ((bf16[8,8,256]{2,1,0:T(8,128)(2,1)}), bf16[8,8,256]{2,1,0:T(8,128)(2,1)S(1)}, u32[]{:S(2)}, u32[]{:S(2)}) async-start(bf16[8,8,256]{2,1,0:T(8,128)(2,1)} %get-tuple-element.37), calls=%async_computation | async-start | bytes 65536 | tf_op jit(solution)/shard_map/all_to_all | solution.py:629
  27.4 23.0 %all-to-all-start.1 = ((bf16[8,8,256]{2,1,0:T(8,128)(2,1)}), bf16[8,8,256]{2,1,0:T(8,128)(2,1)S(1)}, u32[]{:S(2)}, u32[]{:S(2)}) async-start(bf16[8,8,256]{2,1,0:T(8,128)(2,1)} %get-tuple-element.39), calls=%async_computation.1 | async-start | bytes 65536 | tf_op jit(solution)/shard_map/all_to_all | solution.py:629
  75.5 5.1 %collective-permute-start = (bf16[64,8,768]{2,1,0:T(8,128)(2,1)S(1)}, bf16[64,8,768]{2,1,0:T(8,128)(2,1)S(1)}, u32[]{:S(2)}, u32[]{:S(2)}) collective-permute-start(bf16[64,8,768]{2,1,0:T(8,128)(2,1)S(1)} %all_to_all.20.from_ref), channel_id=1, source_target_pairs={{0,8},{8,0},{1,9},{9,1},{2,10},{10,2},{3,11},{11,3},{4,12},{12,4},... | collective-permute-start | bytes 2359304 | tf_op jit(solution)/shard_map/ppermute | solution.py:633
  105.9 4.8 %collective-permute-start.1 = (bf16[64,72,128]{2,1,0:T(8,128)(2,1)S(1)}, bf16[64,72,128]{2,1,0:T(8,128)(2,1)S(1)}, u32[]{:S(2)}, u32[]{:S(2)}) collective-permute-start(bf16[64,72,128]{2,1,0:T(8,128)(2,1)S(1)} %all_to_all.21.mine_ref), channel_id=1, source_target_pairs={{0,8},{8,0},{1,9},{9,1},{2,10},{10,2},{3,11},{11,3},{4,12},{12,4},... | collective-permute-start | bytes 3538952 | tf_op jit(solution)/shard_map/ppermute | solution.py:633

commit v7 on v6

--- a/solution.py
+++ b/solution.py
@@ -330,9 +330,10 @@
     branch_second_ref,
     *refs,
 ):
-    first = len(refs) == 8
+    first = len(refs) == 11
     sums = () if first else refs[:2]
-    u_ref, features_ref, two_ref, feature_back_ref, one_ref, back_two_ref = refs[-8:-2]
+    start = len(sums)
+    u_ref, features_ref, two_ref, feature_back_ref, one_ref, back_two_ref = refs[start : start + 6]
     core = core_ref[0]
     width = third_ref.shape[0]
     half = u_ref.shape[0]
@@ -360,8 +361,11 @@
     back_one = (dot(back_two, branch_second_ref[...], NT) * (1.0 - one * one)).astype(BF16)
     rows = dot(columns, back_one, TN)
     if first:
-        refs[-2][...] = rows
-        refs[-1][...] = total
+        refs[6][...] = rows
+        refs[7][...] = total
+        refs[8][...] = dot(u, features_ref[...], TN)
+        refs[9][...] = dot(two_ref[...], feature_back, TN)
+        refs[10][...] = dot(one_ref[...], back_two, TN)
         return
     rows_ref, first_ref = refs[-2:]
     rows, total = rows + sums[0][...], total + sums[1][...]
@@ -376,11 +380,10 @@
 
 
 def gradient_kernel(scale, *refs):
-    mine, other, outs = refs[:6], refs[6:12], refs[12:]
-    for out_ref, (left, right), by in zip(outs, ((0, 1), (2, 3), (4, 5)), (scale, None, None)):
-        parts = [dot(half[left][...], half[right][...], TN) for half in (mine, other)]
-        total = parts[0] + parts[1]
-        out_ref[...] = total if by is None else total * by
+    mine, other, outs = refs[:3], refs[3:9], refs[9:]
+    for k, by in enumerate((scale, None, None)):
+        total = mine[k][...] + dot(other[2 * k][...], other[2 * k + 1][...], TN)
+        outs[k][...] = total if by is None else total * by
 
 
 def spread_rows(from_ref, grad_ref):
@@ -497,7 +500,7 @@
         ],
         out_shape=[
             pltpu.HBM((5, funcs, points), BF16),
-            pltpu.HBM((funcs, width), BF16),
+            jax.ShapeDtypeStruct((funcs, width), BF16),
             jax.ShapeDtypeStruct(ones.shape, BF16),
         ],
         scratch_shapes=[pltpu.VMEM((funcs, width), F32)],
@@ -546,9 +549,9 @@
         there(points_all),
         there(inner),
         there(cots),
-        there(feats),
+        feats,
         coords,
-        there(weights),
+        weights,
         first,
         second,
     )
@@ -558,6 +561,7 @@
     count, own, width = got.shape[0] * got.shape[1], got.shape[1], third.shape[0]
     rows = fields * (width // LANES) + own
     last = [jax.ShapeDtypeStruct((fields, width), F32), jax.ShapeDtypeStruct((own, 2 * LANES), F32)]
+    last += [jax.ShapeDtypeStruct((width, width), F32)] * 3
     if sums:
         last = [jax.ShapeDtypeStruct((rows, LANES), BF16), jax.ShapeDtypeStruct((2, width), F32)]
     return pl.pallas_call(
@@ -570,10 +574,10 @@
 
 
 def gradient_call(mine, other, scale):
-    shape = (mine[0].shape[1], mine[1].shape[1])
+    shape = mine[0].shape
     return pl.pallas_call(
         functools.partial(gradient_kernel, scale),
-        in_specs=[LOCAL] * 12,
+        in_specs=[LOCAL] * 9,
         out_shape=[jax.ShapeDtypeStruct(shape, F32)] * 3,
         compiler_params=SMALL,
         name="branch_gradients",
@@ -704,11 +708,13 @@
         fields=fields // 2,
         scale=scale,
     )
-    *half_mine, rows, total = branch(got=every)
+    *_, rows, total, sum_t3, sum_b3, sum_b2 = branch(got=every)
     *half_other, rows, grad_t1 = branch(got=every_other, sums=(rows, total))
     mine = swap(told(rows), ("pairs", "pts"))
     other = across_chip(mine)
-    grad_t3, grad_b3, grad_b2 = gradient_call(half_mine, half_other, scale)
+    grad_t3, grad_b3, grad_b2 = gradient_call(
+        (sum_t3, sum_b3, sum_b2), half_other, scale
+    )
     kept, grad_t2 = mine_call(core, mine, branch_first.shape, width)
     grad_b1 = other_call(core, other, kept, branch_first.shape).reshape(branch_first.shape)
     return (grad_b1, grad_b2, grad_b3, grad_t1, grad_t2, grad_t3)

time: 112 us -> 112 us (level)
  transfers between devices with their start and end apart: 4 -> 4, of which waited for: 1 -> 0; matrix products, arithmetic and copies ran while one was open for 0% -> 0% of each run, Pallas kernels for 26% -> 27%
where the time goes in v7:
time: 112 us
  blocking collectives  48.6 us (43%)
  Pallas kernels  42.2 us (38%)
  starting transfers between devices  19.2 us (17%)
    all_to_all x2, blocking collectives, swap(): return lax.all_to_all(parts, axes, split_axis=0, concat_axis=0, tiled=True)  48.6 us
    pallas_call x1, Pallas kernels, backward_call(): pl.pallas_call(backward_kernel, grid=(points // tile,), in_specs=[pl.Bloc...  16 us
    all_to_all x2, starting transfers between devices, swap(): return lax.all_to_all(parts, axes, split_axis=0, concat_axis=0, tiled=True)  14.1 us
    pallas_call x1, Pallas kernels, forward_call(): pl.pallas_call(forward_kernel, grid=(points // tile,), in_specs=[pl.Block...  9.3 us
    pallas_call x1, Pallas kernels, project_call(): pl.pallas_call(functools.partial(project_kernel, weight, scale), grid=(po...  7.13 us
    ppermute x2, starting transfers between devices, across_chip(): return lax.ppermute(value, 'core', [(0, 1), (1, 0)])  5.03 us
    pallas_call x2, Pallas kernels, branch_call(): pl.pallas_call(functools.partial(branch_kernel, scale, fields), in_specs=...  3.16 us
    pallas_call x1, Pallas kernels, first_call(): pl.pallas_call(first_kernel, grid=(STEPS,), in_specs=[pl.BlockSpec((own,...  2.57 us
  transfers between devices with their start and end apart: 4, of which 0 were waited for; matrix products, arithmetic and copies ran while one was open for 0% of the time, Pallas kernels for 27%

profile of v7, /device:TPU:1, one launch (start us, length us, event | category | flops | bytes accessed | tf_op | source)
XLA Modules:
  0.0 111.5 jit_solution(10017751597562640557)
XLA Ops:
  0.6 0.0 copy-start.7
  0.7 2.6 %branch_first.1 = (bf16[8,256]{1,0:T(8,128)(2,1)S(1)}, bf16[8,8,256]{2,1,0:T(8,128)(2,1)}) custom-call(bf16[8,4096]{1,0:T(8,128)(2,1)} %sensors_ref.1, bf16[4096,256]{1,0:T(8,128)(2,1)} %first_ref.3), custom_call_target="tpu_custom_call" | custom-call | tf_op jit(solution)/shard_map/branch_first/pallas_call | solution.py:437
  3.3 7.5 %all-to-all-start = ((bf16[8,8,256]{2,1,0:T(8,128)(2,1)}), bf16[8,8,256]{2,1,0:T(8,128)(2,1)S(1)}, u32[]{:S(2)}, u32[]{:S(2)}) async-start(bf16[8,8,256]{2,1,0:T(8,128)(2,1)} %get-tuple-element.34), calls=%async_computation | async-start | bytes 65536 | tf_op jit(solution)/shard_map/all_to_all | solution.py:633
  10.8 0.2 reshape.25
  10.9 0.1 copy.18
  11.1 9.3 %trunk_forward.1 = (bf16[4,2048,256]{2,1,0:T(8,128)(2,1)}, f32[2048,256]{1,0:T(8,128)}, bf16[7,2048,256]{2,1,0:T(8,128)(2,1)}, bf16[5,2048,256]{2,1,0:T(8,128)(2,1)}, bf16[8,256,256]{2,1,0:T(8,128)(2,1)}) custom-call(f32[2,2048]{1,0:T(2,128)S(1)} %copy-done.4, f32[2,256]{1,0:T(2,128)S(1)} %copy-done.5, bf16[256,256]{1,0:T(8,128)(2,1)S(1)} %copy-done.3), custom_call_target="tpu_custom_call" | custom-call | tf_op jit(solution)/shard_map/trunk_forward/pallas_call | solution.py:459
  20.4 0.0 all-to-all-done.ones_ref
  20.4 7.1 %project.1 = (bf16[5,64,2048]{2,1,0:T(8,128)(2,1)}, bf16[64,256]{1,0:T(8,128)(2,1)S(1)}, bf16[8,8,256]{2,1,0:T(8,128)(2,1)}) custom-call(bf16[8,8,256]{2,1,0:T(8,128)(2,1)S(1)} %all-to-all-done.ones_ref, bf16[256,256]{1,0:T(8,128)(2,1)S(1)} %copy-done, bf16[256,256]{1,0:T(8,128)(2,1)S(1)} %copy-done.1, bf16[256,256]{1,0:T(8,128)(2,1)S(1)} %copy-done.2, ...), custom_call_target="tpu_custom_call" | custom-call | tf_op jit(solution)/shard_map/project/pallas_call | solution.py:485
  27.5 6.6 %all-to-all-start.1 = ((bf16[8,8,256]{2,1,0:T(8,128)(2,1)}), bf16[8,8,256]{2,1,0:T(8,128)(2,1)S(1)}, u32[]{:S(2)}, u32[]{:S(2)}) async-start(bf16[8,8,256]{2,1,0:T(8,128)(2,1)} %get-tuple-element.36), calls=%async_computation.1 | async-start | bytes 65536 | tf_op jit(solution)/shard_map/all_to_all | solution.py:633
  34.2 16.0 %trunk_backward.1 = f32[64,8,192]{2,1,0:T(8,128)S(1)} custom-call(f32[2048,256]{1,0:T(8,128)} %get-tuple-element.37.squash_ref, bf16[4,2048,256]{2,1,0:T(8,128)(2,1)} %get-tuple-element.38.points_ref, bf16[7,2048,256]{2,1,0:T(8,128)(2,1)} %get-tuple-element.39.inner_ref, bf16[5,64,2048]{2,1,0:T(8,128)(2,1)} %get-tuple-element.40.cots_ref, ...), custom_call_target="tpu_custom_call" | custom-call | flops 5637144576 | bytes 25165824 | tf_op jit(solution)/shard_map/trunk_backward/pallas_call | solution.py:518
  50.2 0.0 all-to-all-done.1
  50.3 0.2 pad_maximum_fusion
  50.5 24.8 %all_to_all.20.from_ref = bf16[64,8,768]{2,1,0:T(8,128)(2,1)S(1)} all-to-all(bf16[64,8,768]{2,1,0:T(8,128)(2,1)S(1)} %pad_maximum_fusion), channel_id=1, replica_groups=mesh['pairs'=8,'core'=2,'pts'=8] {'pairs','pts'}, dimensions={0} | all-to-all | bytes 1572864 | tf_op jit(solution)/shard_map/all_to_all | solution.py:633
  75.3 3.1 %collective-permute-start = (bf16[64,8,768]{2,1,0:T(8,128)(2,1)S(1)}, bf16[64,8,768]{2,1,0:T(8,128)(2,1)S(1)}, u32[]{:S(2)}, u32[]{:S(2)}) collective-permute-start(bf16[64,8,768]{2,1,0:T(8,128)(2,1)S(1)} %all_to_all.20.from_ref), channel_id=1, source_target_pairs={{0,8},{8,0},{1,9},{9,1},{2,10},{10,2},{3,11},{11,3},{4,12},{12,4},... | collective-permute-start | bytes 2359304 | tf_op jit(solution)/shard_map/ppermute | solution.py:637
  78.4 1.9 %branch_mine.1 = (bf16[512,256]{1,0:T(8,128)(2,1)}, bf16[512,256]{1,0:T(8,128)(2,1)}, bf16[512,256]{1,0:T(8,128)(2,1)}, bf16[512,256]{1,0:T(8,128)(2,1)}, bf16[5...) custom-call(s32[1]{0:T(128)} %bitcast.core_ref, ...), custom_call_target="tpu_custom_call" | custom-call | tf_op jit(solution)/shard_map/branch_mine/pallas_call | solution.py:567
  80.3 0.0 collective-permute-done.from_ref
  80.3 1.3 %branch_other.1 = (bf16[512,256]{1,0:T(8,128)(2,1)S(1)}, bf16[512,256]{1,0:T(8,128)(2,1)S(1)}, bf16[512,256]{1,0:T(8,128)(2,1)S(1)}, bf16[512,256]{1,0:T(8,128)(...) custom-call(s32[1]{0:T(128)} %bitcast.core_ref, ...), custom_call_target="tpu_custom_call" | custom-call | tf_op jit(solution)/shard_map/branch_other/pallas_call | solution.py:567
  81.6 0.2 broadcast_in_dim.8
  81.8 23.8 %all_to_all.21.mine_ref = bf16[64,72,128]{2,1,0:T(8,128)(2,1)S(1)} all-to-all(bf16[64,72,128]{2,1,0:T(8,128)(2,1)S(1)} %broadcast_in_dim.8), channel_id=1, replica_groups=mesh['pairs'=8,'core'=2,'pts'=8] {'pairs','pts'}, dimensions={0} | all-to-all | bytes 2359296 | tf_op jit(solution)/shard_map/all_to_all | solution.py:633
  105.6 1.9 %collective-permute-start.1 = (bf16[64,72,128]{2,1,0:T(8,128)(2,1)S(1)}, bf16[64,72,128]{2,1,0:T(8,128)(2,1)S(1)}, u32[]{:S(2)}, u32[]{:S(2)}) collective-permute-start(bf16[64,72,128]{2,1,0:T(8,128)(2,1)S(1)} %all_to_all.21.mine_ref), channel_id=1, source_target_pairs={{0,8},{8,0},{1,9},{9,1},{2,10},{10,2},{3,11},{11,3},{4,12},{12,4},... | collective-permute-start | bytes 3538952 | tf_op jit(solution)/shard_map/ppermute | solution.py:637
  107.5 1.2 %branch_gradients.1 = (f32[256,256]{1,0:T(8,128)}, f32[256,256]{1,0:T(8,128)}, f32[256,256]{1,0:T(8,128)}) custom-call(f32[256,256]{1,0:T(8,128)S(1)} %get-tuple-element.48.refs_0_, f32[256,256]{1,0:T(8,128)S(1)} %get-tuple-element.49.refs_1_, f32[256,256]{1,0:T(8,128)S(1)} %get-tuple-element.50.refs_2_, bf16[512,256]{1,0:T(8,128)(2,1)S(1)} %get-tuple-element.51.refs_3_, ...), custom_call_target="tpu_custom_call" | custom-call | tf_op jit(solution)/shard_map/branch_gradients/pallas_call | solution.py:578
  108.7 1.5 %spread_mine.1 = (f32[64,2,32,256]{3,2,1,0:T(8,128)}, f32[256,256]{1,0:T(8,128)}) custom-call(s32[1]{0:T(128)} %bitcast.core_ref, bf16[64,72,128]{2,1,0:T(8,128)(2,1)S(1)} %all_to_all.21.mine_ref), custom_call_target="tpu_custom_call" | custom-call | tf_op jit(solution)/shard_map/spread_mine/pallas_call | solution.py:601
  110.1 0.0 collective-permute-done.1.other_ref
  110.2 1.4 %spread_other.1 = f32[64,2,32,256]{3,2,1,0:T(8,128)} custom-call(s32[1]{0:T(128)} %bitcast.core_ref, bf16[64,72,128]{2,1,0:T(8,128)(2,1)S(1)} %collective-permute-done.1.other_ref, f32[64,2,32,256]{3,2,1,0:T(8,128)} %get-tuple-element.47.kept_ref), custom_call_target="tpu_custom_call", output_to_operand_aliasing={{}: (2, {})} | custom-call | tf_op jit(solution)/shard_map/spread_other/pallas_call | solution.py:617
  (19 shorter events, 0.1 us)
Async XLA Ops:
  0.6 10.1 %copy-start.7 = (bf16[8,4096]{1,0:T(8,128)(2,1)S(1)}, bf16[8,4096]{1,0:T(8,128)(2,1)}, u32[]{:S(2)}) copy-start(bf16[8,4096]{1,0:T(8,128)(2,1)} %sensors_ref.1) | copy-start | bytes 196612
  0.6 10.4 %copy-start.4 = (f32[2,2048]{1,0:T(2,128)S(1)}, f32[2,2048]{1,0:T(2,128)}, u32[]{:S(2)}) copy-start(f32[2,2048]{1,0:T(2,128)} %coords_ref.3) | copy-start | bytes 49156
  0.7 10.4 %copy-start.5 = (f32[2,256]{1,0:T(2,128)S(1)}, f32[2,256]{1,0:T(2,128)}, u32[]{:S(2)}) copy-start(f32[2,256]{1,0:T(2,128)} %first_ref.5) | copy-start | bytes 6148
  0.7 10.4 %copy-start.3 = (bf16[256,256]{1,0:T(8,128)(2,1)S(1)}, bf16[256,256]{1,0:T(8,128)(2,1)}, u32[]{:S(2)}) copy-start(bf16[256,256]{1,0:T(8,128)(2,1)} %second_ref.3) | copy-start | bytes 393220
  0.7 19.7 %copy-start = (bf16[256,256]{1,0:T(8,128)(2,1)S(1)}, bf16[256,256]{1,0:T(8,128)(2,1)}, u32[]{:S(2)}) copy-start(bf16[256,256]{1,0:T(8,128)(2,1)} %branch_second_ref.5) | copy-start | bytes 393220
  0.7 19.7 %copy-start.1 = (bf16[256,256]{1,0:T(8,128)(2,1)S(1)}, bf16[256,256]{1,0:T(8,128)(2,1)}, u32[]{:S(2)}) copy-start(bf16[256,256]{1,0:T(8,128)(2,1)} %branch_third_ref.5) | copy-start | bytes 393220
  0.7 19.7 %copy-start.2 = (bf16[256,256]{1,0:T(8,128)(2,1)S(1)}, bf16[256,256]{1,0:T(8,128)(2,1)}, u32[]{:S(2)}) copy-start(bf16[256,256]{1,0:T(8,128)(2,1)} %third_ref.5) | copy-start | bytes 393220
  3.3 17.1 %all-to-all-start = ((bf16[8,8,256]{2,1,0:T(8,128)(2,1)}), bf16[8,8,256]{2,1,0:T(8,128)(2,1)S(1)}, u32[]{:S(2)}, u32[]{:S(2)}) async-start(bf16[8,8,256]{2,1,0:T(8,128)(2,1)} %get-tuple-element.34), calls=%async_computation | async-start | bytes 65536 | tf_op jit(solution)/shard_map/all_to_all | solution.py:633
  20.4 13.8 %copy-start.6 = (bf16[8,256,256]{2,1,0:T(8,128)(2,1)S(1)}, bf16[8,256,256]{2,1,0:T(8,128)(2,1)}, u32[]{:S(2)}) copy-start(bf16[8,256,256]{2,1,0:T(8,128)(2,1)} %get-tuple-element.42.weights_ref) | copy-start | bytes 3145732
  27.5 22.7 %all-to-all-start.1 = ((bf16[8,8,256]{2,1,0:T(8,128)(2,1)}), bf16[8,8,256]{2,1,0:T(8,128)(2,1)S(1)}, u32[]{:S(2)}, u32[]{:S(2)}) async-start(bf16[8,8,256]{2,1,0:T(8,128)(2,1)} %get-tuple-element.36), calls=%async_computation.1 | async-start | bytes 65536 | tf_op jit(solution)/shard_map/all_to_all | solution.py:633
  75.3 5.1 %collective-permute-start = (bf16[64,8,768]{2,1,0:T(8,128)(2,1)S(1)}, bf16[64,8,768]{2,1,0:T(8,128)(2,1)S(1)}, u32[]{:S(2)}, u32[]{:S(2)}) collective-permute-start(bf16[64,8,768]{2,1,0:T(8,128)(2,1)S(1)} %all_to_all.20.from_ref), channel_id=1, source_target_pairs={{0,8},{8,0},{1,9},{9,1},{2,10},{10,2},{3,11},{11,3},{4,12},{12,4},... | collective-permute-start | bytes 2359304 | tf_op jit(solution)/shard_map/ppermute | solution.py:637
  105.6 4.6 %collective-permute-start.1 = (bf16[64,72,128]{2,1,0:T(8,128)(2,1)S(1)}, bf16[64,72,128]{2,1,0:T(8,128)(2,1)S(1)}, u32[]{:S(2)}, u32[]{:S(2)}) collective-permute-start(bf16[64,72,128]{2,1,0:T(8,128)(2,1)S(1)} %all_to_all.21.mine_ref), channel_id=1, source_target_pairs={{0,8},{8,0},{1,9},{9,1},{2,10},{10,2},{3,11},{11,3},{4,12},{12,4},... | collective-permute-start | bytes 3538952 | tf_op jit(solution)/shard_map/ppermute | solution.py:637

commit v8 on v7

--- a/solution.py
+++ b/solution.py
@@ -11,9 +11,9 @@
 DRAG = 0.5
 TILE = 512
 PROJECT = 1024
-ROWS = 16
-PARTS = 2
-CHUNK = 256
+ROWS = 32
+PARTS = 1
+CHUNK = 512
 STEPS = 2
 LANES = 128
 F32 = jnp.float32

time: 112 us -> 112 us (level)
  no operation moved by 1% of the time
where the time goes in v8:
time: 112 us; the launch traced here: 111 us
  blocking collectives  48.6 us (43%)
  Pallas kernels  41.8 us (37%)
  starting transfers between devices  19.2 us (17%)
    all_to_all x2, blocking collectives, swap(): return lax.all_to_all(parts, axes, split_axis=0, concat_axis=0, tiled=True)  48.6 us
    pallas_call x1, Pallas kernels, backward_call(): pl.pallas_call(backward_kernel, grid=(points // tile,), in_specs=[pl.Bloc...  15.7 us
    all_to_all x2, starting transfers between devices, swap(): return lax.all_to_all(parts, axes, split_axis=0, concat_axis=0, tiled=True)  14.1 us
    pallas_call x1, Pallas kernels, forward_call(): pl.pallas_call(forward_kernel, grid=(points // tile,), in_specs=[pl.Block...  9.25 us
    pallas_call x1, Pallas kernels, project_call(): pl.pallas_call(functools.partial(project_kernel, weight, scale), grid=(po...  7.1 us
    ppermute x2, starting transfers between devices, across_chip(): return lax.ppermute(value, 'core', [(0, 1), (1, 0)])  5.03 us
    pallas_call x2, Pallas kernels, branch_call(): pl.pallas_call(functools.partial(branch_kernel, scale, fields), in_specs=...  3.16 us
    pallas_call x1, Pallas kernels, first_call(): pl.pallas_call(first_kernel, grid=(STEPS,), in_specs=[pl.BlockSpec((own,...  2.57 us
  transfers between devices with their start and end apart: 4, of which 0 were waited for; matrix products, arithmetic and copies ran while one was open for 0% of the time, Pallas kernels for 27%

profile of v8, /device:TPU:1, one launch (start us, length us, event | category | flops | bytes accessed | tf_op | source)
XLA Modules:
  0.0 111.2 jit_solution(13861871563428488976)
XLA Ops:
  0.6 0.0 copy-start.7
  0.7 2.6 %branch_first.1 = (bf16[8,256]{1,0:T(8,128)(2,1)S(1)}, bf16[8,8,256]{2,1,0:T(8,128)(2,1)}) custom-call(bf16[8,4096]{1,0:T(8,128)(2,1)} %sensors_ref.1, bf16[4096,256]{1,0:T(8,128)(2,1)} %first_ref.3), custom_call_target="tpu_custom_call" | custom-call | tf_op jit(solution)/shard_map/branch_first/pallas_call | solution.py:437
  3.3 7.5 %all-to-all-start = ((bf16[8,8,256]{2,1,0:T(8,128)(2,1)}), bf16[8,8,256]{2,1,0:T(8,128)(2,1)S(1)}, u32[]{:S(2)}, u32[]{:S(2)}) async-start(bf16[8,8,256]{2,1,0:T(8,128)(2,1)} %get-tuple-element.34), calls=%async_computation | async-start | bytes 65536 | tf_op jit(solution)/shard_map/all_to_all | solution.py:633
  10.8 0.2 reshape.25
  10.9 0.1 copy.18
  11.1 9.2 %trunk_forward.1 = (bf16[4,2048,256]{2,1,0:T(8,128)(2,1)}, f32[2048,256]{1,0:T(8,128)}, bf16[7,2048,256]{2,1,0:T(8,128)(2,1)}, bf16[5,2048,256]{2,1,0:T(8,128)(2,1)}, bf16[8,256,256]{2,1,0:T(8,128)(2,1)}) custom-call(f32[2,2048]{1,0:T(2,128)S(1)} %copy-done.4, f32[2,256]{1,0:T(2,128)S(1)} %copy-done.5, bf16[256,256]{1,0:T(8,128)(2,1)S(1)} %copy-done.3), custom_call_target="tpu_custom_call" | custom-call | tf_op jit(solution)/shard_map/trunk_forward/pallas_call | solution.py:459
  20.3 0.0 all-to-all-done.ones_ref
  20.4 7.1 %project.1 = (bf16[5,64,2048]{2,1,0:T(8,128)(2,1)}, bf16[64,256]{1,0:T(8,128)(2,1)S(1)}, bf16[8,8,256]{2,1,0:T(8,128)(2,1)}) custom-call(bf16[8,8,256]{2,1,0:T(8,128)(2,1)S(1)} %all-to-all-done.ones_ref, bf16[256,256]{1,0:T(8,128)(2,1)S(1)} %copy-done, bf16[256,256]{1,0:T(8,128)(2,1)S(1)} %copy-done.1, bf16[256,256]{1,0:T(8,128)(2,1)S(1)} %copy-done.2, ...), custom_call_target="tpu_custom_call" | custom-call | tf_op jit(solution)/shard_map/project/pallas_call | solution.py:485
  27.5 6.6 %all-to-all-start.1 = ((bf16[8,8,256]{2,1,0:T(8,128)(2,1)}), bf16[8,8,256]{2,1,0:T(8,128)(2,1)S(1)}, u32[]{:S(2)}, u32[]{:S(2)}) async-start(bf16[8,8,256]{2,1,0:T(8,128)(2,1)} %get-tuple-element.36), calls=%async_computation.1 | async-start | bytes 65536 | tf_op jit(solution)/shard_map/all_to_all | solution.py:633
  34.1 15.7 %trunk_backward.1 = f32[64,8,192]{2,1,0:T(8,128)S(1)} custom-call(f32[2048,256]{1,0:T(8,128)} %get-tuple-element.37.squash_ref, bf16[4,2048,256]{2,1,0:T(8,128)(2,1)} %get-tuple-element.38.points_ref, bf16[7,2048,256]{2,1,0:T(8,128)(2,1)} %get-tuple-element.39.inner_ref, bf16[5,64,2048]{2,1,0:T(8,128)(2,1)} %get-tuple-element.40.cots_ref, ...), custom_call_target="tpu_custom_call" | custom-call | flops 5637144576 | bytes 25165824 | tf_op jit(solution)/shard_map/trunk_backward/pallas_call | solution.py:518
  49.9 0.0 all-to-all-done.1
  49.9 0.2 pad_maximum_fusion
  50.2 24.8 %all_to_all.20.from_ref = bf16[64,8,768]{2,1,0:T(8,128)(2,1)S(1)} all-to-all(bf16[64,8,768]{2,1,0:T(8,128)(2,1)S(1)} %pad_maximum_fusion), channel_id=1, replica_groups=mesh['pairs'=8,'core'=2,'pts'=8] {'pairs','pts'}, dimensions={0} | all-to-all | bytes 1572864 | tf_op jit(solution)/shard_map/all_to_all | solution.py:633
  74.9 3.1 %collective-permute-start = (bf16[64,8,768]{2,1,0:T(8,128)(2,1)S(1)}, bf16[64,8,768]{2,1,0:T(8,128)(2,1)S(1)}, u32[]{:S(2)}, u32[]{:S(2)}) collective-permute-start(bf16[64,8,768]{2,1,0:T(8,128)(2,1)S(1)} %all_to_all.20.from_ref), channel_id=1, source_target_pairs={{0,8},{8,0},{1,9},{9,1},{2,10},{10,2},{3,11},{11,3},{4,12},{12,4},... | collective-permute-start | bytes 2359304 | tf_op jit(solution)/shard_map/ppermute | solution.py:637
  78.1 1.9 %branch_mine.1 = (bf16[512,256]{1,0:T(8,128)(2,1)}, bf16[512,256]{1,0:T(8,128)(2,1)}, bf16[512,256]{1,0:T(8,128)(2,1)}, bf16[512,256]{1,0:T(8,128)(2,1)}, bf16[5...) custom-call(s32[1]{0:T(128)} %bitcast.core_ref, ...), custom_call_target="tpu_custom_call" | custom-call | tf_op jit(solution)/shard_map/branch_mine/pallas_call | solution.py:567
  79.9 0.0 collective-permute-done.from_ref
  80.0 1.3 %branch_other.1 = (bf16[512,256]{1,0:T(8,128)(2,1)S(1)}, bf16[512,256]{1,0:T(8,128)(2,1)S(1)}, bf16[512,256]{1,0:T(8,128)(2,1)S(1)}, bf16[512,256]{1,0:T(8,128)(...) custom-call(s32[1]{0:T(128)} %bitcast.core_ref, ...), custom_call_target="tpu_custom_call" | custom-call | tf_op jit(solution)/shard_map/branch_other/pallas_call | solution.py:567
  81.3 0.2 broadcast_in_dim.8
  81.4 23.8 %all_to_all.21.mine_ref = bf16[64,72,128]{2,1,0:T(8,128)(2,1)S(1)} all-to-all(bf16[64,72,128]{2,1,0:T(8,128)(2,1)S(1)} %broadcast_in_dim.8), channel_id=1, replica_groups=mesh['pairs'=8,'core'=2,'pts'=8] {'pairs','pts'}, dimensions={0} | all-to-all | bytes 2359296 | tf_op jit(solution)/shard_map/all_to_all | solution.py:633
  105.2 1.9 %collective-permute-start.1 = (bf16[64,72,128]{2,1,0:T(8,128)(2,1)S(1)}, bf16[64,72,128]{2,1,0:T(8,128)(2,1)S(1)}, u32[]{:S(2)}, u32[]{:S(2)}) collective-permute-start(bf16[64,72,128]{2,1,0:T(8,128)(2,1)S(1)} %all_to_all.21.mine_ref), channel_id=1, source_target_pairs={{0,8},{8,0},{1,9},{9,1},{2,10},{10,2},{3,11},{11,3},{4,12},{12,4},... | collective-permute-start | bytes 3538952 | tf_op jit(solution)/shard_map/ppermute | solution.py:637
  107.1 1.2 %branch_gradients.1 = (f32[256,256]{1,0:T(8,128)}, f32[256,256]{1,0:T(8,128)}, f32[256,256]{1,0:T(8,128)}) custom-call(f32[256,256]{1,0:T(8,128)S(1)} %get-tuple-element.48.refs_0_, f32[256,256]{1,0:T(8,128)S(1)} %get-tuple-element.49.refs_1_, f32[256,256]{1,0:T(8,128)S(1)} %get-tuple-element.50.refs_2_, bf16[512,256]{1,0:T(8,128)(2,1)S(1)} %get-tuple-element.51.refs_3_, ...), custom_call_target="tpu_custom_call" | custom-call | tf_op jit(solution)/shard_map/branch_gradients/pallas_call | solution.py:578
  108.3 1.5 %spread_mine.1 = (f32[64,2,32,256]{3,2,1,0:T(8,128)}, f32[256,256]{1,0:T(8,128)}) custom-call(s32[1]{0:T(128)} %bitcast.core_ref, bf16[64,72,128]{2,1,0:T(8,128)(2,1)S(1)} %all_to_all.21.mine_ref), custom_call_target="tpu_custom_call" | custom-call | tf_op jit(solution)/shard_map/spread_mine/pallas_call | solution.py:601
  109.8 0.0 collective-permute-done.1.other_ref
  109.8 1.4 %spread_other.1 = f32[64,2,32,256]{3,2,1,0:T(8,128)} custom-call(s32[1]{0:T(128)} %bitcast.core_ref, bf16[64,72,128]{2,1,0:T(8,128)(2,1)S(1)} %collective-permute-done.1.other_ref, f32[64,2,32,256]{3,2,1,0:T(8,128)} %get-tuple-element.47.kept_ref), custom_call_target="tpu_custom_call", output_to_operand_aliasing={{}: (2, {})} | custom-call | tf_op jit(solution)/shard_map/spread_other/pallas_call | solution.py:617
  (19 shorter events, 0.1 us)
Async XLA Ops:
  0.6 10.1 %copy-start.7 = (bf16[8,4096]{1,0:T(8,128)(2,1)S(1)}, bf16[8,4096]{1,0:T(8,128)(2,1)}, u32[]{:S(2)}) copy-start(bf16[8,4096]{1,0:T(8,128)(2,1)} %sensors_ref.1) | copy-start | bytes 196612
  0.6 10.4 %copy-start.4 = (f32[2,2048]{1,0:T(2,128)S(1)}, f32[2,2048]{1,0:T(2,128)}, u32[]{:S(2)}) copy-start(f32[2,2048]{1,0:T(2,128)} %coords_ref.3) | copy-start | bytes 49156
  0.7 10.4 %copy-start.5 = (f32[2,256]{1,0:T(2,128)S(1)}, f32[2,256]{1,0:T(2,128)}, u32[]{:S(2)}) copy-start(f32[2,256]{1,0:T(2,128)} %first_ref.5) | copy-start | bytes 6148
  0.7 10.4 %copy-start.3 = (bf16[256,256]{1,0:T(8,128)(2,1)S(1)}, bf16[256,256]{1,0:T(8,128)(2,1)}, u32[]{:S(2)}) copy-start(bf16[256,256]{1,0:T(8,128)(2,1)} %second_ref.3) | copy-start | bytes 393220
  0.7 19.7 %copy-start = (bf16[256,256]{1,0:T(8,128)(2,1)S(1)}, bf16[256,256]{1,0:T(8,128)(2,1)}, u32[]{:S(2)}) copy-start(bf16[256,256]{1,0:T(8,128)(2,1)} %branch_second_ref.5) | copy-start | bytes 393220
  0.7 19.7 %copy-start.1 = (bf16[256,256]{1,0:T(8,128)(2,1)S(1)}, bf16[256,256]{1,0:T(8,128)(2,1)}, u32[]{:S(2)}) copy-start(bf16[256,256]{1,0:T(8,128)(2,1)} %branch_third_ref.5) | copy-start | bytes 393220
  0.7 19.7 %copy-start.2 = (bf16[256,256]{1,0:T(8,128)(2,1)S(1)}, bf16[256,256]{1,0:T(8,128)(2,1)}, u32[]{:S(2)}) copy-start(bf16[256,256]{1,0:T(8,128)(2,1)} %third_ref.5) | copy-start | bytes 393220
  3.3 17.0 %all-to-all-start = ((bf16[8,8,256]{2,1,0:T(8,128)(2,1)}), bf16[8,8,256]{2,1,0:T(8,128)(2,1)S(1)}, u32[]{:S(2)}, u32[]{:S(2)}) async-start(bf16[8,8,256]{2,1,0:T(8,128)(2,1)} %get-tuple-element.34), calls=%async_computation | async-start | bytes 65536 | tf_op jit(solution)/shard_map/all_to_all | solution.py:633
  20.4 13.8 %copy-start.6 = (bf16[8,256,256]{2,1,0:T(8,128)(2,1)S(1)}, bf16[8,256,256]{2,1,0:T(8,128)(2,1)}, u32[]{:S(2)}) copy-start(bf16[8,256,256]{2,1,0:T(8,128)(2,1)} %get-tuple-element.42.weights_ref) | copy-start | bytes 3145732
  27.5 22.4 %all-to-all-start.1 = ((bf16[8,8,256]{2,1,0:T(8,128)(2,1)}), bf16[8,8,256]{2,1,0:T(8,128)(2,1)S(1)}, u32[]{:S(2)}, u32[]{:S(2)}) async-start(bf16[8,8,256]{2,1,0:T(8,128)(2,1)} %get-tuple-element.36), calls=%async_computation.1 | async-start | bytes 65536 | tf_op jit(solution)/shard_map/all_to_all | solution.py:633
  74.9 5.1 %collective-permute-start = (bf16[64,8,768]{2,1,0:T(8,128)(2,1)S(1)}, bf16[64,8,768]{2,1,0:T(8,128)(2,1)S(1)}, u32[]{:S(2)}, u32[]{:S(2)}) collective-permute-start(bf16[64,8,768]{2,1,0:T(8,128)(2,1)S(1)} %all_to_all.20.from_ref), channel_id=1, source_target_pairs={{0,8},{8,0},{1,9},{9,1},{2,10},{10,2},{3,11},{11,3},{4,12},{12,4},... | collective-permute-start | bytes 2359304 | tf_op jit(solution)/shard_map/ppermute | solution.py:637
  105.2 4.6 %collective-permute-start.1 = (bf16[64,72,128]{2,1,0:T(8,128)(2,1)S(1)}, bf16[64,72,128]{2,1,0:T(8,128)(2,1)S(1)}, u32[]{:S(2)}, u32[]{:S(2)}) collective-permute-start(bf16[64,72,128]{2,1,0:T(8,128)(2,1)S(1)} %all_to_all.21.mine_ref), channel_id=1, source_target_pairs={{0,8},{8,0},{1,9},{9,1},{2,10},{10,2},{3,11},{11,3},{4,12},{12,4},... | collective-permute-start | bytes 3538952 | tf_op jit(solution)/shard_map/ppermute | solution.py:637
